TPU v7x, 32 devices: a whole 2x2x4 slice. The times are simulated.
32 devices in a mesh: dp: 8 (over z, core), seq: 4 (over y, x).
Axes of the slice: x: 2, y: 2, z: 4, core: 2. Of those that a mesh axis runs over, the one named last changes fastest.
Arguments:
- inputs: bfloat16 [8, 1024, 1024], P('dp', 'seq'), may hold values from -6 to 6
- segments: int32 [8, 1024], P('dp'), may hold values from 0 to 8, as said below
- cotangent: bfloat16 [8, 1024, 1024], P('dp', 'seq'), may hold values from -6 to 6
- mixer_gate: bfloat16 [1024, 1536], P(('dp', 'seq')), may hold values from -0.1875 to 0.1875
- mixer_input: bfloat16 [1024, 1792], P(('dp', 'seq')), may hold values from -0.1875 to 0.1875
- mixer_step: bfloat16 [1024, 24], P(('dp', 'seq')), may hold values from -0.1875 to 0.1875
- mixer_output: bfloat16 [1536, 1024], P(('dp', 'seq')), may hold values from -0.15625 to 0.15625
- query_weight: bfloat16 [1024, 512], P(('dp', 'seq')), may hold values from -0.1875 to 0.1875
- key_weight: bfloat16 [1024, 128], P(('dp', 'seq')), may hold values from -0.1875 to 0.1875
- value_weight: bfloat16 [1024, 128], P(('dp', 'seq')), may hold values from -0.1875 to 0.1875
- output_weight: bfloat16 [512, 1024], P(('dp', 'seq')), may hold values from -1.5 to 1.5
- gate_weight: bfloat16 [1024, 2048], P(('dp', 'seq')), may hold values from -0.1875 to 0.1875
- up_weight: bfloat16 [1024, 2048], P(('dp', 'seq')), may hold values from -0.1875 to 0.1875
- down_weight: bfloat16 [2048, 1024], P(('dp', 'seq')), may hold values from -0.125 to 0.125
- input_gain: float32 [1024], replicated, may hold values from 0.25 to 1.75
- second_gain: float32 [1024], replicated, may hold values from 0.25 to 1.75
- mixer_gain: float32 [1536], replicated, may hold values from 0.25 to 1.75
- filter_taps: float32 [4, 1792], replicated, may hold values from -3 to 3
- filter_bias: float32 [1792], replicated, may hold values from -3 to 3
- decay_log: float32 [24], replicated, may hold values from -7.5 to -3
- step_bias: float32 [24], replicated, may hold values from -1 to 1
- skip_gain: float32 [24], replicated, may hold values from 0.5 to 1.5
Outputs:
- result: bfloat16 [8, 1024, 1024], P('dp', 'seq')
- input_grad: float32 [8, 1024, 1024], P('dp', 'seq')
- grad_mixer_gate: float32 [1024, 1536], P(('dp', 'seq'))
- grad_mixer_input: float32 [1024, 1792], P(('dp', 'seq'))
- grad_mixer_step: float32 [1024, 24], P(('dp', 'seq'))
- grad_mixer_output: float32 [1536, 1024], P(('dp', 'seq'))
- grad_query: float32 [1024, 512], P(('dp', 'seq'))
- grad_key: float32 [1024, 128], P(('dp', 'seq'))
- grad_value: float32 [1024, 128], P(('dp', 'seq'))
- grad_output: float32 [512, 1024], P(('dp', 'seq'))
- grad_gate: float32 [1024, 2048], P(('dp', 'seq'))
- grad_up: float32 [1024, 2048], P(('dp', 'seq'))
- grad_down: float32 [2048, 1024], P(('dp', 'seq'))
- grad_input_gain: float32 [1024], replicated
- grad_second_gain: float32 [1024], replicated
- grad_mixer_gain: float32 [1536], replicated
- grad_filter_taps: float32 [4, 1792], replicated
- grad_filter_bias: float32 [1792], replicated
- grad_decay_log: float32 [24], replicated
- grad_step_bias: float32 [24], replicated
- grad_skip_gain: float32 [24], replicated
Inputs may be any that keep to these rules, and one draw needn't show every extreme that they name: `segments`: in each sequence the segment numbers start at 0 and never fall; in one sequence, drawn from the seed, all 1024 tokens form one document.
All inputs are finite; a program needn't handle non-finite values.
Results may differ from a plain program's by a relative error of at most 0.014.
Values may be sent and summed in bfloat16 or wider, within the bound.
No kernel may reach another device: no remote copies, remote signals or barrier semaphores. Data moves between devices by JAX's collectives and lax.ppermute only.
A program may use at most 256 MiB of HBM per device.

v0:
```python
import jax
import jax.numpy as jnp
from jax import lax
from jax.sharding import PartitionSpec as P

HEADS = 8
KV_HEADS = 2
HEAD = 64
SSM_HEADS = 24
SSM_HEAD = 64
STATE = 128
CONV = 4


eps = 1e-05
rope_theta = 100000000000.0
score_scale = 0.125
block_keys = 512


def passed_along(x, axis, by):
    length = lax.axis_size(axis)
    pairs = [(i, i + by) for i in range(length) if 0 <= i + by < length]
    return lax.ppermute(x, axis, pairs)


def entering_2(x, axis, combine, identity):
    length, index = (lax.axis_size(axis), lax.axis_index(axis))
    everything = jax.tree.map(
        lambda part, kind: lax.all_gather(part.astype(kind), axis), x, (jnp.bfloat16, jnp.bfloat16)
    )
    start = jax.tree.map(
        lambda part, zero: jnp.broadcast_to(jnp.asarray(zero, part.dtype), part.shape), x, identity
    )

    def turn(k, before):
        reached = k < index
        new = combine(
            before, jax.tree.map(lambda part, own: part[k].astype(own.dtype), everything, x)
        )
        return jax.tree.map(lambda a, b: jnp.where(reached, a, b), new, before)

    return lax.fori_loop(0, length, turn, start)


def carried_in(x, axis, join, neutral):
    count = lax.axis_size(axis)
    place = lax.axis_index(axis)
    ahead = count - 1 - place
    gathered = jax.tree.map(
        lambda a, kind: lax.all_gather(a.astype(kind), axis),
        x,
        jax.tree.map(lambda a: jnp.bfloat16 if a.dtype == jnp.float32 else a.dtype, x),
    )
    state = jax.tree.map(lambda a, e: jnp.zeros_like(a) + jnp.asarray(e, a.dtype), x, neutral)

    def one(turn, state):
        source = count - 1 - turn
        return join(
            state,
            jax.tree.map(
                lambda a, own: lax.dynamic_index_in_dim(a, source, 0, False).astype(own.dtype),
                gathered,
                x,
            ),
        )

    return lax.fori_loop(0, ahead, one, state)


def matmul(left, right):
    return jnp.dot(left, right, preferred_element_type=jnp.float32)


def rows_product(left, right):
    return lax.dot_general(
        left, right, (((0,), (0,)), ((), ())), preferred_element_type=jnp.float32
    )


def back_product(left, right):
    return lax.dot_general(
        left, right, (((1,), (1,)), ((), ())), preferred_element_type=jnp.float32
    )


def rms_scale(tensor, scale_gain):
    return tensor * lax.rsqrt(jnp.mean(tensor * tensor, axis=-1, keepdims=True) + eps) * scale_gain


def rotate(tensor, positions, direction):
    half_width = tensor.shape[-1] // 2
    frequency = rope_theta ** (-jnp.arange(half_width, dtype=jnp.float32) / half_width)
    angle = positions.astype(jnp.float32)[:, None] * frequency[None, :]
    cosine = jnp.cos(angle)[:, None, :]
    sine_part = direction * jnp.sin(angle)[:, None, :]
    first_half = tensor[..., :half_width]
    second_half = tensor[..., half_width:]
    return jnp.concatenate(
        [
            first_half * cosine - second_half * sine_part,
            second_half * cosine + first_half * sine_part,
        ],
        axis=-1,
    )


def conv_apply(extended, ext_segments, filter_taps, filter_bias):
    length = extended.shape[0] - CONV + 1
    own_segment = ext_segments[CONV - 1 :]
    summed = jnp.zeros((length, extended.shape[1]), jnp.float32) + filter_bias[None, :]
    for offset in range(CONV):
        match_mask = (ext_segments[offset : offset + length] == own_segment).astype(jnp.float32)[
            :, None
        ]
        summed = (
            summed + filter_taps[offset][None, :] * extended[offset : offset + length] * match_mask
        )
    return jax.nn.silu(summed)


def ssd_split(filtered, step_raw, step_bias, decay_log):
    length = filtered.shape[0]
    inner = SSM_HEADS * SSM_HEAD
    values = filtered[:, :inner].reshape(length, SSM_HEADS, SSM_HEAD)
    write_map = filtered[:, inner : inner + STATE]
    read_map = filtered[:, inner + STATE :]
    stride = jax.nn.softplus(step_raw + step_bias)
    running = jnp.cumsum(stride * -jnp.exp(decay_log), axis=0)
    return (values, write_map, read_map, stride, running)


def ssd_state(filtered, step_raw, step_bias, decay_log, doc_ids, seg_prior):
    values, write_map, read_map, stride, running = ssd_split(
        filtered, step_raw, step_bias, decay_log
    )
    final_log = running[-1]
    keep_end = (doc_ids == doc_ids[-1]).astype(jnp.float32)[:, None]
    end_weights = jnp.exp(final_log[None, :] - running) * keep_end * stride
    end_state = jnp.einsum(
        "th,thd,tn->hdn", end_weights, values, write_map, precision=lax.Precision.HIGHEST
    )
    decay_total = jnp.exp(final_log) * (doc_ids[-1] == seg_prior).astype(jnp.float32)
    return (decay_total, end_state)


def ssd_output(
    filtered, step_raw, step_bias, decay_log, skip_gain, doc_ids, seg_prior, start_state
):
    values, write_map, read_map, stride, running = ssd_split(
        filtered, step_raw, step_bias, decay_log
    )
    length = filtered.shape[0]
    token_order = jnp.arange(length)
    allowed = (token_order[:, None] >= token_order[None, :]) & (
        doc_ids[:, None] == doc_ids[None, :]
    )
    gap_logs = running.T[:, :, None] - running.T[:, None, :]
    decay_mat = jnp.where(allowed[None], jnp.exp(jnp.minimum(gap_logs, 0.0)), 0.0)
    inner_prod = jnp.dot(read_map, write_map.T, precision=lax.Precision.HIGHEST)
    mixing = decay_mat * inner_prod[None] * stride.T[:, None, :]
    local_part = jnp.einsum("hts,shd->thd", mixing, values, precision=lax.Precision.HIGHEST)
    entering = (doc_ids == seg_prior).astype(jnp.float32)[:, None] * jnp.exp(running)
    carried = (
        jnp.einsum("hdn,tn->thd", start_state, read_map, precision=lax.Precision.HIGHEST)
        * entering[:, :, None]
    )
    summed = local_part + carried + skip_gain[None, :, None] * values
    return summed.reshape(length, SSM_HEADS * SSM_HEAD)


def gated_norm(ssm_out, gate_mix, mixer_gain):
    return rms_scale(ssm_out * jax.nn.silu(gate_mix), mixer_gain)


def swiglu(gate_val, up_val):
    return jax.nn.silu(gate_val) * up_val


def chain_combine(earlier, later):
    return (earlier[0] * later[0], later[0][:, None, None] * earlier[1] + later[1])


def reverse_combine(earlier, later):
    return (later[0] * earlier[0], later[1] + later[0][:, None, None] * earlier[1])


def block_scores(query_group, key_block, key_start, positions, own_segments, all_segs, block_size):
    raw_scores = (
        jnp.einsum("prd,kd->rpk", query_group, key_block, preferred_element_type=jnp.float32)
        * score_scale
    )
    key_positions = key_start + jnp.arange(block_size)
    key_segments = lax.dynamic_slice_in_dim(all_segs, key_start, block_size)
    allowed = (key_positions[None, :] <= positions[:, None]) & (
        key_segments[None, :] == own_segments[:, None]
    )
    return jnp.where(allowed[None], raw_scores, -1e30)


def body(
    inputs,
    segments,
    cotangent,
    mixer_gate,
    mixer_input,
    mixer_step,
    mixer_output,
    query_weight,
    key_weight,
    value_weight,
    output_weight,
    gate_weight,
    up_weight,
    down_weight,
    input_gain,
    second_gain,
    mixer_gain,
    filter_taps,
    filter_bias,
    decay_log,
    step_bias,
    skip_gain,
):
    piece_index = lax.axis_index("seq")
    local_len = inputs.shape[1]
    seq_len = segments.shape[1]
    first_token = piece_index * local_len
    all_segs = segments[0]
    own_segments = lax.dynamic_slice_in_dim(all_segs, first_token, local_len)
    rim_index = first_token - (CONV - 1) + jnp.arange(CONV - 1)
    rim_segments = jnp.where(rim_index >= 0, jnp.take(all_segs, jnp.maximum(rim_index, 0)), -1)
    seg_before = rim_segments[CONV - 2]
    positions = first_token + jnp.arange(local_len)
    ext_segments = jnp.concatenate([rim_segments, own_segments])
    gathered = (
        lax.all_gather(mixer_gate, ("dp", "seq"), axis=0, tiled=True),
        lax.all_gather(mixer_input, ("dp", "seq"), axis=0, tiled=True),
        lax.all_gather(mixer_step, ("dp", "seq"), axis=0, tiled=True),
        lax.all_gather(mixer_output, ("dp", "seq"), axis=0, tiled=True),
        lax.all_gather(query_weight, ("dp", "seq"), axis=0, tiled=True),
        lax.all_gather(key_weight, ("dp", "seq"), axis=0, tiled=True),
        lax.all_gather(value_weight, ("dp", "seq"), axis=0, tiled=True),
        lax.all_gather(output_weight, ("dp", "seq"), axis=0, tiled=True),
        lax.all_gather(gate_weight, ("dp", "seq"), axis=0, tiled=True),
        lax.all_gather(up_weight, ("dp", "seq"), axis=0, tiled=True),
        lax.all_gather(down_weight, ("dp", "seq"), axis=0, tiled=True),
    )
    tokens = inputs[0].astype(jnp.float32)
    normed, norm_back = jax.vjp(rms_scale, tokens, input_gain)
    normed_low = normed.astype(jnp.bfloat16)
    gate_mix = matmul(normed_low, gathered[0])
    mixed_raw = matmul(normed_low, gathered[1]).astype(jnp.bfloat16)
    step_raw = matmul(normed_low, gathered[2])
    queries = matmul(normed_low, gathered[4])
    keys_raw = matmul(normed_low, gathered[5])
    values_low = matmul(normed_low, gathered[6]).astype(jnp.bfloat16)
    rim_rows = passed_along(mixed_raw[local_len - CONV + 1 :], "seq", 1)
    extended = jnp.concatenate([rim_rows, mixed_raw], axis=0).astype(jnp.float32)

    def filter_fn(ext_rows, taps, bias):
        return conv_apply(ext_rows, ext_segments, taps, bias)

    filtered, filter_back = jax.vjp(filter_fn, extended, filter_taps, filter_bias)
    filtered_low = lax.optimization_barrier(filtered.astype(jnp.bfloat16)).astype(jnp.float32)

    def state_fn(xc_rows, step_in, bias, decay):
        return ssd_state(xc_rows, step_in, bias, decay, own_segments, seg_before)

    (carry_decay, carry_state), state_back = jax.vjp(
        state_fn, filtered_low, step_raw, step_bias, decay_log
    )
    incoming = entering_2(
        (carry_decay, carry_state),
        "seq",
        chain_combine,
        (jnp.ones_like(carry_decay), jnp.zeros_like(carry_state)),
    )

    def output_fn(xc_rows, step_in, bias, decay, skip, start_state):
        return ssd_output(
            xc_rows, step_in, bias, decay, skip, own_segments, seg_before, start_state
        )

    ssm_out, output_back = jax.vjp(
        output_fn, filtered_low, step_raw, step_bias, decay_log, skip_gain, incoming[1]
    )
    gated_out, gated_back = jax.vjp(gated_norm, ssm_out, gate_mix, mixer_gain)
    gated_low = gated_out.astype(jnp.bfloat16)
    mixer_result = matmul(gated_low, gathered[3])
    query_rot = rotate(queries.reshape(local_len, HEADS, HEAD), positions, 1.0).astype(jnp.bfloat16)
    key_rot = rotate(keys_raw.reshape(local_len, KV_HEADS, HEAD), positions, 1.0).astype(
        jnp.bfloat16
    )
    key_all, value_all = (
        lax.all_gather(key_rot.reshape(local_len, KV_HEADS * HEAD), "seq", axis=0, tiled=True),
        lax.all_gather(values_low, "seq", axis=0, tiled=True),
    )
    repeat = HEADS // KV_HEADS
    block_size = min(block_keys, seq_len)
    block_count = seq_len // block_size
    group_lse = []
    group_out = []
    group_exact = []
    for group_index in range(KV_HEADS):
        query_group = query_rot[:, group_index * repeat : (group_index + 1) * repeat]
        key_group = key_all[:, group_index * HEAD : (group_index + 1) * HEAD]
        value_group = value_all[:, group_index * HEAD : (group_index + 1) * HEAD]

        def lse_step(running, block_index):
            key_block = lax.dynamic_slice_in_dim(key_group, block_index * block_size, block_size)
            scores = block_scores(
                query_group,
                key_block,
                block_index * block_size,
                positions,
                own_segments,
                all_segs,
                block_size,
            )
            new_max = jnp.maximum(running[0], jnp.max(scores, axis=-1))
            new_sum = running[1] * jnp.exp(running[0] - new_max) + jnp.sum(
                jnp.exp(scores - new_max[..., None]), axis=-1
            )
            return ((new_max, new_sum), None)

        start_pair = (
            jnp.full((repeat, local_len), -1e30, jnp.float32),
            jnp.zeros((repeat, local_len), jnp.float32),
        )
        final_pair, unused = lax.scan(lse_step, start_pair, jnp.arange(block_count))
        lse_group = final_pair[0] + jnp.log(final_pair[1])

        def out_step(summed, block_index):
            key_block = lax.dynamic_slice_in_dim(key_group, block_index * block_size, block_size)
            value_block = lax.dynamic_slice_in_dim(
                value_group, block_index * block_size, block_size
            )
            scores = block_scores(
                query_group,
                key_block,
                block_index * block_size,
                positions,
                own_segments,
                all_segs,
                block_size,
            )
            probs = jnp.exp(scores - lse_group[..., None])
            prob_low = probs.astype(jnp.bfloat16)
            low_part = summed[0] + jnp.einsum(
                "rpk,kd->prd", prob_low, value_block, preferred_element_type=jnp.float32
            )
            exact_part = summed[1] + jnp.einsum(
                "rpk,kd->prd",
                probs,
                value_block.astype(jnp.float32),
                preferred_element_type=jnp.float32,
            )
            return ((low_part, exact_part), None)

        zero_out = jnp.zeros((local_len, repeat, HEAD), jnp.float32)
        (out_group, exact_group), unused = lax.scan(
            out_step, (zero_out, zero_out), jnp.arange(block_count)
        )
        group_lse.append(lse_group)
        group_out.append(out_group)
        group_exact.append(exact_group)
    attended = jnp.concatenate(group_out, axis=1)
    attended_low = attended.reshape(local_len, HEADS * HEAD).astype(jnp.bfloat16)
    attn_result = matmul(attended_low, gathered[7])
    middle = tokens + attn_result + mixer_result
    second, second_back = jax.vjp(rms_scale, middle, second_gain)
    second_low = second.astype(jnp.bfloat16)
    gate_val = matmul(second_low, gathered[8])
    up_val = matmul(second_low, gathered[9])
    activated, act_back = jax.vjp(swiglu, gate_val, up_val)
    activated_low = activated.astype(jnp.bfloat16)
    result = (middle + matmul(activated_low, gathered[10])).astype(jnp.bfloat16)
    reused = (
        lax.all_gather(mixer_gate, ("dp", "seq"), axis=0, tiled=True),
        lax.all_gather(mixer_input, ("dp", "seq"), axis=0, tiled=True),
        lax.all_gather(mixer_step, ("dp", "seq"), axis=0, tiled=True),
        lax.all_gather(mixer_output, ("dp", "seq"), axis=0, tiled=True),
        lax.all_gather(query_weight, ("dp", "seq"), axis=0, tiled=True),
        lax.all_gather(key_weight, ("dp", "seq"), axis=0, tiled=True),
        lax.all_gather(value_weight, ("dp", "seq"), axis=0, tiled=True),
        lax.all_gather(output_weight, ("dp", "seq"), axis=0, tiled=True),
        lax.all_gather(gate_weight, ("dp", "seq"), axis=0, tiled=True),
        lax.all_gather(up_weight, ("dp", "seq"), axis=0, tiled=True),
        lax.all_gather(down_weight, ("dp", "seq"), axis=0, tiled=True),
    )
    upstream = cotangent[0].astype(jnp.float32)
    upstream_low = upstream.astype(jnp.bfloat16)
    grad_down = rows_product(activated_low, upstream_low)
    grad_act = back_product(upstream_low, reused[10])
    grad_gate_val, grad_up_val = act_back(grad_act)
    gate_grad_low = grad_gate_val.astype(jnp.bfloat16)
    up_grad_low = grad_up_val.astype(jnp.bfloat16)
    grad_gate = rows_product(second_low, gate_grad_low)
    grad_up = rows_product(second_low, up_grad_low)
    grad_second = back_product(gate_grad_low, reused[8]) + back_product(up_grad_low, reused[9])
    ffn_grads = (
        lax.psum_scatter(grad_gate, ("dp", "seq"), scatter_dimension=0, tiled=True),
        lax.psum_scatter(grad_up, ("dp", "seq"), scatter_dimension=0, tiled=True),
        lax.psum_scatter(grad_down, ("dp", "seq"), scatter_dimension=0, tiled=True),
    )
    grad_middle, grad_second_gain = second_back(grad_second)
    grad_middle = grad_middle + upstream
    branch_low = grad_middle.astype(jnp.bfloat16)
    grad_mixer_output = rows_product(gated_low, branch_low)
    grad_gated = back_product(branch_low, reused[3])
    grad_ssm, grad_zgate, grad_mixer_gain = gated_back(grad_gated)
    zgate_low = grad_zgate.astype(jnp.bfloat16)
    xc_first, step_first, bias_first, decay_first, grad_skip, grad_incoming = output_back(grad_ssm)
    later_sums = carried_in(
        (carry_decay, grad_incoming),
        "seq",
        reverse_combine,
        (jnp.ones_like(carry_decay), jnp.zeros_like(grad_incoming)),
    )
    carried = later_sums[1]
    grad_decay_total = jnp.sum(carried * incoming[1], axis=(1, 2))
    xc_second, step_second, bias_second, decay_second = state_back((grad_decay_total, carried))
    grad_ext, grad_taps, grad_fbias = filter_back(xc_first + xc_second)
    returned = passed_along(grad_ext[: CONV - 1], "seq", -1)
    grad_mixed = grad_ext[CONV - 1 :].at[local_len - CONV + 1 :].add(returned)
    mixed_grad_low = grad_mixed.astype(jnp.bfloat16)
    step_grad_low = (step_first + step_second).astype(jnp.bfloat16)
    grad_output = rows_product(attended_low, branch_low)
    grad_attn = (
        back_product(branch_low, reused[7]).astype(jnp.bfloat16).reshape(local_len, HEADS, HEAD)
    )
    query_grads = []
    key_grads = []
    value_grads = []
    for group_index in range(KV_HEADS):
        query_group = query_rot[:, group_index * repeat : (group_index + 1) * repeat]
        key_group = key_all[:, group_index * HEAD : (group_index + 1) * HEAD]
        value_group = value_all[:, group_index * HEAD : (group_index + 1) * HEAD]
        grad_group = grad_attn[:, group_index * repeat : (group_index + 1) * repeat]
        lse_group = group_lse[group_index]
        row_delta = jnp.einsum(
            "prd,prd->rp", grad_group.astype(jnp.float32), group_exact[group_index]
        )

        def grad_step(grad_rows, block_index):
            key_start = block_index * block_size
            key_block = lax.dynamic_slice_in_dim(key_group, key_start, block_size)
            value_block = lax.dynamic_slice_in_dim(value_group, key_start, block_size)
            scores = block_scores(
                query_group, key_block, key_start, positions, own_segments, all_segs, block_size
            )
            probs = jnp.exp(scores - lse_group[..., None])
            prob_low = probs.astype(jnp.bfloat16)
            value_part = jnp.einsum(
                "rpk,prd->kd", prob_low, grad_group, preferred_element_type=jnp.float32
            )
            grad_probs = jnp.einsum(
                "prd,kd->rpk", grad_group, value_block, preferred_element_type=jnp.float32
            )
            grad_scores = (probs * (grad_probs - row_delta[..., None])).astype(jnp.bfloat16)
            query_part = grad_rows + score_scale * jnp.einsum(
                "rpk,kd->prd", grad_scores, key_block, preferred_element_type=jnp.float32
            )
            key_part = score_scale * jnp.einsum(
                "rpk,prd->kd", grad_scores, query_group, preferred_element_type=jnp.float32
            )
            return (query_part, (key_part, value_part))

        query_part, (key_stack, value_stack) = lax.scan(
            grad_step, jnp.zeros((local_len, repeat, HEAD), jnp.float32), jnp.arange(block_count)
        )
        query_grads.append(query_part)
        key_grads.append(key_stack.reshape(seq_len, HEAD))
        value_grads.append(value_stack.reshape(seq_len, HEAD))
    key_total, value_total = (
        lax.psum_scatter(
            jnp.concatenate(key_grads, axis=1).astype(jnp.bfloat16),
            "seq",
            scatter_dimension=0,
            tiled=True,
        ).astype(jnp.float32),
        lax.psum_scatter(
            jnp.concatenate(value_grads, axis=1).astype(jnp.bfloat16),
            "seq",
            scatter_dimension=0,
            tiled=True,
        ).astype(jnp.float32),
    )
    query_low = (
        rotate(jnp.concatenate(query_grads, axis=1), positions, -1.0)
        .reshape(local_len, HEADS * HEAD)
        .astype(jnp.bfloat16)
    )
    key_low = (
        rotate(key_total.reshape(local_len, KV_HEADS, HEAD), positions, -1.0)
        .reshape(local_len, KV_HEADS * HEAD)
        .astype(jnp.bfloat16)
    )
    value_low = value_total.astype(jnp.bfloat16)
    grad_normed = (
        back_product(zgate_low, reused[0])
        + back_product(mixed_grad_low, reused[1])
        + back_product(step_grad_low, reused[2])
    )
    grad_normed = (
        grad_normed
        + back_product(query_low, reused[4])
        + back_product(key_low, reused[5])
        + back_product(value_low, reused[6])
    )
    mixer_grads = (
        lax.psum_scatter(
            rows_product(normed_low, zgate_low), ("dp", "seq"), scatter_dimension=0, tiled=True
        ),
        lax.psum_scatter(
            rows_product(normed_low, mixed_grad_low), ("dp", "seq"), scatter_dimension=0, tiled=True
        ),
        lax.psum_scatter(
            rows_product(normed_low, step_grad_low), ("dp", "seq"), scatter_dimension=0, tiled=True
        ),
        lax.psum_scatter(grad_mixer_output, ("dp", "seq"), scatter_dimension=0, tiled=True),
        lax.psum_scatter(
            rows_product(normed_low, query_low), ("dp", "seq"), scatter_dimension=0, tiled=True
        ),
        lax.psum_scatter(
            rows_product(normed_low, key_low), ("dp", "seq"), scatter_dimension=0, tiled=True
        ),
        lax.psum_scatter(
            rows_product(normed_low, value_low), ("dp", "seq"), scatter_dimension=0, tiled=True
        ),
        lax.psum_scatter(grad_output, ("dp", "seq"), scatter_dimension=0, tiled=True),
    )
    grad_tokens, grad_input_gain = norm_back(grad_normed)
    grad_tokens = grad_tokens + grad_middle
    small_sums = lax.psum(
        (
            grad_input_gain,
            grad_second_gain,
            grad_mixer_gain,
            grad_taps,
            grad_fbias,
            decay_first + decay_second,
            bias_first + bias_second,
            grad_skip,
        ),
        ("dp", "seq"),
    )
    return (
        result[None],
        grad_tokens[None],
        mixer_grads[0],
        mixer_grads[1],
        mixer_grads[2],
        mixer_grads[3],
        mixer_grads[4],
        mixer_grads[5],
        mixer_grads[6],
        mixer_grads[7],
        ffn_grads[0],
        ffn_grads[1],
        ffn_grads[2],
        small_sums[0],
        small_sums[1],
        small_sums[2],
        small_sums[3],
        small_sums[4],
        small_sums[5],
        small_sums[6],
        small_sums[7],
    )


def solution(mesh):
    placed = (
        P("dp", "seq", None),
        P("dp", None),
        P("dp", "seq", None),
        P(("dp", "seq"), None),
        P(("dp", "seq"), None),
        P(("dp", "seq"), None),
        P(("dp", "seq"), None),
        P(("dp", "seq"), None),
        P(("dp", "seq"), None),
        P(("dp", "seq"), None),
        P(("dp", "seq"), None),
        P(("dp", "seq"), None),
        P(("dp", "seq"), None),
        P(("dp", "seq"), None),
        P(),
        P(),
        P(),
        P(),
        P(),
        P(),
        P(),
        P(),
    )
    return jax.shard_map(
        body,
        mesh=mesh,
        in_specs=placed,
        out_specs=(
            P("dp", "seq", None),
            P("dp", "seq", None),
            P(("dp", "seq"), None),
            P(("dp", "seq"), None),
            P(("dp", "seq"), None),
            P(("dp", "seq"), None),
            P(("dp", "seq"), None),
            P(("dp", "seq"), None),
            P(("dp", "seq"), None),
            P(("dp", "seq"), None),
            P(("dp", "seq"), None),
            P(("dp", "seq"), None),
            P(("dp", "seq"), None),
            P(),
            P(),
            P(),
            P(),
            P(),
            P(),
            P(),
            P(),
        ),
        check_vma=False,
    )
```

profile of v0, /device:TPU:0, one launch (start us, length us, event | category | flops | bytes accessed | tf_op | source)
XLA Modules:
  0.0 2318.5 jit_solution(1769982302739664)
XLA Ops:
  17.2 71.4 %all-gather.2 = bf16[32,32,24]{1,2,0:T(8,128)(2,1)S(1)} all-gather(bf16[1,32,24]{1,2,0:T(8,128)(2,1)} %bitcast.638), channel_id=1, replica_groups=mesh['dp'=8,'seq'=4] {'dp','seq'}, dimensions={0}, use_global_device_ids=true | all-gather | bytes 50688 | tf_op jit(solution)/shard_map/all_gather | solution.py:239
  109.3 67.5 %all_gather.70 = bf16[1024,128]{1,0:T(8,128)(2,1)S(1)} all-gather(bf16[32,128]{1,0:T(8,128)(2,1)S(1)} %copy-done.142), channel_id=1, replica_groups=mesh['dp'=8,'seq'=4] {'dp','seq'}, dimensions={0}, use_global_device_ids=true | all-gather | bytes 270336 | tf_op jit(solution)/shard_map/all_gather | solution.py:242
  178.2 8.6 all_gather.71
  187.6 67.2 %all_gather.68 = bf16[1024,128]{1,0:T(8,128)(2,1)S(1)} all-gather(bf16[32,128]{1,0:T(8,128)(2,1)S(1)} %copy-done.143), channel_id=1, replica_groups=mesh['dp'=8,'seq'=4] {'dp','seq'}, dimensions={0}, use_global_device_ids=true | all-gather | bytes 270336 | tf_op jit(solution)/shard_map/all_gather | solution.py:243
  255.8 8.0 all_gather.69
  264.3 8.0 all-gather.3
  277.7 13.2 while.112
  291.6 9.0 while.113
  302.9 12.5 while.114
  316.1 8.2 while.115
  336.3 6.4 fusion.131
  358.3 48.8 %all-gather.25.cloned.1.call-done = bf16[1024,2048]{1,0:T(8,128)(2,1)} async-done(((bf16[32,2048]{1,0:T(8,128)(2,1)}), bf16[1024,2048]{1,0:T(8,128)(2,1)}) %all-gather.25.cloned.1.call-update) | async-done | bytes 4194320 | tf_op jit(solution)/shard_map/all_gather | solution.py:245
  411.8 58.7 %all-gather.27.cloned.1.call-done = bf16[1024,2048]{1,0:T(8,128)(2,1)} async-done(((bf16[32,2048]{1,0:T(8,128)(2,1)}), bf16[1024,2048]{1,0:T(8,128)(2,1)}) %all-gather.27.cloned.1.call-update) | async-done | bytes 4194320 | tf_op jit(solution)/shard_map/all_gather | solution.py:246
  475.2 58.7 %all-gather.29.cloned.1.call-done = bf16[2048,1024]{1,0:T(8,128)(2,1)} async-done(((bf16[64,1024]{1,0:T(8,128)(2,1)}), bf16[2048,1024]{1,0:T(8,128)(2,1)}) %all-gather.29.cloned.1.call-update) | async-done | bytes 4194320 | tf_op jit(solution)/shard_map/all_gather | solution.py:247
  534.0 6.6 multiply_convert_fusion
  554.7 17.5 while.117
  573.6 15.4 while.118
  603.4 8.7 fusion.171
  618.8 28.6 %all-gather.33.cloned.1.call-done = bf16[96,64,128]{2,1,0:T(8,128)(2,1)} async-done(((bf16[24,64,128]{2,1,0:T(8,128)(2,1)}), bf16[96,64,128]{2,1,0:T(8,128)(2,1)}) %all-gather.33.cloned.1.call-update) | async-done | bytes 1572880 | tf_op jit(solution)/shard_map/all_gather | solution.py:51
  661.3 13.6 reduce-scatter.18.cloned.1.call-done
  712.7 8.7 bitcast_add_fusion
  766.0 41.4 %all-reduce.14 = (f32[1024]{0:T(1024)}, f32[1024]{0:T(1024)}, f32[1536]{0:T(1024)}, f32[4,1792]{1,0:T(4,128)}, f32[1792]{0:T(1024)}, /*index=5*/f32[24]{0:T(128)}, f32[24]{0:T(128)}, f32[24]{0:T(128)}) all-reduce(f32[1024]{0:T(1024)S(1)} %get-tuple-element.1162, ...), channel_id=1, replica_groups=mesh['dp'=8,'seq'=4] {'dp','seq'}, use_global_device_ids=true, to_apply=%region_53.55 | all-reduce | flops 12616 | bytes 100928 | tf_op jit(solution)/shard_map/psum | solution.py:536
  812.5 131.2 %reduce-scatter.28.cloned.1.call-done = f32[32,128]{1,0:T(8,128)} async-done(((f32[1024,128]{1,0:T(8,128)}), f32[32,128]{1,0:T(8,128)}) %reduce-scatter.28.cloned.1.call-update) | async-done | bytes 16400 | tf_op jit(solution)/shard_map/reduce_scatter | solution.py:526
  943.7 132.5 %reduce-scatter.30.cloned.1.call-done = f32[32,128]{1,0:T(8,128)} async-done(((f32[1024,128]{1,0:T(8,128)}), f32[32,128]{1,0:T(8,128)}) %reduce-scatter.30.cloned.1.call-update) | async-done | bytes 16400 | tf_op jit(solution)/shard_map/reduce_scatter | solution.py:529
  1076.1 135.6 %reduce-scatter.32.cloned.1.call-done = f32[16,1024]{1,0:T(8,128)} async-done(((f32[512,1024]{1,0:T(8,128)}), f32[16,1024]{1,0:T(8,128)}) %reduce-scatter.32.cloned.1.call-update) | async-done | bytes 65552 | tf_op jit(solution)/shard_map/reduce_scatter | solution.py:532
  1211.7 135.8 %reduce-scatter.26.cloned.1.call-done = f32[32,512]{1,0:T(8,128)} async-done(((f32[1024,512]{1,0:T(8,128)}), f32[32,512]{1,0:T(8,128)}) %reduce-scatter.26.cloned.1.call-update) | async-done | bytes 65552 | tf_op jit(solution)/shard_map/reduce_scatter | solution.py:523
  1347.5 117.6 %reduce-scatter.24.cloned.1.call-done = f32[48,1024]{1,0:T(8,128)} async-done(((f32[1536,1024]{1,0:T(8,128)}), f32[48,1024]{1,0:T(8,128)}) %reduce-scatter.24.cloned.1.call-update) | async-done | bytes 196624 | tf_op jit(solution)/shard_map/reduce_scatter | solution.py:522
  1465.1 120.1 %reduce-scatter.20.cloned.1.call-done = f32[32,1536]{1,0:T(8,128)} async-done(((f32[1024,1536]{1,0:T(8,128)}), f32[32,1536]{1,0:T(8,128)}) %reduce-scatter.20.cloned.1.call-update) | async-done | bytes 196624 | tf_op jit(solution)/shard_map/reduce_scatter | solution.py:513
  1585.1 185.6 %reduce-scatter.34.cloned.1.call-done = f32[32,2048]{1,0:T(8,128)} async-done(((f32[1024,2048]{1,0:T(8,128)}), f32[32,2048]{1,0:T(8,128)}) %reduce-scatter.34.cloned.1.call-update) | async-done | bytes 262160 | tf_op jit(solution)/shard_map/reduce_scatter | solution.py:403
  1770.7 187.5 %reduce-scatter.36.cloned.1.call-done = f32[32,2048]{1,0:T(8,128)} async-done(((f32[1024,2048]{1,0:T(8,128)}), f32[32,2048]{1,0:T(8,128)}) %reduce-scatter.36.cloned.1.call-update) | async-done | bytes 262160 | tf_op jit(solution)/shard_map/reduce_scatter | solution.py:404
  1958.2 187.4 %reduce-scatter.38.cloned.1.call-done = f32[64,1024]{1,0:T(8,128)} async-done(((f32[2048,1024]{1,0:T(8,128)}), f32[64,1024]{1,0:T(8,128)}) %reduce-scatter.38.cloned.1.call-update) | async-done | bytes 262160 | tf_op jit(solution)/shard_map/reduce_scatter | solution.py:405
  2145.7 165.8 %reduce-scatter.22.cloned.1.call-done = f32[32,1792]{1,0:T(8,128)} async-done(((f32[1024,1792]{1,0:T(8,128)}), f32[32,1792]{1,0:T(8,128)}) %reduce-scatter.22.cloned.1.call-update) | async-done | bytes 229392 | tf_op jit(solution)/shard_map/reduce_scatter | solution.py:516
  (758 shorter events, 289.8 us)
Async XLA Ops:
  7.2 84.6 %all-gather.19.cloned.1.call-start = ((), (), s32[]{:S(2)}) async-start(), calls=%async_computation.15 | async-start | bytes 3784704 | tf_op jit(solution)/shard_map/all_gather | solution.py:238
  8.0 267.0 %all-gather.15.cloned.1.call-start = ((), (), s32[]{:S(2)}) async-start(), calls=%async_computation.13 | async-start | bytes 1081344 | tf_op jit(solution)/shard_map/all_gather | solution.py:241
  8.7 320.6 %all-gather.31.cloned.1.call-start = ((), (), s32[]{:S(2)}) async-start(), calls=%async_computation.33 | async-start | bytes 1966080 | tf_op jit(solution)/shard_map/all_gather | solution.py:30
  10.0 166.9 %copy-start.95 = (f32[256]{0:T(256)}, f32[256]{0:T(256)S(1)}, u32[]{:S(2)}) copy-start(f32[256]{0:T(256)S(1)} %fusion.223) | copy-start | bytes 3076
  90.5 183.8 %copy-start.42 = (f32[24,2,128]{0,2,1:T(8,128)}, f32[24,2,128]{0,2,1:T(8,128)S(1)}, u32[]{:S(2)}) copy-start(f32[24,2,128]{0,2,1:T(8,128)S(1)} %copy.250) | copy-start | bytes 73732
  95.1 2.7 collective-permute-start
  104.4 241.4 %all-gather.21.cloned.1.call-start = ((), (), s32[]{:S(2)}) async-start(), calls=%async_computation.16 | async-start | bytes 3244032 | tf_op jit(solution)/shard_map/all_gather | solution.py:237
  105.0 245.5 %all-gather.23.cloned.1.call-start = ((), (), s32[]{:S(2)}) async-start(), calls=%async_computation.17 | async-start | bytes 3244032 | tf_op jit(solution)/shard_map/all_gather | solution.py:240
  105.6 249.4 %all-gather.17.cloned.1.call-start = ((), (), s32[]{:S(2)}) async-start(), calls=%async_computation.14 | async-start | bytes 1081344 | tf_op jit(solution)/shard_map/all_gather | solution.py:244
  106.1 300.9 %all-gather.25.cloned.1.call-start = ((), (), s32[]{:S(2)}) async-start(), calls=%async_computation.18 | async-start | bytes 4325376 | tf_op jit(solution)/shard_map/all_gather | solution.py:245
  106.9 363.6 %all-gather.27.cloned.1.call-start = ((), (), s32[]{:S(2)}) async-start(), calls=%async_computation.19 | async-start | bytes 4325376 | tf_op jit(solution)/shard_map/all_gather | solution.py:246
  107.6 426.3 %all-gather.29.cloned.1.call-start = ((), (), s32[]{:S(2)}) async-start(), calls=%async_computation.20 | async-start | bytes 4325376 | tf_op jit(solution)/shard_map/all_gather | solution.py:247
  108.4 508.8 %reduce-scatter.16.cloned.1.call-start = ((), (), s32[]{:S(2)}) async-start(), calls=%async_computation.21 | async-start | bytes 327680 | tf_op jit(solution)/shard_map/reduce_scatter | solution.py:477
  350.5 196.0 %copy-start.8 = (f32[256,1536]{1,0:T(8,128)}, f32[256,1536]{1,0:T(8,128)S(1)}, u32[]{:S(2)}) copy-start(f32[256,1536]{1,0:T(8,128)S(1)} %get-tuple-element.1346) | copy-start | bytes 4718596
  350.5 196.0 %copy-start.114 = (f32[256]{0:T(256)}, f32[256]{0:T(256)S(1)}, u32[]{:S(2)}) copy-start(f32[256]{0:T(256)S(1)} %fusion.224) | copy-start | bytes 3076
  357.1 188.9 %copy-start.112 = (f32[256]{0:T(256)}, f32[256]{0:T(256)S(1)}, u32[]{:S(2)}) copy-start(f32[256]{0:T(256)S(1)} %fusion.225) | copy-start | bytes 3076
  358.2 112.3 %copy-start.48 = (bf16[256,1024]{1,0:T(8,128)(2,1)}, bf16[256,1024]{1,0:T(8,128)(2,1)S(1)}, u32[]{:S(2)}) copy-start(bf16[256,1024]{1,0:T(8,128)(2,1)S(1)} %multiply_convert_fusion.4) | copy-start | bytes 1572868
  411.8 122.2 %copy-start.44 = (bf16[1,256,1024]{2,1,0:T(8,128)(2,1)S(1)}, bf16[1,256,1024]{2,1,0:T(8,128)(2,1)}, u32[]{:S(2)}) copy-start(bf16[1,256,1024]{2,1,0:T(8,128)(2,1)} %param.43) | copy-start | bytes 1572868
  591.6 55.8 %all-gather.33.cloned.1.call-start = ((), (), s32[]{:S(2)}) async-start(), calls=%async_computation.34 | async-start | bytes 1966080 | tf_op jit(solution)/shard_map/all_gather | solution.py:51
  601.4 73.6 %reduce-scatter.18.cloned.1.call-start = ((), (), s32[]{:S(2)}) async-start(), calls=%async_computation.22 | async-start | bytes 327680 | tf_op jit(solution)/shard_map/reduce_scatter | solution.py:483
  617.1 193.9 %reduce-scatter.40.cloned.1.call-start = ((), (), s32[]{:S(2)}) async-start(), calls=%async_computation.35 | async-start | bytes 540672
  659.9 283.7 %reduce-scatter.28.cloned.1.call-start = ((), (), s32[]{:S(2)}) async-start(), calls=%async_computation.27 | async-start | bytes 540672 | tf_op jit(solution)/shard_map/reduce_scatter | solution.py:526
  661.3 414.8 %reduce-scatter.30.cloned.1.call-start = ((), (), s32[]{:S(2)}) async-start(), calls=%async_computation.28 | async-start | bytes 540672 | tf_op jit(solution)/shard_map/reduce_scatter | solution.py:529
  677.1 534.6 %reduce-scatter.32.cloned.1.call-start = ((), (), s32[]{:S(2)}) async-start(), calls=%async_computation.29 | async-start | bytes 2162688 | tf_op jit(solution)/shard_map/reduce_scatter | solution.py:532
  679.0 668.5 %reduce-scatter.26.cloned.1.call-start = ((), (), s32[]{:S(2)}) async-start(), calls=%async_computation.26 | async-start | bytes 2162688 | tf_op jit(solution)/shard_map/reduce_scatter | solution.py:523
  682.0 783.0 %reduce-scatter.24.cloned.1.call-start = ((), (), s32[]{:S(2)}) async-start(), calls=%async_computation.25 | async-start | bytes 6488064 | tf_op jit(solution)/shard_map/reduce_scatter | solution.py:522
  687.2 897.9 %reduce-scatter.20.cloned.1.call-start = ((), (), s32[]{:S(2)}) async-start(), calls=%async_computation.23 | async-start | bytes 6488064 | tf_op jit(solution)/shard_map/reduce_scatter | solution.py:513
  692.1 1078.6 %reduce-scatter.34.cloned.1.call-start = ((), (), s32[]{:S(2)}) async-start(), calls=%async_computation.30 | async-start | bytes 8650752 | tf_op jit(solution)/shard_map/reduce_scatter | solution.py:403
  699.0 1259.2 %reduce-scatter.36.cloned.1.call-start = ((), (), s32[]{:S(2)}) async-start(), calls=%async_computation.31 | async-start | bytes 8650752 | tf_op jit(solution)/shard_map/reduce_scatter | solution.py:404
  704.9 1440.8 %reduce-scatter.38.cloned.1.call-start = ((), (), s32[]{:S(2)}) async-start(), calls=%async_computation.32 | async-start | bytes 8650752 | tf_op jit(solution)/shard_map/reduce_scatter | solution.py:405
  711.8 1599.7 %reduce-scatter.22.cloned.1.call-start = ((), (), s32[]{:S(2)}) async-start(), calls=%async_computation.24 | async-start | bytes 7569408 | tf_op jit(solution)/shard_map/reduce_scatter | solution.py:516
  744.3 5.8 collective-permute-start.1
  (184 other events, 1959.7 us)
Sparse Core Ops, SparseCore 0:
  10.9 63.7 all-gather.18
  77.7 52.6 all-gather.14
  132.8 30.9 all-gather.30
  166.6 59.3 all-gather.20
  228.8 58.8 all-gather.22
  290.5 52.5 all-gather.16
  346.0 61.0 all-gather.24
  409.9 60.5 all-gather.26
  473.4 60.5 all-gather.28
  591.7 22.6 reduce-scatter.15
  616.4 30.9 all-gather.32
  650.8 24.1 reduce-scatter.17
  677.2 133.8 reduce-scatter.39
  813.8 129.7 reduce-scatter.27
  946.3 129.7 reduce-scatter.29
  1078.9 132.7 reduce-scatter.31
  1214.4 133.0 reduce-scatter.25
  1354.5 110.5 reduce-scatter.23
  1471.3 113.8 reduce-scatter.19
  1587.9 182.6 reduce-scatter.33
  1773.7 184.4 reduce-scatter.35
  1961.2 184.4 reduce-scatter.37
  2148.7 162.7 reduce-scatter.21
where the time goes:
time: 2330 us; the launch traced here: 2320 us
  waiting for transfers between devices  1720 us (74%)
  blocking collectives  272 us (12%)
  matrix products  174 us (7%)
  local copies, waits for them, and re-layouts  64.8 us (3%)
  other arithmetic  58.8 us (3%)
    reduce_scatter x1, waiting for transfers between devices, body(): lax.psum_scatter(grad_up, ('dp', 'seq'), scatter_dimension=0, tiled=True)  188 us
    reduce_scatter x1, waiting for transfers between devices, body(): lax.psum_scatter(grad_down, ('dp', 'seq'), scatter_dimension=0, tiled=True)  187 us
    reduce_scatter x1, waiting for transfers between devices, body(): lax.psum_scatter(grad_gate, ('dp', 'seq'), scatter_dimension=0, tiled=True)  186 us
    reduce_scatter x1, waiting for transfers between devices, body(): lax.psum_scatter(rows_product(normed_low, mixed_grad_low), ('dp', 'seq'),...  166 us
    reduce_scatter x1, waiting for transfers between devices, body(): lax.psum_scatter(rows_product(normed_low, query_low), ('dp', 'seq'), scat...  136 us
    reduce_scatter x1, waiting for transfers between devices, body(): lax.psum_scatter(grad_output, ('dp', 'seq'), scatter_dimension=0, tiled=T...  136 us
    reduce_scatter x1, waiting for transfers between devices, body(): lax.psum_scatter(rows_product(normed_low, value_low), ('dp', 'seq'), scat...  132 us
    reduce_scatter x1, waiting for transfers between devices, body(): lax.psum_scatter(rows_product(normed_low, key_low), ('dp', 'seq'), scatte...  131 us
  transfers between devices with their start and end apart: 25, of which 18 were waited for; matrix products, arithmetic and copies ran while one was open for 10% of the time, Pallas kernels for 0%

commit v1 on v0

v1 whole, which is shorter than its diff:
```python
import jax
import jax.numpy as jnp
from jax import lax
from jax.sharding import PartitionSpec as P

HEADS = 8
KV_HEADS = 2
HEAD = 64
SSM_HEADS = 24
SSM_HEAD = 64
STATE = 128
CONV = 4


eps = 1e-05
rope_theta = 100000000000.0
score_scale = 0.125


def passed_along(x, axis, by):
    length = lax.axis_size(axis)
    pairs = [(i, i + by) for i in range(length) if 0 <= i + by < length]
    return lax.ppermute(x, axis, pairs)


def matmul(left, right):
    return jnp.dot(left, right, preferred_element_type=jnp.float32)


def rows_product(left, right):
    return lax.dot_general(
        left, right, (((0,), (0,)), ((), ())), preferred_element_type=jnp.float32
    )


def back_product(left, right):
    return lax.dot_general(
        left, right, (((1,), (1,)), ((), ())), preferred_element_type=jnp.float32
    )


def rms_scale(tensor, scale_gain):
    return tensor * lax.rsqrt(jnp.mean(tensor * tensor, axis=-1, keepdims=True) + eps) * scale_gain


def rotate(tensor, positions, direction):
    half_width = tensor.shape[-1] // 2
    frequency = rope_theta ** (-jnp.arange(half_width, dtype=jnp.float32) / half_width)
    angle = positions.astype(jnp.float32)[:, None] * frequency[None, :]
    cosine = jnp.cos(angle)[:, None, :]
    sine_part = direction * jnp.sin(angle)[:, None, :]
    first_half = tensor[..., :half_width]
    second_half = tensor[..., half_width:]
    return jnp.concatenate(
        [
            first_half * cosine - second_half * sine_part,
            second_half * cosine + first_half * sine_part,
        ],
        axis=-1,
    )


def conv_apply(extended, ext_segments, filter_taps, filter_bias):
    length = extended.shape[0] - CONV + 1
    own_segment = ext_segments[CONV - 1 :]
    summed = jnp.zeros((length, extended.shape[1]), jnp.float32) + filter_bias[None, :]
    for offset in range(CONV):
        match_mask = (ext_segments[offset : offset + length] == own_segment).astype(jnp.float32)[
            :, None
        ]
        summed = (
            summed + filter_taps[offset][None, :] * extended[offset : offset + length] * match_mask
        )
    return jax.nn.silu(summed)


def running_sum(x):
    order = jnp.arange(x.shape[0])
    earlier = (order[:, None] >= order[None, :]).astype(jnp.float32)
    return jnp.dot(earlier, x, precision=lax.Precision.HIGHEST)


def ssd_split(filtered, step_raw, step_bias, decay_log):
    length = filtered.shape[0]
    inner = SSM_HEADS * SSM_HEAD
    values = filtered[:, :inner].reshape(length, SSM_HEADS, SSM_HEAD)
    write_map = filtered[:, inner : inner + STATE]
    read_map = filtered[:, inner + STATE :]
    stride = jax.nn.softplus(step_raw + step_bias)
    running = running_sum(stride * -jnp.exp(decay_log))
    return (values, write_map, read_map, stride, running)


def ssd_state(filtered, step_raw, step_bias, decay_log, doc_ids, seg_prior):
    values, write_map, read_map, stride, running = ssd_split(
        filtered, step_raw, step_bias, decay_log
    )
    final_log = running[-1]
    keep_end = (doc_ids == doc_ids[-1]).astype(jnp.float32)[:, None]
    end_weights = jnp.exp(final_log[None, :] - running) * keep_end * stride
    end_state = jnp.einsum(
        "th,thd,tn->hdn", end_weights, values, write_map, precision=lax.Precision.HIGHEST
    )
    decay_total = jnp.exp(final_log) * (doc_ids[-1] == seg_prior).astype(jnp.float32)
    return (decay_total, end_state)


def ssd_output(
    filtered, step_raw, step_bias, decay_log, skip_gain, doc_ids, seg_prior, start_state
):
    values, write_map, read_map, stride, running = ssd_split(
        filtered, step_raw, step_bias, decay_log
    )
    length = filtered.shape[0]
    token_order = jnp.arange(length)
    allowed = (token_order[:, None] >= token_order[None, :]) & (
        doc_ids[:, None] == doc_ids[None, :]
    )
    gap_logs = running.T[:, :, None] - running.T[:, None, :]
    decay_mat = jnp.where(allowed[None], jnp.exp(jnp.minimum(gap_logs, 0.0)), 0.0)
    inner_prod = jnp.dot(read_map, write_map.T, precision=lax.Precision.HIGHEST)
    mixing = decay_mat * inner_prod[None] * stride.T[:, None, :]
    local_part = jnp.einsum("hts,shd->thd", mixing, values, precision=lax.Precision.HIGHEST)
    entering = (doc_ids == seg_prior).astype(jnp.float32)[:, None] * jnp.exp(running)
    carried = (
        jnp.einsum("hdn,tn->thd", start_state, read_map, precision=lax.Precision.HIGHEST)
        * entering[:, :, None]
    )
    summed = local_part + carried + skip_gain[None, :, None] * values
    return summed.reshape(length, SSM_HEADS * SSM_HEAD)


def gated_norm(ssm_out, gate_mix, mixer_gain):
    return rms_scale(ssm_out * jax.nn.silu(gate_mix), mixer_gain)


def swiglu(gate_val, up_val):
    return jax.nn.silu(gate_val) * up_val


def shift_along(x, line, by):
    axis, stride, size = line
    pairs = []
    for index in range(lax.axis_size(axis)):
        place = (index // stride) % size
        pairs.append((index, index + ((place + by) % size - place) * stride))
    return lax.ppermute(x, axis, pairs)


def mesh_lines():
    replicas, pieces = (lax.axis_size("dp"), lax.axis_size("seq"))
    across = 1
    while across * across * 2 <= pieces:
        across *= 2
    lines = {
        "core": ("dp", 1, 2),
        "z": ("dp", 2, replicas // 2),
        "x": ("seq", 1, across),
        "y": ("seq", across, pieces // across),
    }
    return lines


def place_on(line):
    axis, stride, size = line
    return (lax.axis_index(axis) // stride) % size


def tie(*groups):
    return lax.optimization_barrier(groups)


def gather_levels(packed, lines):
    return [packed] + [shift_along(packed, lines["z"], -d) for d in range(1, lines["z"][2])]


def spread(levels, cut, lines):
    owns = []
    for y_last in (True, False):
        first, second = ("x", "y") if y_last else ("y", "x")
        first_size, second_size = (lines[first][2], lines[second][2])
        part = jnp.concatenate([a[:, :cut] if y_last else a[:, cut:] for a in levels], axis=0)
        near = [part] + [shift_along(part, lines[first], -d) for d in range(1, first_size)]
        near = jnp.concatenate(near, axis=0)
        far = [near] + [shift_along(near, lines[second], -d) for d in range(1, second_size)]
        rows = part.shape[0]
        blocks = []
        for y in range(lines["y"][2]):
            for x in range(lines["x"][2]):
                outer, at = (y, x) if y_last else (x, y)
                blocks.append(far[outer][at * rows : (at + 1) * rows])
        owns.append(jnp.concatenate(blocks, axis=0))
    return [(own, shift_along(own, lines["core"], 1)) for own in owns]


def relative_index(row_counts, lines):
    levels, rows_out, across = (lines["z"][2], lines["y"][2], lines["x"][2])
    total = sum(row_counts)
    places = []
    start = 0
    for rows in row_counts:
        column = jnp.arange(levels * 2 * rows_out * across * rows)
        row = column % rows
        device = column // rows
        x = (device % across - place_on(lines["x"])) % across
        y = (device // across % rows_out - place_on(lines["y"])) % rows_out
        core = (device // (across * rows_out) - place_on(lines["core"])) % 2
        level = (device // (across * rows_out * 2) - place_on(lines["z"])) % levels
        block = ((core * rows_out + y) * across + x) * levels + level
        places.append(block * total + start + row)
        start += rows
    return jnp.concatenate(places) if len(places) > 1 else places[0]


def permutation(row_counts, lines):
    index = relative_index(row_counts, lines)
    return (index[:, None] == jnp.arange(index.shape[0])[None, :]).astype(jnp.bfloat16)


def to_relative(low, order):
    return matmul(low, order).astype(jnp.bfloat16)


def from_relative(wide, order):
    high = lax.reduce_precision(wide, 8, 7)
    rest = wide - high
    return back_product(high.astype(jnp.bfloat16), order) + back_product(
        rest.astype(jnp.bfloat16), order
    )


def product_rel(low_rel, weights):
    own, other = weights
    half = own.shape[0]
    return matmul(low_rel[:, :half], own) + matmul(low_rel[:, half:], other)


def back_rel(grad, weights):
    own, other = weights
    return jnp.concatenate([back_product(grad, own), back_product(grad, other)], axis=1)


def owed(items, lines):
    rows_out, across, levels = (lines["y"][2], lines["x"][2], lines["z"][2])
    theirs = []
    if items[0][0] is items[1][0]:
        left = items[0][0]
        grad = jnp.concatenate([items[0][1], items[1][1]], axis=1)
        theirs.append(rows_product(left[:, left.shape[1] // 2 :], grad).astype(jnp.bfloat16))
    else:
        for left, grad in items:
            theirs.append(rows_product(left[:, left.shape[1] // 2 :], grad).astype(jnp.bfloat16))
    received = [shift_along(part, lines["core"], 1) for part in theirs]
    received = yield received
    if len(received) == 1:
        width = items[0][1].shape[1]
        received = [received[0][:, :width], received[0][:, width:]]
    kept = []
    arrived = []
    for (left, grad), add, y_first in zip(items, received, (True, False)):
        first, second = ("y", "x") if y_first else ("x", "y")
        first_size, second_size = (lines[first][2], lines[second][2])
        block = left.shape[1] // 2 // (rows_out * across)

        def of_first(i):
            ids = [(i * across + j) if y_first else (j * across + i) for j in range(second_size)]
            rows = jnp.concatenate([left[:, k * block : (k + 1) * block] for k in ids], axis=1)
            more = jnp.concatenate([add[k * block : (k + 1) * block] for k in ids], axis=0)
            return rows_product(rows, grad) + more.astype(jnp.float32)

        kept.append(of_first(0))
        arrived.append(
            [
                shift_along(of_first(i).astype(jnp.bfloat16), lines[first], i)
                for i in range(1, first_size)
            ]
        )
    arrived = yield arrived
    sums = []
    sent = []
    for own, others, (left, grad), y_first in zip(kept, arrived, items, (True, False)):
        second = lines["x" if y_first else "y"]
        block = own.shape[0] // second[2]

        def of_second(j):
            summed = own[j * block : (j + 1) * block]
            for other in others:
                summed = summed + other[j * block : (j + 1) * block].astype(jnp.float32)
            return summed

        sums.append(of_second(0))
        sent.append(
            [
                shift_along(of_second(j).astype(jnp.bfloat16), second, j)
                for j in range(1, second[2])
            ]
        )
    sent = yield sent

    def of_level(k):
        parts = []
        for own, others in zip(sums, sent):
            rows = own.shape[0] // levels
            summed = own[k * rows : (k + 1) * rows]
            for other in others:
                summed = summed + other[k * rows : (k + 1) * rows].astype(jnp.float32)
            parts.append(summed)
        return jnp.concatenate(parts, axis=1)

    last = [
        shift_along(of_level(k).astype(jnp.bfloat16), lines["z"], k) for k in range(1, levels)
    ]
    last = yield last
    total = of_level(0)
    for part in last:
        total = total + part.astype(jnp.float32)
    width = items[0][1].shape[1]
    yield [total[:, :width], total[:, width:]]


def sum_everywhere(x):
    for axis in ("dp", "seq"):
        size = lax.axis_size(axis)
        step = 1
        while step < size:
            x = x + lax.ppermute(x, axis, [(i, i ^ step) for i in range(size)])
            step *= 2
    return x


def from_earlier(x, by):
    return passed_along(x, "seq", by)


def body(
    inputs,
    segments,
    cotangent,
    mixer_gate,
    mixer_input,
    mixer_step,
    mixer_output,
    query_weight,
    key_weight,
    value_weight,
    output_weight,
    gate_weight,
    up_weight,
    down_weight,
    input_gain,
    second_gain,
    mixer_gain,
    filter_taps,
    filter_bias,
    decay_log,
    step_bias,
    skip_gain,
):
    piece_index = lax.axis_index("seq")
    local_len = inputs.shape[1]
    seq_len = segments.shape[1]
    first_token = piece_index * local_len
    all_segs = segments[0]
    own_segments = lax.dynamic_slice_in_dim(all_segs, first_token, local_len)
    rim_start = jnp.maximum(first_token - (CONV - 1), 0)
    rim_segments = jnp.where(
        piece_index > 0, lax.dynamic_slice_in_dim(all_segs, rim_start, CONV - 1), -1
    )
    seg_before = rim_segments[CONV - 2]
    positions = first_token + jnp.arange(local_len)
    ext_segments = jnp.concatenate([rim_segments, own_segments])
    pieces = lax.axis_size("seq")
    lines = mesh_lines()
    inner = SSM_HEADS * SSM_HEAD
    query_width = HEADS * HEAD
    key_width = KV_HEADS * HEAD
    conv_width = mixer_input.shape[1]
    step_pad = jnp.pad(mixer_step, ((0, 0), (0, 128 - SSM_HEADS)))
    packed_first = jnp.concatenate(
        [mixer_gate, query_weight, step_pad, mixer_input, key_weight, value_weight], axis=1
    )
    first_cut = inner + query_width + step_pad.shape[1]
    packed_branch = jnp.concatenate(
        [jnp.concatenate([mixer_output, output_weight], axis=0), down_weight], axis=1
    )
    packed_up = jnp.concatenate([gate_weight, up_weight], axis=1)
    levels_first = gather_levels(packed_first, lines)
    levels_first, packed_branch = tie(levels_first, packed_branch)
    levels_branch = gather_levels(packed_branch, lines)
    w_first, w_second = spread(levels_first, first_cut, lines)
    w_first, w_second, packed_up, levels_branch = tie(w_first, w_second, packed_up, levels_branch)
    levels_up = gather_levels(packed_up, lines)
    w_branch, w_down = spread(levels_branch, output_weight.shape[1], lines)
    w_gate, w_up = spread(levels_up, gate_weight.shape[1], lines)
    order_tokens = permutation((mixer_gate.shape[0],), lines)
    order_branch = permutation((mixer_output.shape[0], output_weight.shape[0]), lines)
    order_hidden = permutation((down_weight.shape[0],), lines)
    tokens = inputs[0].astype(jnp.float32)
    normed, norm_back = jax.vjp(rms_scale, tokens, input_gain)
    normed_low = normed.astype(jnp.bfloat16)
    normed_rel = to_relative(normed_low, order_tokens)
    first_out = product_rel(normed_rel, w_first)
    second_out = product_rel(normed_rel, w_second)
    gate_mix = first_out[:, :inner]
    queries = first_out[:, inner : inner + query_width]
    step_raw = first_out[:, inner + query_width : inner + query_width + SSM_HEADS]
    mixed_raw = second_out[:, :conv_width].astype(jnp.bfloat16)
    keys_raw = second_out[:, conv_width : conv_width + key_width]
    values_low = second_out[:, conv_width + key_width :].astype(jnp.bfloat16)
    rim_rows = passed_along(mixed_raw[local_len - CONV + 1 :], "seq", 1)
    extended = jnp.concatenate([rim_rows, mixed_raw], axis=0).astype(jnp.float32)

    def filter_fn(ext_rows, taps, bias):
        return conv_apply(ext_rows, ext_segments, taps, bias)

    filtered, filter_back = jax.vjp(filter_fn, extended, filter_taps, filter_bias)
    filtered_low = lax.optimization_barrier(filtered.astype(jnp.bfloat16)).astype(jnp.float32)

    def state_fn(xc_rows, step_in, bias, decay):
        return ssd_state(xc_rows, step_in, bias, decay, own_segments, seg_before)

    (carry_decay, carry_state), state_back = jax.vjp(
        state_fn, filtered_low, step_raw, step_bias, decay_log
    )
    state_rows = SSM_HEADS * SSM_HEAD
    packed_state = jnp.concatenate(
        [
            carry_state.reshape(state_rows, STATE),
            jnp.broadcast_to(carry_decay[:, None], (SSM_HEADS, STATE)),
        ]
    ).astype(jnp.bfloat16)
    earlier_states = [from_earlier(packed_state, d) for d in range(1, pieces)]
    later_decays = [
        from_earlier(packed_state[state_rows:, :1], -d)[:, 0].astype(jnp.float32)
        for d in range(1, pieces)
    ]
    start_state = jnp.zeros_like(carry_state)
    for d in range(pieces - 1, 0, -1):
        there = earlier_states[d - 1].astype(jnp.float32)
        start_state = (
            there[state_rows:, :1][:, :, None] * start_state
            + there[:state_rows].reshape(SSM_HEADS, SSM_HEAD, STATE)
        )
    incoming = (None, start_state)

    def output_fn(xc_rows, step_in, bias, decay, skip, start_state):
        return ssd_output(
            xc_rows, step_in, bias, decay, skip, own_segments, seg_before, start_state
        )

    ssm_out, output_back = jax.vjp(
        output_fn, filtered_low, step_raw, step_bias, decay_log, skip_gain, incoming[1]
    )
    gated_out, gated_back = jax.vjp(gated_norm, ssm_out, gate_mix, mixer_gain)
    gated_low = gated_out.astype(jnp.bfloat16)
    query_rot = rotate(queries.reshape(local_len, HEADS, HEAD), positions, 1.0).astype(jnp.bfloat16)
    key_rot = rotate(keys_raw.reshape(local_len, KV_HEADS, HEAD), positions, 1.0).astype(
        jnp.bfloat16
    )
    own_keys = jnp.concatenate([key_rot.reshape(local_len, key_width), values_low], axis=1)
    all_keys = jnp.concatenate(
        [own_keys] + [from_earlier(own_keys, d) for d in range(1, pieces)], axis=0
    )
    key_positions = jnp.concatenate([positions - d * local_len for d in range(pieces)])
    key_segments = jnp.concatenate(
        [
            lax.dynamic_slice_in_dim(all_segs, jnp.maximum(first_token - d * local_len, 0), local_len)
            for d in range(pieces)
        ]
    )
    allowed = (
        (key_positions[None, :] <= positions[:, None])
        & (key_positions >= 0)[None, :]
        & (key_segments[None, :] == own_segments[:, None])
    )
    repeat = HEADS // KV_HEADS

    def group_scores(group_index):
        query_group = query_rot[:, group_index * repeat : (group_index + 1) * repeat]
        key_group = all_keys[:, group_index * HEAD : (group_index + 1) * HEAD]
        value_group = all_keys[:, key_width + group_index * HEAD : key_width + (group_index + 1) * HEAD]
        scores = (
            jnp.einsum("prd,kd->rpk", query_group, key_group, preferred_element_type=jnp.float32)
            * score_scale
        )
        return (query_group, key_group, value_group, jnp.where(allowed[None], scores, -1e30))

    group_lse = []
    group_out = []
    group_exact = []
    for group_index in range(KV_HEADS):
        query_group, key_group, value_group, scores = group_scores(group_index)
        top = jnp.max(scores, axis=-1)
        lse_group = top + jnp.log(jnp.sum(jnp.exp(scores - top[..., None]), axis=-1))
        probs = jnp.exp(scores - lse_group[..., None])
        group_out.append(
            jnp.einsum(
                "rpk,kd->prd",
                probs.astype(jnp.bfloat16),
                value_group,
                preferred_element_type=jnp.float32,
            )
        )
        group_exact.append(
            jnp.einsum(
                "rpk,kd->prd",
                probs,
                value_group.astype(jnp.float32),
                preferred_element_type=jnp.float32,
            )
        )
        group_lse.append(lse_group)
    attended = jnp.concatenate(group_out, axis=1)
    attended_low = attended.reshape(local_len, HEADS * HEAD).astype(jnp.bfloat16)
    branch_rel = to_relative(jnp.concatenate([gated_low, attended_low], axis=1), order_branch)
    middle = tokens + product_rel(branch_rel, w_branch)
    second, second_back = jax.vjp(rms_scale, middle, second_gain)
    second_low = second.astype(jnp.bfloat16)
    second_rel = to_relative(second_low, order_tokens)
    gate_val = product_rel(second_rel, w_gate)
    up_val = product_rel(second_rel, w_up)
    activated, act_back = jax.vjp(swiglu, gate_val, up_val)
    activated_low = activated.astype(jnp.bfloat16)
    activated_rel = to_relative(activated_low, order_hidden)
    result = (middle + product_rel(activated_rel, w_down)).astype(jnp.bfloat16)
    upstream = cotangent[0].astype(jnp.float32)
    upstream_low = upstream.astype(jnp.bfloat16)
    grad_act = from_relative(back_rel(upstream_low, w_down), order_hidden)
    grad_gate_val, grad_up_val = act_back(grad_act)
    gate_grad_low = grad_gate_val.astype(jnp.bfloat16)
    up_grad_low = grad_up_val.astype(jnp.bfloat16)
    sum_up = owed([(second_rel, gate_grad_low), (second_rel, up_grad_low)], lines)
    up_wait = next(sum_up)
    grad_second = from_relative(
        back_rel(gate_grad_low, w_gate) + back_rel(up_grad_low, w_up), order_tokens
    )
    grad_middle, grad_second_gain = second_back(grad_second)
    grad_middle = grad_middle + upstream
    grad_middle, up_wait = tie(grad_middle, up_wait)
    up_wait = sum_up.send(up_wait)
    branch_low = grad_middle.astype(jnp.bfloat16)
    sum_branch = owed([(activated_rel, upstream_low), (branch_rel, branch_low)], lines)
    branch_wait = next(sum_branch)
    grad_branch = from_relative(back_rel(branch_low, w_branch), order_branch)
    grad_gated = grad_branch[:, :inner]
    grad_attn = grad_branch[:, inner:].astype(jnp.bfloat16).reshape(local_len, HEADS, HEAD)
    grad_ssm, grad_zgate, grad_mixer_gain = gated_back(grad_gated)
    zgate_low = grad_zgate.astype(jnp.bfloat16)
    grad_ssm, zgate_low, branch_wait, up_wait = tie(grad_ssm, zgate_low, branch_wait, up_wait)
    branch_wait = sum_branch.send(branch_wait)
    up_wait = sum_up.send(up_wait)
    query_grads = []
    key_grads = []
    value_grads = []
    for group_index in range(KV_HEADS):
        query_group, key_group, value_group, scores = group_scores(group_index)
        grad_group = grad_attn[:, group_index * repeat : (group_index + 1) * repeat]
        lse_group = group_lse[group_index]
        row_delta = jnp.einsum(
            "prd,prd->rp", grad_group.astype(jnp.float32), group_exact[group_index]
        )
        probs = jnp.exp(scores - lse_group[..., None])
        value_grads.append(
            jnp.einsum(
                "rpk,prd->kd",
                probs.astype(jnp.bfloat16),
                grad_group,
                preferred_element_type=jnp.float32,
            )
        )
        grad_probs = jnp.einsum(
            "prd,kd->rpk", grad_group, value_group, preferred_element_type=jnp.float32
        )
        grad_scores = (probs * (grad_probs - row_delta[..., None])).astype(jnp.bfloat16)
        query_grads.append(
            score_scale
            * jnp.einsum("rpk,kd->prd", grad_scores, key_group, preferred_element_type=jnp.float32)
        )
        key_grads.append(
            score_scale
            * jnp.einsum("rpk,prd->kd", grad_scores, query_group, preferred_element_type=jnp.float32)
        )
    keys_part = jnp.concatenate(key_grads + value_grads, axis=1)
    keys_total = keys_part[:local_len]
    for d in range(1, pieces):
        sent = keys_part[d * local_len : (d + 1) * local_len].astype(jnp.bfloat16)
        keys_total = keys_total + from_earlier(sent, -d).astype(jnp.float32)
    key_total = keys_total[:, :key_width]
    value_total = keys_total[:, key_width:]
    query_low = (
        rotate(jnp.concatenate(query_grads, axis=1), positions, -1.0)
        .reshape(local_len, HEADS * HEAD)
        .astype(jnp.bfloat16)
    )
    key_low = (
        rotate(key_total.reshape(local_len, KV_HEADS, HEAD), positions, -1.0)
        .reshape(local_len, KV_HEADS * HEAD)
        .astype(jnp.bfloat16)
    )
    value_low = value_total.astype(jnp.bfloat16)
    head_low = jnp.concatenate([query_low, key_low, value_low], axis=1)
    sum_heads = owed([(normed_rel, zgate_low), (normed_rel, head_low)], lines)
    grad_ssm, query_low, branch_wait, up_wait = tie(grad_ssm, query_low, branch_wait, up_wait)
    branch_wait = sum_branch.send(branch_wait)
    up_wait = sum_up.send(up_wait)
    xc_first, step_first, bias_first, decay_first, grad_skip, grad_incoming = output_back(grad_ssm)
    heads_wait = next(sum_heads)
    grad_incoming, branch_wait, up_wait = tie(grad_incoming, branch_wait, up_wait)
    branch_wait = sum_branch.send(branch_wait)
    grad_gate, grad_up = sum_up.send(up_wait)
    packed_grad = grad_incoming.astype(jnp.bfloat16)
    carried = jnp.zeros_like(grad_incoming)
    for d in range(pieces - 1, 0, -1):
        there = from_earlier(packed_grad, -d).astype(jnp.float32)
        carried = later_decays[d - 1][:, None, None] * carried + there
    grad_decay_total = jnp.sum(carried * incoming[1], axis=(1, 2))
    xc_second, step_second, bias_second, decay_second = state_back((grad_decay_total, carried))
    xc_second, branch_wait, heads_wait = tie(xc_second, branch_wait, heads_wait)
    grad_down, grad_branch_rows = sum_branch.send(branch_wait)
    heads_wait = sum_heads.send(heads_wait)
    grad_ext, grad_taps, grad_fbias = filter_back(xc_first + xc_second)
    returned = passed_along(grad_ext[: CONV - 1], "seq", -1)
    grad_mixed = grad_ext[CONV - 1 :] + jnp.pad(returned, ((local_len - CONV + 1, 0), (0, 0)))
    mixed_grad_low = grad_mixed.astype(jnp.bfloat16)
    step_grad_low = (step_first + step_second).astype(jnp.bfloat16)
    mixed_grad_low, heads_wait = tie(mixed_grad_low, heads_wait)
    heads_wait = sum_heads.send(heads_wait)
    step_pad_low = jnp.pad(step_grad_low, ((0, 0), (0, 128 - SSM_HEADS)))
    cut = (conv_width + 128) // 256 * 128
    mixed_first = mixed_grad_low[:, :cut]
    mixed_rest = jnp.concatenate([mixed_grad_low[:, cut:], step_pad_low], axis=1)
    sum_mixed = owed([(normed_rel, mixed_first), (normed_rel, mixed_rest)], lines)
    mixed_wait = next(sum_mixed)
    mixed_wait = sum_mixed.send(mixed_wait)
    mixed_wait, heads_wait = tie(mixed_wait, heads_wait)
    heads_wait = sum_heads.send(heads_wait)
    grad_mixer_gate, grad_heads = sum_heads.send(heads_wait)
    mixed_wait = sum_mixed.send(mixed_wait)
    mixed_wait = sum_mixed.send(mixed_wait)
    grad_mixed_first, grad_mixed_rest = sum_mixed.send(mixed_wait)
    first_low = jnp.concatenate([zgate_low, query_low, step_pad_low], axis=1)
    second_grad_low = jnp.concatenate([mixed_grad_low, key_low, value_low], axis=1)
    grad_normed = from_relative(
        back_rel(first_low, w_first) + back_rel(second_grad_low, w_second), order_tokens
    )
    rest_width = conv_width - cut
    mixer_rows = mixer_output.shape[0]
    mixer_grads = (
        grad_mixer_gate,
        jnp.concatenate([grad_mixed_first, grad_mixed_rest[:, :rest_width]], axis=1),
        grad_mixed_rest[:, rest_width : rest_width + SSM_HEADS],
        grad_branch_rows[:mixer_rows],
        grad_heads[:, :query_width],
        grad_heads[:, query_width : query_width + key_width],
        grad_heads[:, query_width + key_width :],
        grad_branch_rows[mixer_rows:],
    )
    ffn_grads = (grad_gate, grad_up, grad_down)
    grad_tokens, grad_input_gain = norm_back(grad_normed)
    grad_tokens = grad_tokens + grad_middle
    small = (
        grad_input_gain,
        grad_second_gain,
        grad_mixer_gain,
        grad_taps,
        grad_fbias,
        decay_first + decay_second,
        bias_first + bias_second,
        grad_skip,
    )
    sizes = [part.size for part in small]
    length = sum(sizes)
    flat = jnp.pad(
        jnp.concatenate([part.reshape(-1) for part in small]), (0, -length % 1024)
    ).reshape(-1, 128)
    flat = sum_everywhere(flat).reshape(-1)
    small_sums = []
    start = 0
    for part in small:
        small_sums.append(flat[start : start + part.size].reshape(part.shape))
        start += part.size
    return (
        result[None],
        grad_tokens[None],
        mixer_grads[0],
        mixer_grads[1],
        mixer_grads[2],
        mixer_grads[3],
        mixer_grads[4],
        mixer_grads[5],
        mixer_grads[6],
        mixer_grads[7],
        ffn_grads[0],
        ffn_grads[1],
        ffn_grads[2],
        small_sums[0],
        small_sums[1],
        small_sums[2],
        small_sums[3],
        small_sums[4],
        small_sums[5],
        small_sums[6],
        small_sums[7],
    )


def solution(mesh):
    placed = (
        P("dp", "seq", None),
        P("dp", None),
        P("dp", "seq", None),
        P(("dp", "seq"), None),
        P(("dp", "seq"), None),
        P(("dp", "seq"), None),
        P(("dp", "seq"), None),
        P(("dp", "seq"), None),
        P(("dp", "seq"), None),
        P(("dp", "seq"), None),
        P(("dp", "seq"), None),
        P(("dp", "seq"), None),
        P(("dp", "seq"), None),
        P(("dp", "seq"), None),
        P(),
        P(),
        P(),
        P(),
        P(),
        P(),
        P(),
        P(),
    )
    return jax.shard_map(
        body,
        mesh=mesh,
        in_specs=placed,
        out_specs=(
            P("dp", "seq", None),
            P("dp", "seq", None),
            P(("dp", "seq"), None),
            P(("dp", "seq"), None),
            P(("dp", "seq"), None),
            P(("dp", "seq"), None),
            P(("dp", "seq"), None),
            P(("dp", "seq"), None),
            P(("dp", "seq"), None),
            P(("dp", "seq"), None),
            P(("dp", "seq"), None),
            P(("dp", "seq"), None),
            P(("dp", "seq"), None),
            P(),
            P(),
            P(),
            P(),
            P(),
            P(),
            P(),
            P(),
        ),
        check_vma=False,
    )
```

time: 2330 us -> 641 us (0.28)
  waiting for transfers between devices: 1720 us -> 191 us
  blocking collectives: 272 us -> 0 us
  starting transfers between devices: 3.51 us -> 118 us
  local copies, waits for them, and re-layouts: 64.8 us -> 94.2 us
  matrix products: 174 us -> 149 us
    reduce_scatter x12 -> x0, waiting for transfers between devices: 1510 us -> none  [the longest x1 188 us: body(): lax.psum_scatter(grad_up, ('dp', 'seq'), scatter_dimension=0, tiled=True)]
    all_gather x6 -> x0, blocking collectives: 231 us -> none  [the longest x1 71.4 us: body(): lax.all_gather(mixer_step, ('dp', 'seq'), axis=0, tiled=True)]
    all_gather x10 -> x0, waiting for transfers between devices: 195 us -> none  [the longest x1 58.7 us: body(): lax.all_gather(down_weight, ('dp', 'seq'), axis=0, tiled=True)]
    ppermute x0 -> x65, waiting for transfers between devices: none -> 142 us  [the longest x60 138 us: shift_along(): return lax.ppermute(x, axis, pairs)]
    ppermute x0 -> x65, starting transfers between devices: none -> 84.3 us  [the longest x60 73.1 us: shift_along(): return lax.ppermute(x, axis, pairs)]
    ppermute x2 -> x17, waiting for transfers between devices: 4.25 us -> 48.7 us  [passed_along(): return lax.ppermute(x, axis, pairs)]
    psum x1 -> x0, blocking collectives: 41.4 us -> none  [body(): lax.psum((grad_input_gain, grad_second_gain, grad_mixer_gain, grad_taps,...]
    ppermute x2 -> x17, starting transfers between devices: 2.58 us -> 33.9 us  [passed_along(): return lax.ppermute(x, axis, pairs)]
  transfers between devices with their start and end apart: 25 -> 82, of which waited for: 18 -> 31; matrix products, arithmetic and copies ran while one was open for 10% -> 35% of each run, Pallas kernels for 0% -> 0%
where the time goes in v1:
time: 641 us; the launch traced here: 630 us
  waiting for transfers between devices  191 us (30%)
  matrix products  149 us (23%)
  starting transfers between devices  118 us (18%)
  local copies, waits for them, and re-layouts  94.2 us (15%)
  other arithmetic  73 us (11%)
    ppermute x60, waiting for transfers between devices, shift_along(): return lax.ppermute(x, axis, pairs)  138 us
    ppermute x60, starting transfers between devices, shift_along(): return lax.ppermute(x, axis, pairs)  73.1 us
    ppermute x17, waiting for transfers between devices, passed_along(): return lax.ppermute(x, axis, pairs)  48.7 us
    dot_general x20, matrix products, back_product(): lax.dot_general(left, right, (((1,), (1,)), ((), ())), preferred_element_...  43.2 us
    unnamed x387, local copies, waits for them, and re-layouts  35.5 us
    ppermute x17, starting transfers between devices, passed_along(): return lax.ppermute(x, axis, pairs)  33.9 us
    dot_general x16, matrix products, matmul(): return jnp.dot(left, right, preferred_element_type=jnp.float32)  30.9 us
    dot_general x21, matrix products, rows_product(): lax.dot_general(left, right, (((0,), (0,)), ((), ())), preferred_element_...  25.7 us
  transfers between devices with their start and end apart: 82, of which 31 were waited for; matrix products, arithmetic and copies ran while one was open for 35% of the time, Pallas kernels for 0%

profile of v1, /device:TPU:0, one launch (start us, length us, event | category | flops | bytes accessed | tf_op | source)
XLA Modules:
  0.0 630.5 jit_solution(156298822356278390)
XLA Ops:
  5.4 5.0 collective-permute-start
  17.4 16.1 %collective-permute-done.1 = bf16[32,4224]{1,0:T(8,128)(2,1)S(1)} collective-permute-done((bf16[32,4224]{1,0:T(8,128)(2,1)S(1)}, bf16[32,4224]{1,0:T(8,128)(2,1)S(1)}, u32[]{:S(2)}, u32[]{:S(2)}) %collective-permute-start.1) | collective-permute-done | bytes 270368 | tf_op jit(solution)/shard_map/ppermute | solution.py:147
  42.2 7.6 %collective-permute-done.6 = bf16[128,2048]{1,0:T(8,128)(2,1)S(1)} collective-permute-done((bf16[128,2048]{1,0:T(8,128)(2,1)S(1)}, bf16[128,2048]{1,0:T(8,128)(2,1)S(1)}, u32[]{:S(2)}, u32[]{:S(2)}) %collective-permute-start.6) | collective-permute-done | bytes 524320 | tf_op jit(solution)/shard_map/ppermute | solution.py:147
  51.4 4.9 collective-permute-done.3
  57.9 18.4 %collective-permute-done.7 = bf16[256,2048]{1,0:T(8,128)(2,1)S(1)} collective-permute-done((bf16[256,2048]{1,0:T(8,128)(2,1)S(1)}, bf16[256,2048]{1,0:T(8,128)(2,1)S(1)}, u32[]{:S(2)}, u32[]{:S(2)}) %collective-permute-start.7) | collective-permute-done | bytes 1048608 | tf_op jit(solution)/shard_map/ppermute | solution.py:147
  99.3 18.4 %collective-permute-done.10 = bf16[64,2048]{1,0:T(8,128)(2,1)S(1)} collective-permute-done((bf16[64,2048]{1,0:T(8,128)(2,1)S(1)}, bf16[64,2048]{1,0:T(8,128)(2,1)S(1)}, u32[]{:S(2)}, u32[]{:S(2)}) %collective-permute-start.10) | collective-permute-done | bytes 262176 | tf_op jit(solution)/shard_map/ppermute | solution.py:147
  123.9 4.0 collective-permute-start.18
  159.3 4.5 collective-permute-start.12
  164.4 5.8 collective-permute-done.12
  170.9 3.9 multiply_convert_fusion.2
  192.1 3.7 collective-permute-start.13
  212.1 7.0 %collective-permute-start.25 = (bf16[128,2048]{1,0:T(8,128)(2,1)}, bf16[128,2048]{1,0:T(8,128)(2,1)}, u32[]{:S(2)}, u32[]{:S(2)}) collective-permute-start(bf16[128,2048]{1,0:T(8,128)(2,1)} %pad_maximum_fusion.9), channel_id=1, source_target_pairs={{0,1},{1,0},{2,3},{3,2},{4,5},{5,4},{6,7},{7,6},{8,9},{9,8},{10,11... | collective-permute-start | bytes 1572872 | tf_op jit(solution)/shard_map/ppermute | solution.py:147
  229.9 5.0 fusion.92
  242.9 3.7 fusion.56
  254.8 8.0 %collective-permute-done.20 = bf16[512,1024]{1,0:T(8,128)(2,1)} collective-permute-done((bf16[512,1024]{1,0:T(8,128)(2,1)}, bf16[512,1024]{1,0:T(8,128)(2,1)}, u32[]{:S(2)}, u32[]{:S(2)}) %collective-permute-start.20) | collective-permute-done | bytes 1048608 | tf_op jit(solution)/shard_map/ppermute | solution.py:147
  265.1 3.7 collective-permute-done.32
  296.2 4.6 multiply_convert_fusion
  302.3 3.8 fusion.57
  355.6 20.8 %collective-permute-done.58 = bf16[256,256]{0,1:T(8,128)(2,1)S(1)} collective-permute-done((bf16[256,256]{0,1:T(8,128)(2,1)S(1)}, bf16[256,256]{0,1:T(8,128)(2,1)S(1)}, u32[]{:S(2)}, u32[]{:S(2)}) %collective-permute-start.58) | collective-permute-done | bytes 131104 | tf_op jit(solution)/shard_map/ppermute | solution.py:23
  378.1 5.3 collective-permute-done.57
  395.5 26.3 %collective-permute-done.41 = bf16[128,2048]{1,0:T(8,128)(2,1)S(1)} collective-permute-done((bf16[128,2048]{1,0:T(8,128)(2,1)S(1)}, bf16[128,2048]{1,0:T(8,128)(2,1)S(1)}, u32[]{:S(2)}, u32[]{:S(2)}) %collective-permute-start.41) | collective-permute-done | bytes 524320 | tf_op jit(solution)/shard_map/ppermute | solution.py:147
  421.9 8.8 %fusion.154 = (f32[24,256]{1,0:T(8,128)S(1)}, f32[24,256]{1,0:T(8,128)S(1)}, f32[24,256]{1,0:T(8,128)}, f32[256,256]{1,0:T(8,128)S(1)}) fusion(f32[24,256]{1,0:T(8,128)S(1)} %bitcast.333, f32[256,256]{1,0:T(8,128)S(1)} %copy-done.83, f32[24,256]{1,0:T(8,128)S(1)} %copy-done.133, pred[256,256]{1,0:T(8,128)(4,1)S(1)} %copy-done.118, ...), kind=kOutput, calls=%fused_computation.271 | convolution fusion | flops 1237760000 | bytes 3072000 | tf_op jit(solution)/shard_map/transpose(jvp(hts,shd->thd))/dot_general | solution.py:123
  431.4 6.8 %bitcast_add_fusion = f32[256,24,64]{0,2,1:T(8,128)} fusion(f32[256,24,64]{0,2,1:T(8,128)S(1)} %bitcast.313, f32[24,64,256]{2,1,0:T(8,128)S(1)} %bitcast.312, f32[24,256]{1,0:T(8,128)S(1)} %copy-done.133, f32[256,256]{1,0:T(8,128)S(1)} %copy-done.83, f32[24,256]{1,0:T(8,128)S(1)} %bitcast.334, pred[256,256]{1,0:T(8,128)(4,1)S(1)} %copy-done.118, ...), kind=kOutput, calls=%fused_computation.156 | convolution fusion | flops 1216610304 | bytes 5095520 | tf_op jit(solution)/shard_map/transpose(jvp(hts,shd->thd))/dot_general | solution.py:123
  458.6 6.4 %collective-permute-done.49 = bf16[32,4096]{1,0:T(8,128)(2,1)} collective-permute-done((bf16[32,4096]{1,0:T(8,128)(2,1)}, bf16[32,4096]{1,0:T(8,128)(2,1)}, u32[]{:S(2)}, u32[]{:S(2)}) %collective-permute-start.49) | collective-permute-done | bytes 262176 | tf_op jit(solution)/shard_map/ppermute | solution.py:147
  473.6 6.1 collective-permute-start.54
  484.1 4.3 collective-permute-done.52
  510.3 4.0 multiply_reduce_fusion.3
  515.7 3.7 pad_add_fusion
  544.9 5.0 collective-permute-done.63
  566.1 3.9 collective-permute-start.78
  613.0 4.1 collective-permute-done.70
  624.9 3.9 collective-permute-done.75
  (819 shorter events, 387.4 us)
Async XLA Ops:
  49.8 26.6 %collective-permute-start.7 = (bf16[256,2048]{1,0:T(8,128)(2,1)S(1)}, bf16[256,2048]{1,0:T(8,128)(2,1)S(1)}, u32[]{:S(2)}, u32[]{:S(2)}) collective-permute-start(bf16[256,2048]{1,0:T(8,128)(2,1)S(1)} %constant_dynamic-update-slice_fusion.17), channel_id=1, source_target_pairs={{0,1},{1,0},{2,3},{3,2},{4,5},{5,4},{6,7},{7,6},{8,9},{9,8},{10,11... | collective-permute-start | bytes 3145736 | tf_op jit(solution)/shard_map/ppermute | solution.py:147
  80.1 37.7 %collective-permute-start.5 = (bf16[512,2176]{1,0:T(8,128)(2,1)}, bf16[512,2176]{1,0:T(8,128)(2,1)}, u32[]{:S(2)}, u32[]{:S(2)}) collective-permute-start(bf16[512,2176]{1,0:T(8,128)(2,1)} %constant_dynamic-update-slice_fusion.11), channel_id=1, source_target_pairs={{0,4},{4,0},{8,12},{12,8},{16,20},{20,16},{24,28},{28,24},{1,5},{5... | collective-permute-start | bytes 6684680 | tf_op jit(solution)/shard_map/ppermute | solution.py:147
  81.0 36.8 %collective-permute-start.8 = (bf16[512,2048]{1,0:T(8,128)(2,1)}, bf16[512,2048]{1,0:T(8,128)(2,1)}, u32[]{:S(2)}, u32[]{:S(2)}) collective-permute-start(bf16[512,2048]{1,0:T(8,128)(2,1)} %slice_dynamic-update-slice_fusion.4), channel_id=1, source_target_pairs={{0,4},{4,0},{8,12},{12,8},{16,20},{20,16},{24,28},{28,24},{1,5},{5... | collective-permute-start | bytes 6291464 | tf_op jit(solution)/shard_map/ppermute | solution.py:147
  91.1 26.7 %collective-permute-start.10 = (bf16[64,2048]{1,0:T(8,128)(2,1)S(1)}, bf16[64,2048]{1,0:T(8,128)(2,1)S(1)}, u32[]{:S(2)}, u32[]{:S(2)}) collective-permute-start(bf16[64,2048]{1,0:T(8,128)(2,1)S(1)} %pad_maximum_fusion.26), channel_id=1, source_target_pairs={{0,16},{4,20},{8,24},{12,28},{16,0},{20,4},{24,8},{28,12},{1,17},{... | collective-permute-start | bytes 786440 | tf_op jit(solution)/shard_map/ppermute | solution.py:147
  94.4 23.3 %collective-permute-start.11 = (bf16[64,2048]{1,0:T(8,128)(2,1)S(1)}, bf16[64,2048]{1,0:T(8,128)(2,1)S(1)}, u32[]{:S(2)}, u32[]{:S(2)}) collective-permute-start(bf16[64,2048]{1,0:T(8,128)(2,1)S(1)} %pad_maximum_fusion.26), channel_id=1, source_target_pairs={{0,8},{4,12},{8,16},{12,20},{16,24},{20,28},{24,0},{28,4},{1,9},{5... | collective-permute-start | bytes 786440 | tf_op jit(solution)/shard_map/ppermute | solution.py:147
  123.9 55.2 %collective-permute-start.18 = (bf16[256,256]{0,1:T(8,128)(2,1)}, bf16[256,256]{0,1:T(8,128)(2,1)}, u32[]{:S(2)}, u32[]{:S(2)}) collective-permute-start(bf16[256,256]{0,1:T(8,128)(2,1)} %pad_maximum_fusion.42), channel_id=1, source_target_pairs={{0,3},{4,7},{8,11},{12,15},{16,19},{20,23},{24,27},{28,31}} | collective-permute-start | bytes 393224 | tf_op jit(solution)/shard_map/ppermute | solution.py:23
  127.9 52.9 %collective-permute-start.17 = (bf16[256,256]{0,1:T(8,128)(2,1)}, bf16[256,256]{0,1:T(8,128)(2,1)}, u32[]{:S(2)}, u32[]{:S(2)}) collective-permute-start(bf16[256,256]{0,1:T(8,128)(2,1)} %pad_maximum_fusion.42), channel_id=1, source_target_pairs={{0,2},{1,3},{4,6},{5,7},{8,10},{9,11},{12,14},{13,15},{16,18},{17,... | collective-permute-start | bytes 393224 | tf_op jit(solution)/shard_map/ppermute | solution.py:23
  129.9 53.5 %collective-permute-start.16 = (bf16[256,256]{0,1:T(8,128)(2,1)}, bf16[256,256]{0,1:T(8,128)(2,1)}, u32[]{:S(2)}, u32[]{:S(2)}) collective-permute-start(bf16[256,256]{0,1:T(8,128)(2,1)} %pad_maximum_fusion.42), channel_id=1, source_target_pairs={{0,1},{1,2},{2,3},{4,5},{5,6},{6,7},{8,9},{9,10},{10,11},{12,13},{... | collective-permute-start | bytes 393224 | tf_op jit(solution)/shard_map/ppermute | solution.py:23
  134.5 57.6 %collective-permute-start.22 = (bf16[32,4096]{1,0:T(8,128)(2,1)}, bf16[32,4096]{1,0:T(8,128)(2,1)}, u32[]{:S(2)}, u32[]{:S(2)}) collective-permute-start(bf16[32,4096]{1,0:T(8,128)(2,1)} %pad_maximum_fusion.27), channel_id=1, source_target_pairs={{0,24},{4,28},{8,0},{12,4},{16,8},{20,12},{24,16},{28,20},{1,25},{... | collective-permute-start | bytes 786440 | tf_op jit(solution)/shard_map/ppermute | solution.py:147
  170.1 27.5 %collective-permute-start.23 = (bf16[32,4096]{1,0:T(8,128)(2,1)}, bf16[32,4096]{1,0:T(8,128)(2,1)}, u32[]{:S(2)}, u32[]{:S(2)}) collective-permute-start(bf16[32,4096]{1,0:T(8,128)(2,1)} %pad_maximum_fusion.27), channel_id=1, source_target_pairs={{0,16},{4,20},{8,24},{12,28},{16,0},{20,4},{24,8},{28,12},{1,17},{... | collective-permute-start | bytes 786440 | tf_op jit(solution)/shard_map/ppermute | solution.py:147
  180.9 55.5 %collective-permute-start.19 = (bf16[256,1024]{1,0:T(8,128)(2,1)}, bf16[256,1024]{1,0:T(8,128)(2,1)}, u32[]{:S(2)}, u32[]{:S(2)}) collective-permute-start(bf16[256,1024]{1,0:T(8,128)(2,1)} %pad_maximum_fusion.8), channel_id=1, source_target_pairs={{0,1},{1,0},{2,3},{3,2},{4,5},{5,4},{6,7},{7,6},{8,9},{9,8},{10,11... | collective-permute-start | bytes 1572872 | tf_op jit(solution)/shard_map/ppermute | solution.py:147
  183.3 57.6 %collective-permute-start.31 = (bf16[256,1024]{1,0:T(8,128)(2,1)}, bf16[256,1024]{1,0:T(8,128)(2,1)}, u32[]{:S(2)}, u32[]{:S(2)}) collective-permute-start(bf16[256,1024]{1,0:T(8,128)(2,1)} %pad_maximum_fusion.11), channel_id=1, source_target_pairs={{0,2},{1,3},{2,0},{3,1},{4,6},{5,7},{6,4},{7,5},{8,10},{9,11},{10,... | collective-permute-start | bytes 1572872 | tf_op jit(solution)/shard_map/ppermute | solution.py:147
  206.0 42.9 %collective-permute-start.28 = (bf16[128,2048]{1,0:T(8,128)(2,1)}, bf16[128,2048]{1,0:T(8,128)(2,1)}, u32[]{:S(2)}, u32[]{:S(2)}) collective-permute-start(bf16[128,2048]{1,0:T(8,128)(2,1)} %pad_maximum_fusion.10), channel_id=1, source_target_pairs={{0,2},{1,3},{2,0},{3,1},{4,6},{5,7},{6,4},{7,5},{8,10},{9,11},{10,... | collective-permute-start | bytes 1572872 | tf_op jit(solution)/shard_map/ppermute | solution.py:147
  212.1 40.7 %collective-permute-start.25 = (bf16[128,2048]{1,0:T(8,128)(2,1)}, bf16[128,2048]{1,0:T(8,128)(2,1)}, u32[]{:S(2)}, u32[]{:S(2)}) collective-permute-start(bf16[128,2048]{1,0:T(8,128)(2,1)} %pad_maximum_fusion.9), channel_id=1, source_target_pairs={{0,1},{1,0},{2,3},{3,2},{4,5},{5,4},{6,7},{7,6},{8,9},{9,8},{10,11... | collective-permute-start | bytes 1572872 | tf_op jit(solution)/shard_map/ppermute | solution.py:147
  238.6 24.2 %collective-permute-start.20 = (bf16[512,1024]{1,0:T(8,128)(2,1)}, bf16[512,1024]{1,0:T(8,128)(2,1)}, u32[]{:S(2)}, u32[]{:S(2)}) collective-permute-start(bf16[512,1024]{1,0:T(8,128)(2,1)} %get-tuple-element.407), channel_id=1, source_target_pairs={{0,2},{1,3},{2,0},{3,1},{4,6},{5,7},{6,4},{7,5},{8,10},{9,11},{10,... | collective-permute-start | bytes 3145736 | tf_op jit(solution)/shard_map/ppermute | solution.py:147
  242.8 26.0 %collective-permute-start.32 = (bf16[512,1024]{1,0:T(8,128)(2,1)}, bf16[512,1024]{1,0:T(8,128)(2,1)}, u32[]{:S(2)}, u32[]{:S(2)}) collective-permute-start(bf16[512,1024]{1,0:T(8,128)(2,1)} %constant_dynamic-update-slice_fusion.59), channel_id=1, source_target_pairs={{0,1},{1,0},{2,3},{3,2},{4,5},{5,4},{6,7},{7,6},{8,9},{9,8},{10,11... | collective-permute-start | bytes 3145736 | tf_op jit(solution)/shard_map/ppermute | solution.py:147
  250.8 29.1 %collective-permute-start.29 = (bf16[256,2048]{1,0:T(8,128)(2,1)}, bf16[256,2048]{1,0:T(8,128)(2,1)S(1)}, u32[]{:S(2)}, u32[]{:S(2)}) collective-permute-start(bf16[256,2048]{1,0:T(8,128)(2,1)} %constant_dynamic-update-slice_fusion.49), channel_id=1, source_target_pairs={{0,1},{1,0},{2,3},{3,2},{4,5},{5,4},{6,7},{7,6},{8,9},{9,8},{10,11... | collective-permute-start | bytes 3145736 | tf_op jit(solution)/shard_map/ppermute | solution.py:147
  254.8 26.4 %collective-permute-start.26 = (bf16[256,2048]{1,0:T(8,128)(2,1)}, bf16[256,2048]{1,0:T(8,128)(2,1)S(1)}, u32[]{:S(2)}, u32[]{:S(2)}) collective-permute-start(bf16[256,2048]{1,0:T(8,128)(2,1)} %get-tuple-element.405), channel_id=1, source_target_pairs={{0,2},{1,3},{2,0},{3,1},{4,6},{5,7},{6,4},{7,5},{8,10},{9,11},{10,... | collective-permute-start | bytes 3145736 | tf_op jit(solution)/shard_map/ppermute | solution.py:147
  306.9 76.7 %collective-permute-start.35 = (bf16[1024,1024]{1,0:T(8,128)(2,1)S(1)}, bf16[1024,1024]{1,0:T(8,128)(2,1)}, u32[]{:S(2)}, u32[]{:S(2)}) collective-permute-start(bf16[1024,1024]{1,0:T(8,128)(2,1)S(1)} %convolution_convert_fusion.4), channel_id=1, source_target_pairs={{0,4},{4,0},{8,12},{12,8},{16,20},{20,16},{24,28},{28,24},{1,5},{5... | collective-permute-start | bytes 6291464 | tf_op jit(solution)/shard_map/ppermute | solution.py:147
  345.2 38.4 %collective-permute-start.36 = (bf16[1024,1024]{1,0:T(8,128)(2,1)S(1)}, bf16[1024,1024]{1,0:T(8,128)(2,1)S(1)}, u32[]{:S(2)}, u32[]{:S(2)}) collective-permute-start(bf16[1024,1024]{1,0:T(8,128)(2,1)S(1)} %convolution_convert_fusion.3), channel_id=1, source_target_pairs={{0,4},{4,0},{8,12},{12,8},{16,20},{20,16},{24,28},{28,24},{1,5},{5... | collective-permute-start | bytes 6291464 | tf_op jit(solution)/shard_map/ppermute | solution.py:147
  345.3 38.3 %collective-permute-start.37 = (bf16[256,2048]{1,0:T(8,128)(2,1)S(1)}, bf16[256,2048]{1,0:T(8,128)(2,1)S(1)}, u32[]{:S(2)}, u32[]{:S(2)}) collective-permute-start(bf16[256,2048]{1,0:T(8,128)(2,1)S(1)} %add_convert_fusion.2), channel_id=1, source_target_pairs={{0,2},{1,3},{2,0},{3,1},{4,6},{5,7},{6,4},{7,5},{8,10},{9,11},{10,... | collective-permute-start | bytes 3145736 | tf_op jit(solution)/shard_map/ppermute | solution.py:147
  350.6 32.9 %collective-permute-start.38 = (bf16[256,2048]{1,0:T(8,128)(2,1)S(1)}, bf16[256,2048]{1,0:T(8,128)(2,1)S(1)}, u32[]{:S(2)}, u32[]{:S(2)}) collective-permute-start(bf16[256,2048]{1,0:T(8,128)(2,1)S(1)} %fusion.55), channel_id=1, source_target_pairs={{0,1},{1,0},{2,3},{3,2},{4,5},{5,4},{6,7},{7,6},{8,9},{9,8},{10,11... | collective-permute-start | bytes 3145736 | tf_op jit(solution)/shard_map/ppermute | solution.py:147
  385.3 36.5 %collective-permute-start.39 = (bf16[512,1024]{1,0:T(8,128)(2,1)S(1)}, bf16[512,1024]{1,0:T(8,128)(2,1)S(1)}, u32[]{:S(2)}, u32[]{:S(2)}) collective-permute-start(bf16[512,1024]{1,0:T(8,128)(2,1)S(1)} %add_convert_fusion.1), channel_id=1, source_target_pairs={{0,2},{1,3},{2,0},{3,1},{4,6},{5,7},{6,4},{7,5},{8,10},{9,11},{10,... | collective-permute-start | bytes 3145736 | tf_op jit(solution)/shard_map/ppermute | solution.py:147
  386.7 35.1 %collective-permute-start.40 = (bf16[512,1024]{1,0:T(8,128)(2,1)S(1)}, bf16[512,1024]{1,0:T(8,128)(2,1)S(1)}, u32[]{:S(2)}, u32[]{:S(2)}) collective-permute-start(bf16[512,1024]{1,0:T(8,128)(2,1)S(1)} %add_convert_fusion), channel_id=1, source_target_pairs={{0,1},{1,0},{2,3},{3,2},{4,5},{5,4},{6,7},{7,6},{8,9},{9,8},{10,11... | collective-permute-start | bytes 3145736 | tf_op jit(solution)/shard_map/ppermute | solution.py:147
  387.2 34.7 %collective-permute-start.41 = (bf16[128,2048]{1,0:T(8,128)(2,1)S(1)}, bf16[128,2048]{1,0:T(8,128)(2,1)S(1)}, u32[]{:S(2)}, u32[]{:S(2)}) collective-permute-start(bf16[128,2048]{1,0:T(8,128)(2,1)S(1)} %get-tuple-element.311), channel_id=1, source_target_pairs={{0,1},{1,0},{2,3},{3,2},{4,5},{5,4},{6,7},{7,6},{8,9},{9,8},{10,11... | collective-permute-start | bytes 1572872 | tf_op jit(solution)/shard_map/ppermute | solution.py:147
  389.5 32.3 %collective-permute-start.42 = (bf16[128,2048]{1,0:T(8,128)(2,1)S(1)}, bf16[128,2048]{1,0:T(8,128)(2,1)S(1)}, u32[]{:S(2)}, u32[]{:S(2)}) collective-permute-start(bf16[128,2048]{1,0:T(8,128)(2,1)S(1)} %get-tuple-element.313), channel_id=1, source_target_pairs={{0,2},{1,3},{2,0},{3,1},{4,6},{5,7},{6,4},{7,5},{8,10},{9,11},{10,... | collective-permute-start | bytes 1572872 | tf_op jit(solution)/shard_map/ppermute | solution.py:147
  440.7 24.2 %collective-permute-start.46 = (bf16[256,1024]{1,0:T(8,128)(2,1)}, bf16[256,1024]{1,0:T(8,128)(2,1)}, u32[]{:S(2)}, u32[]{:S(2)}) collective-permute-start(bf16[256,1024]{1,0:T(8,128)(2,1)} %get-tuple-element.307), channel_id=1, source_target_pairs={{0,1},{1,0},{2,3},{3,2},{4,5},{5,4},{6,7},{7,6},{8,9},{9,8},{10,11... | collective-permute-start | bytes 1572872 | tf_op jit(solution)/shard_map/ppermute | solution.py:147
  458.5 50.2 %collective-permute-start.60 = (bf16[512,2304]{1,0:T(8,128)(2,1)}, bf16[512,2304]{1,0:T(8,128)(2,1)}, u32[]{:S(2)}, u32[]{:S(2)}) collective-permute-start(bf16[512,2304]{1,0:T(8,128)(2,1)} %convolution_convert_fusion.1), channel_id=1, source_target_pairs={{0,4},{4,0},{8,12},{12,8},{16,20},{20,16},{24,28},{28,24},{1,5},{5... | collective-permute-start | bytes 7077896 | tf_op jit(solution)/shard_map/ppermute | solution.py:147
  467.6 24.2 %collective-permute-start.51 = (bf16[24,64,128]{2,1,0:T(8,128)(2,1)S(1)}, bf16[24,64,128]{2,1,0:T(8,128)(2,1)S(1)}, u32[]{:S(2)}, u32[]{:S(2)}) collective-permute-start(bf16[24,64,128]{2,1,0:T(8,128)(2,1)S(1)} %fusion.93), channel_id=1, source_target_pairs={{3,0},{7,4},{11,8},{15,12},{19,16},{23,20},{27,24},{31,28}} | collective-permute-start | bytes 1179656 | tf_op jit(solution)/shard_map/ppermute | solution.py:23
  473.6 35.1 %collective-permute-start.54 = (bf16[64,2048]{1,0:T(8,128)(2,1)}, bf16[64,2048]{1,0:T(8,128)(2,1)}, u32[]{:S(2)}, u32[]{:S(2)}) collective-permute-start(bf16[64,2048]{1,0:T(8,128)(2,1)} %pad_maximum_fusion.33), channel_id=1, source_target_pairs={{0,8},{4,12},{8,16},{12,20},{16,24},{20,28},{24,0},{28,4},{1,9},{5... | collective-permute-start | bytes 786440 | tf_op jit(solution)/shard_map/ppermute | solution.py:147
  483.3 25.4 %collective-permute-start.55 = (bf16[64,2048]{1,0:T(8,128)(2,1)}, bf16[64,2048]{1,0:T(8,128)(2,1)}, u32[]{:S(2)}, u32[]{:S(2)}) collective-permute-start(bf16[64,2048]{1,0:T(8,128)(2,1)} %pad_maximum_fusion.34), channel_id=1, source_target_pairs={{0,16},{4,20},{8,24},{12,28},{16,0},{20,4},{24,8},{28,12},{1,17},{... | collective-permute-start | bytes 786440 | tf_op jit(solution)/shard_map/ppermute | solution.py:147
  565.5 23.1 %collective-permute-start.64 = (bf16[512,1920]{1,0:T(8,128)(2,1)S(1)}, bf16[512,1920]{1,0:T(8,128)(2,1)S(1)}, u32[]{:S(2)}, u32[]{:S(2)}) collective-permute-start(bf16[512,1920]{1,0:T(8,128)(2,1)S(1)} %convolution_convert_fusion.2), channel_id=1, source_target_pairs={{0,4},{4,0},{8,12},{12,8},{16,20},{20,16},{24,28},{28,24},{1,5},{5... | collective-permute-start | bytes 5898248 | tf_op jit(solution)/shard_map/ppermute | solution.py:147
  (233 other events, 2751.4 us)

commit v2 on v1

v2 whole, which is shorter than its diff:
```python
import functools

import jax
import jax.numpy as jnp
from jax import lax
from jax.experimental import pallas as pl
from jax.experimental.pallas import tpu as pltpu
from jax.sharding import PartitionSpec as P

HEADS = 8
KV_HEADS = 2
HEAD = 64
SSM_HEADS = 24
SSM_HEAD = 64
STATE = 128
CONV = 4


eps = 1e-05
rope_theta = 100000000000.0
score_scale = 0.125


def passed_along(x, axis, by):
    length = lax.axis_size(axis)
    pairs = [(i, i + by) for i in range(length) if 0 <= i + by < length]
    return lax.ppermute(x, axis, pairs)


def matmul(left, right):
    return jnp.dot(left, right, preferred_element_type=jnp.float32)


def rows_product(left, right):
    return lax.dot_general(
        left, right, (((0,), (0,)), ((), ())), preferred_element_type=jnp.float32
    )


def back_product(left, right):
    return lax.dot_general(
        left, right, (((1,), (1,)), ((), ())), preferred_element_type=jnp.float32
    )


def rms_scale(tensor, scale_gain):
    return tensor * lax.rsqrt(jnp.mean(tensor * tensor, axis=-1, keepdims=True) + eps) * scale_gain


def rotation_tables(positions):
    half_width = HEAD // 2
    frequency = rope_theta ** (-jnp.arange(half_width, dtype=jnp.float32) / half_width)
    angle = positions.astype(jnp.float32)[:, None] * frequency[None, :]
    cosine = jnp.cos(angle)
    sine = jnp.sin(angle)
    return (
        jnp.concatenate([cosine] * 4, axis=1),
        jnp.concatenate([-sine, sine, -sine, sine], axis=1),
    )


def conv_apply(extended, ext_segments, filter_taps, filter_bias):
    length = extended.shape[0] - CONV + 1
    own_segment = ext_segments[CONV - 1 :]
    summed = jnp.zeros((length, extended.shape[1]), jnp.float32) + filter_bias[None, :]
    for offset in range(CONV):
        match_mask = (ext_segments[offset : offset + length] == own_segment).astype(jnp.float32)[
            :, None
        ]
        summed = (
            summed + filter_taps[offset][None, :] * extended[offset : offset + length] * match_mask
        )
    return jax.nn.silu(summed)


def running_sum(x):
    order = jnp.arange(x.shape[0])
    earlier = (order[:, None] >= order[None, :]).astype(jnp.float32)
    return jnp.dot(earlier, x, precision=lax.Precision.HIGHEST)


def later_sum(x):
    order = jnp.arange(x.shape[0])
    later = (order[:, None] <= order[None, :]).astype(jnp.float32)
    return jnp.dot(later, x, precision=lax.Precision.HIGHEST)


PAIR = 128
DECAY_ROWS = 32


def dot_nn(left, right):
    return jnp.dot(left, right, preferred_element_type=jnp.float32)


def dot_nt(left, right):
    return lax.dot_general(
        left, right, (((1,), (1,)), ((), ())), preferred_element_type=jnp.float32
    )


def dot_tn(left, right):
    return lax.dot_general(
        left, right, (((0,), (0,)), ((), ())), preferred_element_type=jnp.float32
    )


def low(x):
    return x.astype(jnp.bfloat16)


def lane_index(shape):
    return lax.broadcasted_iota(jnp.int32, shape, 1)


def column_of(table, index):
    return jnp.sum(jnp.where(lane_index(table.shape) == index, table, 0.0), axis=1, keepdims=True)


def set_column(ref, index, column):
    table = ref[...]
    ref[...] = jnp.where(lane_index(table.shape) == index, column, table)


def by_head(first, second, shape):
    return jnp.where(lane_index(shape) < HEAD, first, second)


def whole_spec(shape):
    return pl.BlockSpec(shape, lambda i: (0,) * len(shape))


def pair_spec(rows):
    return pl.BlockSpec((rows, PAIR), lambda i: (0, i))


def state_spec():
    return pl.BlockSpec((PAIR, STATE), lambda i: (i, 0))


def call(kernel, grid, in_specs, out_specs, out_shape, scratch=(), flops=0):
    return pl.pallas_call(
        kernel,
        grid=(grid,),
        in_specs=in_specs,
        out_specs=out_specs,
        out_shape=out_shape,
        scratch_shapes=list(scratch),
        compiler_params=pltpu.CompilerParams(
            dimension_semantics=("arbitrary",), vmem_limit_bytes=40 * 1024 * 1024
        ),
        cost_estimate=pl.CostEstimate(flops=flops, bytes_accessed=4000000, transcendentals=0),
    )


def float_out(*shape):
    return jax.ShapeDtypeStruct(shape, jnp.float32)


def masked_products(read_ref, write_ref, seg_col, seg_row):
    products = dot_nt(read_ref[...], write_ref[...])
    row = lax.broadcasted_iota(jnp.int32, products.shape, 0)
    allowed = (row >= lane_index(products.shape)) & (seg_col[...] == seg_row[...])
    return jnp.where(allowed, products, 0.0)


def ssd_local_kernel(
    value_ref, write_ref, read_ref, run_ref, run_row, stride_row, end_ref, skip_ref, seg_col,
    seg_row, out_ref, state_ref, products,
):
    step = pl.program_id(0)

    @pl.when(step == 0)
    def _():
        products[...] = masked_products(read_ref, write_ref, seg_col, seg_row)

    value = value_ref[...]
    wide = value.astype(jnp.float32)
    outs = []
    for half in range(2):
        head = 2 * step + half
        gap = column_of(run_ref[...], head) - run_row[pl.ds(head, 1), :]
        mixing = jnp.exp(jnp.minimum(gap, 0.0)) * products[...] * stride_row[pl.ds(head, 1), :]
        outs.append(dot_nn(low(mixing), value))
    skip = by_head(
        column_of(skip_ref[...], 2 * step), column_of(skip_ref[...], 2 * step + 1), (1, PAIR)
    )
    out_ref[...] = by_head(outs[0], outs[1], wide.shape) + skip * wide
    weight = by_head(
        column_of(end_ref[...], 2 * step), column_of(end_ref[...], 2 * step + 1), wide.shape
    )
    state_ref[...] = dot_tn(low(weight * wide), write_ref[...])


def ssd_local(filtered, running, run_rows, stride_rows, end_weights, skip_gain, seg_col, seg_row):
    length = filtered.shape[0]
    pairs = SSM_HEADS // 2
    inner = SSM_HEADS * SSM_HEAD
    return call(
        ssd_local_kernel,
        pairs,
        [
            pair_spec(length),
            pl.BlockSpec((length, STATE), lambda i: (0, pairs)),
            pl.BlockSpec((length, STATE), lambda i: (0, pairs + 1)),
            whole_spec((length, SSM_HEADS)),
            whole_spec((SSM_HEADS, length)),
            whole_spec((SSM_HEADS, length)),
            whole_spec((length, SSM_HEADS)),
            whole_spec((1, SSM_HEADS)),
            whole_spec((length, 1)),
            whole_spec((1, length)),
        ],
        [pair_spec(length), state_spec()],
        [float_out(length, inner), float_out(inner, STATE)],
        [pltpu.VMEM((length, length), jnp.float32)],
        2 * SSM_HEADS * length * length * PAIR,
    )(
        filtered, filtered, filtered, running, run_rows, stride_rows, end_weights,
        skip_gain[None, :], seg_col, seg_row,
    )


def chained(message_refs, step):
    first = (lax.broadcasted_iota(jnp.int32, (PAIR, STATE), 0) // SSM_HEAD) == 0
    state = jnp.zeros((PAIR, STATE), jnp.float32)
    for block_ref, decay_ref in reversed(message_refs):
        decays = decay_ref[...].astype(jnp.float32)
        row = lax.broadcasted_iota(jnp.int32, decays.shape, 0)
        one = jnp.sum(jnp.where(row == 2 * step, decays, 0.0), axis=0, keepdims=True)
        two = jnp.sum(jnp.where(row == 2 * step + 1, decays, 0.0), axis=0, keepdims=True)
        state = jnp.where(first, one, two) * state + block_ref[...].astype(jnp.float32)
    return state


def message_specs(count):
    blocks = SSM_HEADS * SSM_HEAD // DECAY_ROWS
    return [
        spec
        for _ in range(count)
        for spec in (state_spec(), pl.BlockSpec((DECAY_ROWS, STATE), lambda i: (blocks, 0)))
    ]


def packed_message(states, decays):
    rows = jnp.broadcast_to(jnp.pad(decays, (0, DECAY_ROWS - SSM_HEADS))[:, None], (DECAY_ROWS, STATE))
    return jnp.concatenate([low(states), low(rows)])


def ssd_entering_kernel(local_ref, read_ref, enter_ref, *refs):
    message_refs, (out_ref, state_ref) = (refs[:-2], refs[-2:])
    step = pl.program_id(0)
    shape = local_ref.shape
    state_ref[...] = chained(list(zip(message_refs[::2], message_refs[1::2])), step)
    enter = by_head(
        column_of(enter_ref[...], 2 * step), column_of(enter_ref[...], 2 * step + 1), shape
    )
    out_ref[...] = local_ref[...] + enter * dot_nt(read_ref[...], low(state_ref[...]))


def ssd_entering(local, filtered, entering, messages):
    length = filtered.shape[0]
    pairs = SSM_HEADS // 2
    inner = SSM_HEADS * SSM_HEAD
    return call(
        ssd_entering_kernel,
        pairs,
        [
            pair_spec(length),
            pl.BlockSpec((length, STATE), lambda i: (0, pairs + 1)),
            whole_spec((length, SSM_HEADS)),
        ]
        + message_specs(len(messages)),
        [pair_spec(length), state_spec()],
        [float_out(*local.shape), float_out(inner, STATE)],
        (),
        2 * SSM_HEADS * length * STATE * SSM_HEAD,
    )(local, filtered, entering, *[m for message in messages for m in (message, message)])


def ssd_back_kernel(
    grad_ref, value_ref, write_ref, read_ref, run_ref, run_row, stride_row, enter_ref, skip_ref,
    state_ref, seg_col, seg_row, value_grad, state_grad, row_sum, col_sum, write_grad, read_grad,
    products, total,
):
    step = pl.program_id(0)

    @pl.when(step == 0)
    def _():
        products[...] = masked_products(read_ref, write_ref, seg_col, seg_row)
        total[...] = jnp.zeros_like(total)
        row_sum[...] = jnp.zeros_like(row_sum)
        read_grad[...] = jnp.zeros_like(read_grad)

    value = value_ref[...]
    grad = grad_ref[...]
    shape = grad.shape
    skip = by_head(
        column_of(skip_ref[...], 2 * step), column_of(skip_ref[...], 2 * step + 1), (1, PAIR)
    )
    enter = by_head(
        column_of(enter_ref[...], 2 * step), column_of(enter_ref[...], 2 * step + 1), shape
    )
    state = low(state_ref[...])
    read = read_ref[...]
    entered = enter * grad
    from_state = entered * dot_nt(read, state)
    entered = low(entered)
    state_grad[...] = dot_tn(entered, read)
    read_grad[...] += dot_nn(entered, state)
    into_values = skip * grad
    for half in range(2):
        head = 2 * step + half
        inside = (lane_index(shape) // HEAD) == half
        part = low(jnp.where(inside, grad, 0.0))
        gap = column_of(run_ref[...], head) - run_row[pl.ds(head, 1), :]
        decay = jnp.exp(jnp.minimum(gap, 0.0))
        strides = stride_row[pl.ds(head, 1), :]
        weighted = dot_nt(part, value) * decay
        total[...] += weighted * strides
        scaled = weighted * products[...]
        col_sum[pl.ds(head, 1), :] = jnp.sum(scaled, axis=0, keepdims=True)
        rows = jnp.sum(scaled * strides, axis=1, keepdims=True) + jnp.sum(
            jnp.where(inside, from_state, 0.0), axis=1, keepdims=True
        )
        set_column(row_sum, head, rows)
        mixing = decay * products[...] * strides
        into_values = into_values + dot_tn(low(mixing), part)
    value_grad[...] = into_values

    @pl.when(step == pl.num_programs(0) - 1)
    def _():
        sums = total[...]
        row = lax.broadcasted_iota(jnp.int32, sums.shape, 0)
        allowed = (row >= lane_index(sums.shape)) & (seg_col[...] == seg_row[...])
        sums = low(jnp.where(allowed, sums, 0.0))
        write_grad[...] = dot_tn(sums, read)
        read_grad[...] += dot_nn(sums, write_ref[...])


def ssd_back(
    grad, filtered, running, run_rows, stride_rows, entering, skip_gain, state, seg_col, seg_row
):
    length = filtered.shape[0]
    pairs = SSM_HEADS // 2
    inner = SSM_HEADS * SSM_HEAD
    return call(
        ssd_back_kernel,
        pairs,
        [
            pair_spec(length),
            pair_spec(length),
            pl.BlockSpec((length, STATE), lambda i: (0, pairs)),
            pl.BlockSpec((length, STATE), lambda i: (0, pairs + 1)),
            whole_spec((length, SSM_HEADS)),
            whole_spec((SSM_HEADS, length)),
            whole_spec((SSM_HEADS, length)),
            whole_spec((length, SSM_HEADS)),
            whole_spec((1, SSM_HEADS)),
            state_spec(),
            whole_spec((length, 1)),
            whole_spec((1, length)),
        ],
        [
            pair_spec(length),
            state_spec(),
            whole_spec((length, SSM_HEADS)),
            whole_spec((SSM_HEADS, length)),
            whole_spec((length, STATE)),
            whole_spec((length, STATE)),
        ],
        [
            float_out(length, inner),
            float_out(inner, STATE),
            float_out(length, SSM_HEADS),
            float_out(SSM_HEADS, length),
            float_out(length, STATE),
            float_out(length, STATE),
        ],
        [pltpu.VMEM((length, length), jnp.float32), pltpu.VMEM((length, length), jnp.float32)],
        4 * SSM_HEADS * length * length * PAIR,
    )(
        grad, filtered, filtered, filtered, running, run_rows, stride_rows, entering,
        skip_gain[None, :], state, seg_col, seg_row,
    )


def ssd_state_back_kernel(
    value_ref, write_ref, end_ref, before_ref, write_before, start_ref, *refs
):
    message_refs, (value_grad, end_grad, write_grad, decay_grad) = (refs[:-4], refs[-4:])
    step = pl.program_id(0)

    @pl.when(step == 0)
    def _():
        end_grad[...] = jnp.zeros_like(end_grad)
        write_grad[...] = write_before[...]
        decay_grad[...] = jnp.zeros_like(decay_grad)

    wide = value_ref[...].astype(jnp.float32)
    shape = wide.shape
    weight = by_head(
        column_of(end_ref[...], 2 * step), column_of(end_ref[...], 2 * step + 1), shape
    )
    carried = chained(list(zip(message_refs[::2], message_refs[1::2])), step)
    products = jnp.sum(carried * start_ref[...], axis=1, keepdims=True)
    first = lax.broadcasted_iota(jnp.int32, products.shape, 0) // SSM_HEAD == 0
    head = lane_index(decay_grad.shape)
    for half in range(2):
        total = jnp.sum(jnp.where(first == (half == 0), products, 0.0), axis=0, keepdims=True)
        decay_grad[...] = jnp.where(head == 2 * step + half, total, decay_grad[...])
    carried = low(carried)
    reached = dot_nt(write_ref[...], carried)
    value_grad[...] = before_ref[...] + weight * reached
    write_grad[...] += dot_nn(low(weight * wide), carried)
    product = wide * reached
    for half in range(2):
        inside = (lane_index(shape) // HEAD) == half
        set_column(
            end_grad,
            2 * step + half,
            jnp.sum(jnp.where(inside, product, 0.0), axis=1, keepdims=True),
        )


def ssd_state_back(filtered, end_weights, value_before, write_before, start, messages):
    length = filtered.shape[0]
    pairs = SSM_HEADS // 2
    return call(
        ssd_state_back_kernel,
        pairs,
        [
            pair_spec(length),
            pl.BlockSpec((length, STATE), lambda i: (0, pairs)),
            whole_spec((length, SSM_HEADS)),
            pair_spec(length),
            whole_spec((length, STATE)),
            state_spec(),
        ]
        + message_specs(len(messages)),
        [
            pair_spec(length),
            whole_spec((length, SSM_HEADS)),
            whole_spec((length, STATE)),
            whole_spec((1, SSM_HEADS)),
        ],
        [
            float_out(*value_before.shape),
            float_out(length, SSM_HEADS),
            float_out(length, STATE),
            float_out(1, SSM_HEADS),
        ],
        (),
        4 * SSM_HEADS * length * STATE * SSM_HEAD,
    )(
        filtered, filtered, end_weights, value_before, write_before, start,
        *[m for message in messages for m in (message, message)],
    )


def turned(x, cosine, sine):
    quarter = HEAD // 2
    after = pltpu.roll(x, x.shape[1] - quarter, 1)
    earlier = pltpu.roll(x, quarter, 1)
    other = jnp.where(lane_index(x.shape) % HEAD < quarter, after, earlier)
    return x * cosine + other * sine


def group_rows(both, group):
    wide = both.astype(jnp.float32)
    kept = jnp.where(lane_index(wide.shape) // HEAD == group, wide, 0.0)
    return low(kept + pltpu.roll(kept, HEAD, 1))


def attention_mask(bias, pos_col, pos_row, seg_col, seg_row):
    allowed = (
        (pos_row[...] <= pos_col[...]) & (pos_row[...] >= 0) & (seg_row[...] == seg_col[...])
    )
    bias[...] = jnp.where(allowed, 0.0, -1e30)


def attention_kernel(
    query_ref, keys_ref, values_ref, cos_ref, sin_ref, pos_col, pos_row, seg_col, seg_row, out_ref,
    lse_ref, bias,
):
    step = pl.program_id(0)

    @pl.when(step == 0)
    def _():
        attention_mask(bias, pos_col, pos_row, seg_col, seg_row)
        lse_ref[...] = jnp.zeros_like(lse_ref)

    group = step * 2 // (HEADS // KV_HEADS)
    keys = group_rows(keys_ref[...], group)
    values = group_rows(values_ref[...], group)
    query = low(turned(query_ref[...], cos_ref[...], sin_ref[...])).astype(jnp.float32)
    outs = []
    for half in range(2):
        inside = (lane_index(query.shape) // HEAD) == half
        part = low(jnp.where(inside, query, 0.0))
        scores = dot_nt(part, keys) * score_scale + bias[...]
        top = jnp.max(scores, axis=1, keepdims=True)
        lse = top + jnp.log(jnp.sum(jnp.exp(scores - top), axis=1, keepdims=True))
        outs.append(dot_nn(low(jnp.exp(scores - lse)), values))
        set_column(lse_ref, 2 * step + half, lse)
    out_ref[...] = low(by_head(outs[0], outs[1], query.shape))


def attention_specs(length, keys):
    return [
        whole_spec((length, PAIR)),
        whole_spec((length, PAIR)),
        whole_spec((length, 1)),
        whole_spec((1, keys)),
        whole_spec((length, 1)),
        whole_spec((1, keys)),
    ]


def attention(queries, all_keys, places):
    length = queries.shape[0]
    keys = all_keys.shape[0]
    return call(
        attention_kernel,
        HEADS // 2,
        [
            pair_spec(length),
            pl.BlockSpec((keys, PAIR), lambda i: (0, 0)),
            pl.BlockSpec((keys, PAIR), lambda i: (0, 1)),
        ]
        + attention_specs(length, keys),
        [pair_spec(length), whole_spec((length, HEADS))],
        [jax.ShapeDtypeStruct(queries.shape, jnp.bfloat16), float_out(length, HEADS)],
        [pltpu.VMEM((length, keys), jnp.float32)],
        4 * HEADS * length * keys * PAIR,
    )(queries, all_keys, all_keys, *places)


def attention_back_kernel(
    query_ref, grad_ref, lse_ref, keys_ref, values_ref, cos_ref, sin_ref, pos_col, pos_row,
    seg_col, seg_row, query_grad, key_grad, value_grad, bias,
):
    step = pl.program_id(0)

    @pl.when(step == 0)
    def _():
        attention_mask(bias, pos_col, pos_row, seg_col, seg_row)
        key_grad[...] = jnp.zeros_like(key_grad)
        value_grad[...] = jnp.zeros_like(value_grad)

    group = step * 2 // (HEADS // KV_HEADS)
    keys = group_rows(keys_ref[...], group)
    values = group_rows(values_ref[...], group)
    query = low(turned(query_ref[...], cos_ref[...], sin_ref[...])).astype(jnp.float32)
    grad = low(grad_ref[...]).astype(jnp.float32)
    into_query = []
    into_keys = jnp.zeros(key_grad.shape, jnp.float32)
    into_values = jnp.zeros(key_grad.shape, jnp.float32)
    for half in range(2):
        inside = (lane_index(query.shape) // HEAD) == half
        part = low(jnp.where(inside, query, 0.0))
        grad_part = low(jnp.where(inside, grad, 0.0))
        scores = dot_nt(part, keys) * score_scale + bias[...]
        probs = jnp.exp(scores - column_of(lse_ref[...], 2 * step + half))
        grad_probs = dot_nt(grad_part, values)
        delta = jnp.sum(probs * grad_probs, axis=1, keepdims=True)
        grad_scores = low(probs * (grad_probs - delta))
        into_query.append(dot_nn(grad_scores, keys))
        into_keys = into_keys + dot_tn(grad_scores, part)
        into_values = into_values + dot_tn(low(probs), grad_part)
    wide = by_head(into_query[0], into_query[1], query.shape) * score_scale
    query_grad[...] = low(turned(wide, cos_ref[...], -sin_ref[...]))
    mine = lane_index(into_keys.shape) // HEAD == group
    into_keys = into_keys + pltpu.roll(into_keys, HEAD, 1)
    into_values = into_values + pltpu.roll(into_values, HEAD, 1)
    key_grad[...] += jnp.where(mine, into_keys * score_scale, 0.0)
    value_grad[...] += jnp.where(mine, into_values, 0.0)


def attention_back(queries, grads, lse, all_keys, places):
    length = queries.shape[0]
    keys = all_keys.shape[0]
    return call(
        attention_back_kernel,
        HEADS // 2,
        [
            pair_spec(length),
            pair_spec(length),
            whole_spec((length, HEADS)),
            pl.BlockSpec((keys, PAIR), lambda i: (0, 0)),
            pl.BlockSpec((keys, PAIR), lambda i: (0, 1)),
        ]
        + attention_specs(length, keys),
        [pair_spec(length), whole_spec((keys, PAIR)), whole_spec((keys, PAIR))],
        [
            jax.ShapeDtypeStruct(queries.shape, jnp.bfloat16),
            float_out(keys, PAIR),
            float_out(keys, PAIR),
        ],
        [pltpu.VMEM((length, keys), jnp.float32)],
        10 * HEADS * length * keys * PAIR,
    )(queries, grads, lse, all_keys, all_keys, *places)


def turn_pair(x, cosine, sine):
    quarter = HEAD // 2
    pieces = [x[:, k * quarter : (k + 1) * quarter] for k in range(x.shape[1] // quarter)]
    other = jnp.concatenate([pieces[k ^ 1] for k in range(len(pieces))], axis=1)
    return x * cosine + other * sine


def gated_norm(ssm_out, gate_mix, mixer_gain):
    return rms_scale(ssm_out * jax.nn.silu(gate_mix), mixer_gain)


def swiglu(gate_val, up_val):
    return jax.nn.silu(gate_val) * up_val


def shift_along(x, line, by):
    axis, stride, size = line
    pairs = []
    for index in range(lax.axis_size(axis)):
        place = (index // stride) % size
        pairs.append((index, index + ((place + by) % size - place) * stride))
    return lax.ppermute(x, axis, pairs)


def mesh_lines():
    replicas, pieces = (lax.axis_size("dp"), lax.axis_size("seq"))
    across = 1
    while across * across * 2 <= pieces:
        across *= 2
    lines = {
        "core": ("dp", 1, 2),
        "z": ("dp", 2, replicas // 2),
        "x": ("seq", 1, across),
        "y": ("seq", across, pieces // across),
    }
    return lines


def place_on(line):
    axis, stride, size = line
    return (lax.axis_index(axis) // stride) % size


def tie(*groups):
    return lax.optimization_barrier(groups)


def shift_piece(x, lines, down, right):
    rows, across = (lines["y"][2], lines["x"][2])
    pairs = []
    for index in range(rows * across):
        y, x_place = (index // across, index % across)
        pairs.append((index, (y + down) % rows * across + (x_place + right) % across))
    return lax.ppermute(x, "seq", pairs)


def offsets(lines):
    return [(y, x) for y in range(lines["y"][2]) for x in range(lines["x"][2])]


def level_groups(line):
    axis, stride, size = line
    return [[c + stride * k for k in range(size)] for c in range(stride)]


def gather_levels(packed, lines):
    return lax.all_gather(packed, "dp")


def spread(both, widths, lines):
    levels, rows, width = (lines["z"][2], both.shape[1], both.shape[2])
    mine = lax.dynamic_index_in_dim(
        both.reshape(levels, 2, rows, width), place_on(lines["core"]), 1, False
    ).reshape(levels * rows, width)
    blocks = [shift_piece(mine, lines, -y, -x) if y or x else mine for y, x in offsets(lines)]
    found = []
    start = 0
    for size in widths:
        own = jnp.concatenate([block[:, start : start + size] for block in blocks], axis=0)
        found.append((own, shift_along(own, lines["core"], 1)))
        start += size
    return found


def relative_index(row_counts, lines):
    levels, rows_out, across = (lines["z"][2], lines["y"][2], lines["x"][2])
    total = sum(row_counts)
    places = []
    start = 0
    for rows in row_counts:
        column = jnp.arange(levels * 2 * rows_out * across * rows)
        row = column % rows
        device = column // rows
        x = (device % across - place_on(lines["x"])) % across
        y = (device // across % rows_out - place_on(lines["y"])) % rows_out
        core = (device // (across * rows_out) - place_on(lines["core"])) % 2
        level = device // (across * rows_out * 2)
        block = ((core * rows_out + y) * across + x) * levels + level
        places.append(block * total + start + row)
        start += rows
    return jnp.concatenate(places) if len(places) > 1 else places[0]


def permutation(row_counts, lines):
    index = relative_index(row_counts, lines)
    return (index[:, None] == jnp.arange(index.shape[0])[None, :]).astype(jnp.bfloat16)


def to_relative(low, order):
    return matmul(low, order).astype(jnp.bfloat16)


def from_relative(wide, order):
    high = lax.reduce_precision(wide, 8, 7)
    rest = wide - high
    return back_product(high.astype(jnp.bfloat16), order) + back_product(
        rest.astype(jnp.bfloat16), order
    )


def product_rel(low_rel, weights):
    own, other = weights
    half = own.shape[0]
    return matmul(low_rel[:, :half], own) + matmul(low_rel[:, half:], other)


def back_rel(grad, weights):
    own, other = weights
    return jnp.concatenate([back_product(grad, own), back_product(grad, other)], axis=1)


def owed(left, grad, lines, last_by_level):
    levels = lines["z"][2]
    half = left.shape[1] // 2
    block = half // len(offsets(lines))
    theirs = rows_product(left[:, half:], grad).astype(jnp.bfloat16)
    received = yield shift_along(theirs, lines["core"], 1)
    pieces = []
    for k, (y, x) in enumerate(offsets(lines)):
        rows = slice(k * block, (k + 1) * block)
        piece = rows_product(left[:, rows], grad) + received[rows].astype(jnp.float32)
        if k:
            piece = shift_piece(piece.astype(jnp.bfloat16), lines, y, x)
        pieces.append(piece)
    pieces = yield pieces
    if last_by_level:
        rows = block // levels
        parts = []
        for k in range(levels):
            start = (place_on(lines["z"]) + k) % levels * rows
            total = sum(
                lax.dynamic_slice_in_dim(piece, start, rows).astype(jnp.float32)
                for piece in pieces
            )
            if k:
                total = shift_along(total.astype(jnp.bfloat16), lines["z"], k)
            parts.append(total)
        parts = yield parts
        yield sum(part.astype(jnp.float32) for part in parts)
    else:
        total = sum(piece.astype(jnp.float32) for piece in pieces).astype(jnp.bfloat16)
        yield lax.psum_scatter(
            total,
            "dp",
            scatter_dimension=0,
            axis_index_groups=level_groups(lines["z"]),
            tiled=True,
        ).astype(jnp.float32)


def sum_everywhere(x):
    for axis in ("dp", "seq"):
        size = lax.axis_size(axis)
        step = 1
        while step < size:
            x = x + lax.ppermute(x, axis, [(i, i ^ step) for i in range(size)])
            step *= 2
    return x


def from_earlier(x, by):
    return passed_along(x, "seq", by)


def body(
    inputs,
    segments,
    cotangent,
    mixer_gate,
    mixer_input,
    mixer_step,
    mixer_output,
    query_weight,
    key_weight,
    value_weight,
    output_weight,
    gate_weight,
    up_weight,
    down_weight,
    input_gain,
    second_gain,
    mixer_gain,
    filter_taps,
    filter_bias,
    decay_log,
    step_bias,
    skip_gain,
):
    piece_index = lax.axis_index("seq")
    local_len = inputs.shape[1]
    seq_len = segments.shape[1]
    first_token = piece_index * local_len
    all_segs = segments[0]
    own_segments = lax.dynamic_slice_in_dim(all_segs, first_token, local_len)
    rim_start = jnp.maximum(first_token - (CONV - 1), 0)
    rim_segments = jnp.where(
        piece_index > 0, lax.dynamic_slice_in_dim(all_segs, rim_start, CONV - 1), -1
    )
    seg_before = rim_segments[CONV - 2]
    positions = first_token + jnp.arange(local_len)
    ext_segments = jnp.concatenate([rim_segments, own_segments])
    pieces = lax.axis_size("seq")
    lines = mesh_lines()
    inner = SSM_HEADS * SSM_HEAD
    query_width = HEADS * HEAD
    key_width = KV_HEADS * HEAD
    conv_width = mixer_input.shape[1]
    step_pad = jnp.pad(mixer_step, ((0, 0), (0, 128 - SSM_HEADS)))
    packed_input = jnp.concatenate([mixer_input, step_pad], axis=1)
    packed_gate = jnp.concatenate([mixer_gate, query_weight, key_weight, value_weight], axis=1)
    packed_branch = jnp.concatenate(
        [jnp.concatenate([mixer_output, output_weight], axis=0), down_weight], axis=1
    )
    packed_up = jnp.concatenate([gate_weight, up_weight], axis=1)
    both_input = gather_levels(packed_input, lines)
    both_input, packed_gate = tie(both_input, packed_gate)
    both_gate = gather_levels(packed_gate, lines)
    both_gate, packed_branch = tie(both_gate, packed_branch)
    both_branch = gather_levels(packed_branch, lines)
    both_branch, packed_up = tie(both_branch, packed_up)
    both_up = gather_levels(packed_up, lines)
    (w_input,) = spread(both_input, (packed_input.shape[1],), lines)
    (w_mix,) = spread(both_gate, (packed_gate.shape[1],), lines)
    w_branch, w_down = spread(both_branch, (output_weight.shape[1],) * 2, lines)
    (w_up,) = spread(both_up, (packed_up.shape[1],), lines)
    order_tokens = permutation((mixer_gate.shape[0],), lines)
    order_branch = permutation((mixer_output.shape[0], output_weight.shape[0]), lines)
    order_hidden = permutation((down_weight.shape[0],), lines)
    tokens = inputs[0].astype(jnp.float32)
    normed, norm_back = jax.vjp(rms_scale, tokens, input_gain)
    normed_low = normed.astype(jnp.bfloat16)
    normed_rel = to_relative(normed_low, order_tokens)
    input_out = product_rel(normed_rel, w_input)
    mixed_raw = input_out[:, :conv_width].astype(jnp.bfloat16)
    step_raw = input_out[:, conv_width : conv_width + SSM_HEADS]
    mix_out = product_rel(normed_rel, w_mix)
    gate_mix = mix_out[:, :inner]
    queries = mix_out[:, inner : inner + query_width]
    keys_raw = mix_out[:, inner + query_width : inner + query_width + key_width]
    values_low = mix_out[:, inner + query_width + key_width :].astype(jnp.bfloat16)
    rim_rows = passed_along(mixed_raw[local_len - CONV + 1 :], "seq", 1)
    extended = jnp.concatenate([rim_rows, mixed_raw], axis=0).astype(jnp.float32)

    def filter_fn(ext_rows, taps, bias):
        return conv_apply(ext_rows, ext_segments, taps, bias)

    filtered, filter_back = jax.vjp(filter_fn, extended, filter_taps, filter_bias)
    filtered_low = filtered.astype(jnp.bfloat16)
    stride_in = step_raw + step_bias
    stride = jax.nn.softplus(stride_in)
    rate = -jnp.exp(decay_log)
    running = running_sum(stride * rate)
    run_rows = running.T
    stride_rows = stride.T
    final_log = running[-1]
    keep_end = (own_segments == own_segments[-1]).astype(jnp.float32)[:, None]
    end_decay = jnp.exp(final_log[None, :] - running) * keep_end
    end_weights = end_decay * stride
    carry_decay = jnp.exp(final_log) * (own_segments[-1] == seg_before).astype(jnp.float32)
    entering = (own_segments == seg_before).astype(jnp.float32)[:, None] * jnp.exp(running)
    seg_col = own_segments[:, None]
    seg_row = own_segments[None, :]
    local_out, carry_state = ssd_local(
        filtered_low, running, run_rows, stride_rows, end_weights, skip_gain, seg_col, seg_row
    )
    packed_state = packed_message(carry_state, carry_decay)
    earlier_states = [from_earlier(packed_state, d) for d in range(1, pieces)]
    ssm_out, start_rows = ssd_entering(local_out, filtered_low, entering, earlier_states)
    gated_out, gated_back = jax.vjp(gated_norm, ssm_out, gate_mix, mixer_gain)
    gated_low = gated_out.astype(jnp.bfloat16)
    cosine, sine = rotation_tables(positions)
    key_rot = turn_pair(keys_raw, cosine, sine).astype(jnp.bfloat16)
    own_keys = jnp.concatenate([key_rot, values_low], axis=1)
    all_keys = jnp.concatenate(
        [own_keys] + [from_earlier(own_keys, d) for d in range(1, pieces)], axis=0
    )
    key_positions = jnp.concatenate([positions - d * local_len for d in range(pieces)])
    key_segments = jnp.concatenate(
        [
            lax.dynamic_slice_in_dim(all_segs, jnp.maximum(first_token - d * local_len, 0), local_len)
            for d in range(pieces)
        ]
    )
    places = (
        cosine,
        sine,
        positions[:, None],
        key_positions[None, :],
        seg_col,
        key_segments[None, :],
    )
    attended_low, lse = attention(queries, all_keys, places)
    branch_rel = to_relative(jnp.concatenate([gated_low, attended_low], axis=1), order_branch)
    middle = tokens + product_rel(branch_rel, w_branch)
    second, second_back = jax.vjp(rms_scale, middle, second_gain)
    second_low = second.astype(jnp.bfloat16)
    second_rel = to_relative(second_low, order_tokens)
    hidden = product_rel(second_rel, w_up)
    gate_val = hidden[:, : gate_weight.shape[1]]
    up_val = hidden[:, gate_weight.shape[1] :]
    activated, act_back = jax.vjp(swiglu, gate_val, up_val)
    activated_low = activated.astype(jnp.bfloat16)
    activated_rel = to_relative(activated_low, order_hidden)
    result = (middle + product_rel(activated_rel, w_down)).astype(jnp.bfloat16)
    upstream = cotangent[0].astype(jnp.float32)
    upstream_low = upstream.astype(jnp.bfloat16)
    sum_down = owed(activated_rel, upstream_low, lines, False)
    down_wait = next(sum_down)
    grad_act = from_relative(back_rel(upstream_low, w_down), order_hidden)
    grad_gate_val, grad_up_val = act_back(grad_act)
    up_low = jnp.concatenate([grad_gate_val, grad_up_val], axis=1).astype(jnp.bfloat16)
    up_low, down_wait = tie(up_low, down_wait)
    down_wait = sum_down.send(down_wait)
    sum_up = owed(second_rel, up_low, lines, False)
    up_wait = next(sum_up)
    grad_second = from_relative(back_rel(up_low, w_up), order_tokens)
    grad_middle, grad_second_gain = second_back(grad_second)
    grad_middle = grad_middle + upstream
    grad_middle, up_wait = tie(grad_middle, up_wait)
    up_wait = sum_up.send(up_wait)
    branch_low = grad_middle.astype(jnp.bfloat16)
    sum_branch = owed(branch_rel, branch_low, lines, False)
    branch_wait = next(sum_branch)
    grad_branch = from_relative(back_rel(branch_low, w_branch), order_branch)
    grad_gated = grad_branch[:, :inner]
    grad_attn = grad_branch[:, inner:]
    grad_ssm, grad_zgate, grad_mixer_gain = gated_back(grad_gated)
    zgate_low = grad_zgate.astype(jnp.bfloat16)
    grad_ssm, down_wait = tie(grad_ssm, down_wait)
    grad_down = sum_down.send(down_wait)
    value_grad, grad_incoming, row_sum, col_sum, write_grad, read_grad = ssd_back(
        grad_ssm, filtered_low, running, run_rows, stride_rows, entering, skip_gain, start_rows,
        seg_col, seg_row,
    )
    packed_grad = packed_message(grad_incoming, carry_decay)
    later_grads = [from_earlier(packed_grad, -d) for d in range(1, pieces)]
    grad_attn, branch_wait, value_grad = tie(grad_attn, branch_wait, value_grad)
    branch_wait = sum_branch.send(branch_wait)
    query_low, key_part, value_part = attention_back(queries, grad_attn, lse, all_keys, places)
    keys_part = jnp.concatenate([key_part, value_part], axis=1)
    keys_total = keys_part[:local_len]
    for d in range(1, pieces):
        sent = keys_part[d * local_len : (d + 1) * local_len].astype(jnp.bfloat16)
        keys_total = keys_total + from_earlier(sent, -d).astype(jnp.float32)
    key_total = keys_total[:, :key_width]
    value_total = keys_total[:, key_width:]
    key_low = turn_pair(key_total, cosine, -sine).astype(jnp.bfloat16)
    value_low = value_total.astype(jnp.bfloat16)
    mix_low = jnp.concatenate([zgate_low, query_low, key_low, value_low], axis=1)
    sum_mix = owed(normed_rel, mix_low, lines, False)
    mix_wait = next(sum_mix)
    grad_skip = jnp.sum(
        jnp.sum(grad_ssm * filtered_low[:, :inner].astype(jnp.float32), axis=0).reshape(
            SSM_HEADS, SSM_HEAD
        ),
        axis=1,
    )
    value_grad, end_grad, write_grad, decay_grad = ssd_state_back(
        filtered_low, end_weights, value_grad, write_grad, start_rows, later_grads
    )
    grad_decay_total = decay_grad[0]
    col_part = col_sum.T
    ended = end_grad * end_weights
    grad_running = row_sum - stride * col_part - ended
    grad_final = jnp.sum(ended, axis=0) + grad_decay_total * carry_decay
    last_row = (jnp.arange(local_len) == local_len - 1).astype(jnp.float32)[:, None]
    grad_logs = later_sum(grad_running + last_row * grad_final[None, :])
    grad_stride = col_part + end_grad * end_decay + grad_logs * rate
    grad_step = grad_stride * jax.nn.sigmoid(stride_in)
    grad_decay_log = rate * jnp.sum(grad_logs * stride, axis=0)
    grad_step_bias = jnp.sum(grad_step, axis=0)
    xc_grad = jnp.concatenate([value_grad, write_grad, read_grad], axis=1)
    xc_grad, up_wait, mix_wait = tie(xc_grad, up_wait, mix_wait)
    grad_ups = sum_up.send(up_wait)
    mix_wait = sum_mix.send(mix_wait)
    grad_ext, grad_taps, grad_fbias = filter_back(xc_grad)
    returned = passed_along(grad_ext[: CONV - 1], "seq", -1)
    grad_mixed = grad_ext[CONV - 1 :] + jnp.pad(returned, ((local_len - CONV + 1, 0), (0, 0)))
    step_pad_low = jnp.pad(grad_step.astype(jnp.bfloat16), ((0, 0), (0, 128 - SSM_HEADS)))
    input_low = jnp.concatenate([grad_mixed.astype(jnp.bfloat16), step_pad_low], axis=1)
    input_low, branch_wait = tie(input_low, branch_wait)
    grad_branch_rows = sum_branch.send(branch_wait)
    sum_input = owed(normed_rel, input_low, lines, True)
    input_wait = next(sum_input)
    input_wait = sum_input.send(input_wait)
    mix_wait, input_wait = tie(mix_wait, input_wait)
    grad_mix = sum_mix.send(mix_wait)
    grad_normed = from_relative(
        back_rel(input_low, w_input) + back_rel(mix_low, w_mix), order_tokens
    )
    input_wait = sum_input.send(input_wait)
    grad_inputs = sum_input.send(input_wait)
    mixer_rows = mixer_output.shape[0]
    mixer_grads = (
        grad_mix[:, :inner],
        grad_inputs[:, :conv_width],
        grad_inputs[:, conv_width : conv_width + SSM_HEADS],
        grad_branch_rows[:mixer_rows],
        grad_mix[:, inner : inner + query_width],
        grad_mix[:, inner + query_width : inner + query_width + key_width],
        grad_mix[:, inner + query_width + key_width :],
        grad_branch_rows[mixer_rows:],
    )
    ffn_grads = (grad_ups[:, : gate_weight.shape[1]], grad_ups[:, gate_weight.shape[1] :], grad_down)
    grad_tokens, grad_input_gain = norm_back(grad_normed)
    grad_tokens = grad_tokens + grad_middle
    small = (
        grad_input_gain,
        grad_second_gain,
        grad_mixer_gain,
        grad_taps,
        grad_fbias,
        grad_decay_log,
        grad_step_bias,
        grad_skip,
    )
    sizes = [part.size for part in small]
    length = sum(sizes)
    flat = jnp.pad(
        jnp.concatenate([part.reshape(-1) for part in small]), (0, -length % 1024)
    ).reshape(-1, 128)
    flat = sum_everywhere(flat).reshape(-1)
    small_sums = []
    start = 0
    for part in small:
        small_sums.append(flat[start : start + part.size].reshape(part.shape))
        start += part.size
    return (
        result[None],
        grad_tokens[None],
        mixer_grads[0],
        mixer_grads[1],
        mixer_grads[2],
        mixer_grads[3],
        mixer_grads[4],
        mixer_grads[5],
        mixer_grads[6],
        mixer_grads[7],
        ffn_grads[0],
        ffn_grads[1],
        ffn_grads[2],
        small_sums[0],
        small_sums[1],
        small_sums[2],
        small_sums[3],
        small_sums[4],
        small_sums[5],
        small_sums[6],
        small_sums[7],
    )


def solution(mesh):
    placed = (
        P("dp", "seq", None),
        P("dp", None),
        P("dp", "seq", None),
        P(("dp", "seq"), None),
        P(("dp", "seq"), None),
        P(("dp", "seq"), None),
        P(("dp", "seq"), None),
        P(("dp", "seq"), None),
        P(("dp", "seq"), None),
        P(("dp", "seq"), None),
        P(("dp", "seq"), None),
        P(("dp", "seq"), None),
        P(("dp", "seq"), None),
        P(("dp", "seq"), None),
        P(),
        P(),
        P(),
        P(),
        P(),
        P(),
        P(),
        P(),
    )
    return jax.shard_map(
        body,
        mesh=mesh,
        in_specs=placed,
        out_specs=(
            P("dp", "seq", None),
            P("dp", "seq", None),
            P(("dp", "seq"), None),
            P(("dp", "seq"), None),
            P(("dp", "seq"), None),
            P(("dp", "seq"), None),
            P(("dp", "seq"), None),
            P(("dp", "seq"), None),
            P(("dp", "seq"), None),
            P(("dp", "seq"), None),
            P(("dp", "seq"), None),
            P(("dp", "seq"), None),
            P(("dp", "seq"), None),
            P(),
            P(),
            P(),
            P(),
            P(),
            P(),
            P(),
            P(),
        ),
        check_vma=False,
    )
```

time: 641 us -> 551 us (0.86)
  local copies, waits for them, and re-layouts: 94.2 us -> 43.2 us
  Pallas kernels: 0 us -> 45.4 us
  matrix products: 149 us -> 108 us
  starting transfers between devices: 118 us -> 81.2 us
  other arithmetic: 73 us -> 50.7 us
  blocking collectives: 0 us -> 17.9 us
  waiting for transfers between devices: 191 us -> 177 us
  between operations: 5.27 us -> 18.8 us
    ppermute x60 -> x13, waiting for transfers between devices: 138 us -> 5.03 us  [shift_along(): return lax.ppermute(x, axis, pairs)]
    ppermute x0 -> x27, waiting for transfers between devices: none -> 94.5 us  [shift_piece(): return lax.ppermute(x, 'seq', pairs)]
    ppermute x60 -> x13, starting transfers between devices: 73.1 us -> 5.73 us  [shift_along(): return lax.ppermute(x, axis, pairs)]
    pallas_call x0 -> x6, Pallas kernels: none -> 45.4 us  [the longest x1 11.3 us: ssd_back(): call(ssd_back_kernel, pairs, [pair_spec(length), pair_spec(length), pl.Bl...]
    dot_general x26 -> x1, matrix products: 46.8 us -> 2.1 us  [later_sum(): return jnp.dot(later, x, precision=lax.Precision.HIGHEST)]
    ppermute x0 -> x27, starting transfers between devices: none -> 40.9 us  [shift_piece(): return lax.ppermute(x, 'seq', pairs)]
    all_gather x0 -> x3, waiting for transfers between devices: none -> 26.6 us  [gather_levels(): return lax.all_gather(packed, 'dp')]
    ppermute x17 -> x14, waiting for transfers between devices: 48.7 us -> 24.2 us  [passed_along(): return lax.ppermute(x, axis, pairs)]
  transfers between devices with their start and end apart: 82 -> 66, of which waited for: 31 -> 27; matrix products, arithmetic and copies ran while one was open for 35% -> 32% of each run, Pallas kernels for 0% -> 8%
where the time goes in v2:
time: 551 us; the launch traced here: 542 us
  waiting for transfers between devices  177 us (32%)
  matrix products  108 us (20%)
  starting transfers between devices  81.2 us (15%)
  other arithmetic  50.7 us (9%)
  Pallas kernels  45.4 us (8%)
  local copies, waits for them, and re-layouts  43.2 us (8%)
  between operations  18.8 us (3%)
  blocking collectives  17.9 us (3%)
    ppermute x27, waiting for transfers between devices, shift_piece(): return lax.ppermute(x, 'seq', pairs)  94.5 us
    ppermute x27, starting transfers between devices, shift_piece(): return lax.ppermute(x, 'seq', pairs)  40.9 us
    dot_general x25, matrix products, rows_product(): lax.dot_general(left, right, (((0,), (0,)), ((), ())), preferred_element_...  40.5 us
    dot_general x18, matrix products, back_product(): lax.dot_general(left, right, (((1,), (1,)), ((), ())), preferred_element_...  38.1 us
    ppermute x14, starting transfers between devices, passed_along(): return lax.ppermute(x, axis, pairs)  32.2 us
    dot_general x14, matrix products, matmul(): return jnp.dot(left, right, preferred_element_type=jnp.float32)  27.3 us
    all_gather x3, waiting for transfers between devices, gather_levels(): return lax.all_gather(packed, 'dp')  26.6 us
    ppermute x14, waiting for transfers between devices, passed_along(): return lax.ppermute(x, axis, pairs)  24.2 us
  transfers between devices with their start and end apart: 66, of which 27 were waited for; matrix products, arithmetic and copies ran while one was open for 32% of the time, Pallas kernels for 8%

profile of v2, /device:TPU:0, one launch (start us, length us, event | category | flops | bytes accessed | tf_op | source)
XLA Modules:
  0.0 542.0 jit_solution(16496917573766680045)
XLA Ops:
  9.0 17.9 %all-gather = bf16[256,1920]{1,0:T(8,128)(2,1)S(1)} all-gather(bf16[32,1920]{1,0:T(8,128)(2,1)S(1)} %fusion.158), channel_id=2, replica_groups=mesh['dp'=8,'seq'=4] {'dp'}, dimensions={0}, use_global_device_ids=true | all-gather | bytes 1105920 | tf_op jit(solution)/shard_map/all_gather | solution.py:671
  37.3 15.7 %all-gather.8.cloned.1.call-done = bf16[256,2304]{1,0:T(8,128)(2,1)} async-done(((bf16[32,2304]{1,0:T(8,128)(2,1)}), bf16[256,2304]{1,0:T(8,128)(2,1)}) %all-gather.8.cloned.1.call-update) | async-done | bytes 1179664 | tf_op jit(solution)/shard_map/all_gather | solution.py:671
  72.9 10.9 %all-gather.10.cloned.1.call-done = bf16[512,2048]{1,0:T(8,128)(2,1)} async-done(((bf16[64,2048]{1,0:T(8,128)(2,1)}), bf16[512,2048]{1,0:T(8,128)(2,1)}) %all-gather.10.cloned.1.call-update) | async-done | bytes 2097168 | tf_op jit(solution)/shard_map/all_gather | solution.py:671
  84.0 7.7 %collective-permute-done.9 = bf16[128,2304]{1,0:T(8,128)(2,1)} collective-permute-done((bf16[128,2304]{1,0:T(8,128)(2,1)}, bf16[128,2304]{1,0:T(8,128)(2,1)}, u32[]{:S(2)}, u32[]{:S(2)}) %collective-permute-start.9) | collective-permute-done | bytes 589856 | tf_op jit(solution)/shard_map/ppermute | solution.py:658
  100.5 5.6 %shard_map.373 = (f32[256,1536]{1,0:T(8,128)S(1)}, f32[1536,128]{1,0:T(8,128)S(1)}) custom-call(bf16[256,1792]{1,0:T(8,128)(2,1)S(1)} %get-tuple-element.237.value_ref.write_ref.read_ref, bf16[256,1792]{1,0:T(8,128)(2,1)S(1)} %get-tuple-element.237.value_ref.write_ref.read_ref, bf16[256,1792]{1,0:T(8,128)(2,1)S(1)} %get-tuple-element.237.value_ref.write_ref.read_ref, ...), custom_call_target="tpu_custom_call" | custom-call | flops 402653184 | bytes 4000000 | tf_op jit(solution)/shard_map/pallas_call | solution.py:199
  119.2 9.3 %collective-permute-done.6.refs_2_.refs_3_ = bf16[1568,128]{1,0:T(8,128)(2,1)S(1)} collective-permute-done((bf16[1568,128]{1,0:T(8,128)(2,1)S(1)}, bf16[1568,128]{1,0:T(8,128)(2,1)S(1)}, u32[]{:S(2)}, u32[]{:S(2)}) %collective-permute-start.6) | collective-permute-done | bytes 401440 | tf_op jit(solution)/shard_map/ppermute | solution.py:27
  140.3 3.8 collective-permute-start.17
  152.5 16.0 %collective-permute-done.17 = bf16[256,2048]{1,0:T(8,128)(2,1)} collective-permute-done((bf16[256,2048]{1,0:T(8,128)(2,1)}, bf16[256,2048]{1,0:T(8,128)(2,1)}, u32[]{:S(2)}, u32[]{:S(2)}) %collective-permute-start.17) | collective-permute-done | bytes 1048608 | tf_op jit(solution)/shard_map/ppermute | solution.py:658
  170.8 20.0 %collective-permute-done.21 = bf16[128,4096]{1,0:T(8,128)(2,1)S(1)} collective-permute-done((bf16[128,4096]{1,0:T(8,128)(2,1)S(1)}, bf16[128,4096]{1,0:T(8,128)(2,1)S(1)}, u32[]{:S(2)}, u32[]{:S(2)}) %collective-permute-start.21) | collective-permute-done | bytes 1048608 | tf_op jit(solution)/shard_map/ppermute | solution.py:658
  190.8 4.9 collective-permute-start.14
  195.7 16.7 %collective-permute-done.20 = bf16[128,4096]{1,0:T(8,128)(2,1)S(1)} collective-permute-done((bf16[128,4096]{1,0:T(8,128)(2,1)S(1)}, bf16[128,4096]{1,0:T(8,128)(2,1)S(1)}, u32[]{:S(2)}, u32[]{:S(2)}) %collective-permute-start.20) | collective-permute-done | bytes 1048608 | tf_op jit(solution)/shard_map/ppermute | solution.py:658
  212.4 3.6 collective-permute-start.13
  220.0 14.8 %collective-permute-done.16 = bf16[256,2048]{1,0:T(8,128)(2,1)S(1)} collective-permute-done((bf16[256,2048]{1,0:T(8,128)(2,1)}, bf16[256,2048]{1,0:T(8,128)(2,1)S(1)}, u32[]{:S(2)}, u32[]{:S(2)}) %collective-permute-start.16) | collective-permute-done | bytes 1048608 | tf_op jit(solution)/shard_map/ppermute | solution.py:658
  239.8 7.7 %shard_map.375 = (bf16[256,512]{1,0:T(8,128)(2,1)S(1)}, f32[256,8]{1,0:T(8,128)S(1)}) custom-call(f32[256,512]{1,0:T(8,128)S(1)} %slice.505.query_ref, bf16[1024,256]{1,0:T(8,128)(2,1)S(1)} %pad_maximum_fusion.11.keys_ref.values_ref, bf16[1024,256]{1,0:T(8,128)(2,1)S(1)} %pad_maximum_fusion.11.keys_ref.values_ref, ...), custom_call_target="tpu_custom_call" | custom-call | flops 1073741824 | bytes 4000000 | tf_op jit(solution)/shard_map/pallas_call | solution.py:523
  261.1 4.0 fusion.24
  267.9 3.5 fusion
  271.4 4.4 fusion.32
  303.3 3.5 fusion.3
  306.9 3.7 fusion.21
  314.2 11.3 %shard_map.376 = (f32[256,1536]{1,0:T(8,128)S(1)}, f32[1536,128]{1,0:T(8,128)S(1)}, f32[256,24]{1,0:T(8,128)S(1)}, f32[24,256]{1,0:T(8,128)S(1)}, f32[256,128]{1,0:T(8,128)S(1)}, /*index=5*/f32[256,128]{1,0:T(8,128)S(1)}) custom-call(f32[256,1536]{1,0:T(8,128)S(1)} %get-tuple-element.90.grad_ref, ...), custom_call_target="tpu_custom_call" | custom-call | flops 805306368 | bytes 4000000 | tf_op jit(solution)/shard_map/pallas_call | solution.py:347
  342.4 3.5 fusion.13
  352.0 9.3 %reduce-scatter.11.cloned.1.call-done = bf16[64,1024]{1,0:T(8,128)(2,1)} async-done(((bf16[256,1024]{1,0:T(8,128)(2,1)}), bf16[64,1024]{1,0:T(8,128)(2,1)}) %reduce-scatter.11.cloned.1.call-update) | async-done | bytes 131088 | tf_op jit(solution)/shard_map/reduce_scatter | solution.py:766
  366.4 10.0 %shard_map.378 = (bf16[256,512]{1,0:T(8,128)(2,1)S(1)}, f32[1024,128]{1,0:T(8,128)S(1)}, f32[1024,128]{1,0:T(8,128)S(1)}) custom-call(f32[256,512]{1,0:T(8,128)S(1)} %copy-done.11, f32[256,512]{1,0:T(8,128)S(1)} %copy-done.14, f32[256,8]{1,0:T(8,128)S(1)} %copy-done.36, bf16[1024,256]{1,0:T(8,128)(2,1)S(1)} %copy-done.13, bf16[1024,256]{1,0:T(8,128)(2,1)S(1)} %copy-done.13, ...), custom_call_target="tpu_custom_call" | custom-call | flops 2684354560 | bytes 4000000 | tf_op jit(solution)/shard_map/pallas_call | solution.py:583
  383.2 7.9 %shard_map.377 = (f32[256,1536]{1,0:T(8,128)S(1)}, f32[256,24]{1,0:T(8,128)S(1)}, f32[256,128]{1,0:T(8,128)S(1)}, f32[1,24]{1,0:T(1,128)S(1)}) custom-call(bf16[256,1792]{1,0:T(8,128)(2,1)S(1)} %get-tuple-element.237.value_ref.write_ref.read_ref, bf16[256,1792]{1,0:T(8,128)(2,1)S(1)} %get-tuple-element.237.value_ref.write_ref.read_ref, ...), custom_call_target="tpu_custom_call" | custom-call | flops 201326592 | bytes 4000000 | tf_op jit(solution)/shard_map/pallas_call | solution.py:429
  391.1 4.8 collective-permute-start.35
  416.6 3.5 collective-permute-done.35
  433.4 9.9 %collective-permute-done.40 = f32[3,1792]{1,0:T(4,128)} collective-permute-done((f32[3,1792]{1,0:T(4,128)}, f32[3,1792]{1,0:T(4,128)}, u32[]{:S(2)}, u32[]{:S(2)}) %collective-permute-start.40) | collective-permute-done | bytes 21536 | tf_op jit(solution)/shard_map/ppermute | solution.py:27
  461.1 3.5 add_convert_fusion
  485.6 5.8 %collective-permute-done.48 = bf16[128,1920]{1,0:T(8,128)(2,1)S(1)} collective-permute-done((bf16[128,1920]{1,0:T(8,128)(2,1)S(1)}, bf16[128,1920]{1,0:T(8,128)(2,1)S(1)}, u32[]{:S(2)}, u32[]{:S(2)}) %collective-permute-start.48) | collective-permute-done | bytes 491552 | tf_op jit(solution)/shard_map/ppermute | solution.py:658
  491.3 8.2 %collective-permute-done.49 = bf16[128,1920]{1,0:T(8,128)(2,1)S(1)} collective-permute-done((bf16[128,1920]{1,0:T(8,128)(2,1)S(1)}, bf16[128,1920]{1,0:T(8,128)(2,1)S(1)}, u32[]{:S(2)}, u32[]{:S(2)}) %collective-permute-start.49) | collective-permute-done | bytes 491552 | tf_op jit(solution)/shard_map/ppermute | solution.py:658
  513.4 4.9 collective-permute-done.52
  520.7 9.7 %reduce-scatter.5.cloned.1.call-done = bf16[32,2304]{1,0:T(8,128)(2,1)} async-done(((bf16[128,2304]{1,0:T(8,128)(2,1)}), bf16[32,2304]{1,0:T(8,128)(2,1)}) %reduce-scatter.5.cloned.1.call-update) | async-done | bytes 147472 | tf_op jit(solution)/shard_map/reduce_scatter | solution.py:766
  (655 shorter events, 257.0 us)
Async XLA Ops:
  7.2 45.7 %all-gather.8.cloned.1.call-start = ((), (), s32[]{:S(2)}) async-start(), calls=%async_computation.8 | async-start | bytes 1327104 | tf_op jit(solution)/shard_map/all_gather | solution.py:671
  28.6 55.3 %all-gather.10.cloned.1.call-start = ((), (), s32[]{:S(2)}) async-start(), calls=%async_computation.9 | async-start | bytes 2359296 | tf_op jit(solution)/shard_map/all_gather | solution.py:671
  53.0 91.1 %all-gather.12.cloned.1.call-start = ((), (), s32[]{:S(2)}) async-start(), calls=%async_computation.10 | async-start | bytes 2359296 | tf_op jit(solution)/shard_map/all_gather | solution.py:671
  64.4 27.3 %collective-permute-start.9 = (bf16[128,2304]{1,0:T(8,128)(2,1)}, bf16[128,2304]{1,0:T(8,128)(2,1)}, u32[]{:S(2)}, u32[]{:S(2)}) collective-permute-start(bf16[128,2304]{1,0:T(8,128)(2,1)} %bitcast.16), channel_id=1, source_target_pairs={{0,2},{1,3},{2,0},{3,1},{4,6},{5,7},{6,4},{7,5},{8,10},{9,11},{10,... | collective-permute-start | bytes 1769480 | tf_op jit(solution)/shard_map/ppermute | solution.py:658
  69.0 28.2 %collective-permute-start.4 = (bf16[3,1792]{1,0:T(4,128)(2,1)S(1)}, bf16[3,1792]{1,0:T(4,128)(2,1)S(1)}, u32[]{:S(2)}, u32[]{:S(2)}) collective-permute-start(bf16[3,1792]{1,0:T(4,128)(2,1)S(1)} %slice.496), channel_id=1, source_target_pairs={{0,1},{1,2},{2,3},{4,5},{5,6},{6,7},{8,9},{9,10},{10,11},{12,13},{... | collective-permute-start | bytes 32264 | tf_op jit(solution)/shard_map/ppermute | solution.py:27
  83.9 277.4 %reduce-scatter.11.cloned.1.call-start = ((), (), s32[]{:S(2)}) async-start(), calls=%async_computation.7 | async-start | bytes 655360 | tf_op jit(solution)/shard_map/reduce_scatter | solution.py:766
  95.3 36.2 %collective-permute-start.11 = (bf16[512,2304]{1,0:T(8,128)(2,1)}, bf16[512,2304]{1,0:T(8,128)(2,1)}, u32[]{:S(2)}, u32[]{:S(2)}) collective-permute-start(bf16[512,2304]{1,0:T(8,128)(2,1)} %pad_maximum_fusion.1), channel_id=1, source_target_pairs={{0,4},{4,0},{8,12},{12,8},{16,20},{20,16},{24,28},{28,24},{1,5},{5... | collective-permute-start | bytes 7077896 | tf_op jit(solution)/shard_map/ppermute | solution.py:626
  140.3 28.2 %collective-permute-start.17 = (bf16[256,2048]{1,0:T(8,128)(2,1)}, bf16[256,2048]{1,0:T(8,128)(2,1)}, u32[]{:S(2)}, u32[]{:S(2)}) collective-permute-start(bf16[256,2048]{1,0:T(8,128)(2,1)} %bitcast.25), channel_id=1, source_target_pairs={{0,3},{1,2},{2,1},{3,0},{4,7},{5,6},{6,5},{7,4},{8,11},{9,10},{10,... | collective-permute-start | bytes 3145736 | tf_op jit(solution)/shard_map/ppermute | solution.py:658
  145.6 45.2 %collective-permute-start.21 = (bf16[128,4096]{1,0:T(8,128)(2,1)S(1)}, bf16[128,4096]{1,0:T(8,128)(2,1)S(1)}, u32[]{:S(2)}, u32[]{:S(2)}) collective-permute-start(bf16[128,4096]{1,0:T(8,128)(2,1)S(1)} %bitcast.162), channel_id=1, source_target_pairs={{0,3},{1,2},{2,1},{3,0},{4,7},{5,6},{6,5},{7,4},{8,11},{9,10},{10,... | collective-permute-start | bytes 3145736 | tf_op jit(solution)/shard_map/ppermute | solution.py:658
  145.7 66.7 %collective-permute-start.20 = (bf16[128,4096]{1,0:T(8,128)(2,1)S(1)}, bf16[128,4096]{1,0:T(8,128)(2,1)S(1)}, u32[]{:S(2)}, u32[]{:S(2)}) collective-permute-start(bf16[128,4096]{1,0:T(8,128)(2,1)S(1)} %bitcast.163), channel_id=1, source_target_pairs={{0,2},{1,3},{2,0},{3,1},{4,6},{5,7},{6,4},{7,5},{8,10},{9,11},{10,... | collective-permute-start | bytes 3145736 | tf_op jit(solution)/shard_map/ppermute | solution.py:658
  147.3 68.7 %collective-permute-start.19 = (bf16[128,4096]{1,0:T(8,128)(2,1)S(1)}, bf16[128,4096]{1,0:T(8,128)(2,1)S(1)}, u32[]{:S(2)}, u32[]{:S(2)}) collective-permute-start(bf16[128,4096]{1,0:T(8,128)(2,1)S(1)} %bitcast.164), channel_id=1, source_target_pairs={{0,1},{1,0},{2,3},{3,2},{4,5},{5,4},{6,7},{7,6},{8,9},{9,8},{10,11... | collective-permute-start | bytes 3145736 | tf_op jit(solution)/shard_map/ppermute | solution.py:658
  151.1 83.7 %collective-permute-start.16 = (bf16[256,2048]{1,0:T(8,128)(2,1)}, bf16[256,2048]{1,0:T(8,128)(2,1)S(1)}, u32[]{:S(2)}, u32[]{:S(2)}) collective-permute-start(bf16[256,2048]{1,0:T(8,128)(2,1)} %bitcast.25), channel_id=1, source_target_pairs={{0,2},{1,3},{2,0},{3,1},{4,6},{5,7},{6,4},{7,5},{8,10},{9,11},{10,... | collective-permute-start | bytes 3145736 | tf_op jit(solution)/shard_map/ppermute | solution.py:658
  168.5 67.4 %collective-permute-start.15 = (bf16[256,2048]{1,0:T(8,128)(2,1)}, bf16[256,2048]{1,0:T(8,128)(2,1)S(1)}, u32[]{:S(2)}, u32[]{:S(2)}) collective-permute-start(bf16[256,2048]{1,0:T(8,128)(2,1)} %bitcast.25), channel_id=1, source_target_pairs={{0,1},{1,0},{2,3},{3,2},{4,5},{5,4},{6,7},{7,6},{8,9},{9,8},{10,11... | collective-permute-start | bytes 3145736 | tf_op jit(solution)/shard_map/ppermute | solution.py:658
  190.8 47.3 %collective-permute-start.14 = (bf16[256,256]{1,0:T(8,128)(2,1)S(1)}, bf16[256,256]{1,0:T(8,128)(2,1)S(1)}, u32[]{:S(2)}, u32[]{:S(2)}) collective-permute-start(bf16[256,256]{1,0:T(8,128)(2,1)S(1)} %pad_maximum_fusion.19), channel_id=1, source_target_pairs={{0,3},{4,7},{8,11},{12,15},{16,19},{20,23},{24,27},{28,31}} | collective-permute-start | bytes 393224 | tf_op jit(solution)/shard_map/ppermute | solution.py:27
  212.4 27.2 %collective-permute-start.13 = (bf16[256,256]{1,0:T(8,128)(2,1)S(1)}, bf16[256,256]{1,0:T(8,128)(2,1)S(1)}, u32[]{:S(2)}, u32[]{:S(2)}) collective-permute-start(bf16[256,256]{1,0:T(8,128)(2,1)S(1)} %pad_maximum_fusion.19), channel_id=1, source_target_pairs={{0,2},{1,3},{4,6},{5,7},{8,10},{9,11},{12,14},{13,15},{16,18},{17,... | collective-permute-start | bytes 393224 | tf_op jit(solution)/shard_map/ppermute | solution.py:27
  285.3 28.8 %collective-permute-start.27 = (bf16[256,1024]{1,0:T(8,128)(2,1)S(1)}, bf16[256,1024]{1,0:T(8,128)(2,1)S(1)}, u32[]{:S(2)}, u32[]{:S(2)}) collective-permute-start(bf16[256,1024]{1,0:T(8,128)(2,1)S(1)} %add_convert_fusion.9), channel_id=1, source_target_pairs={{0,1},{1,0},{2,3},{3,2},{4,5},{5,4},{6,7},{7,6},{8,9},{9,8},{10,11... | collective-permute-start | bytes 1572872 | tf_op jit(solution)/shard_map/ppermute | solution.py:658
  310.7 52.3 %collective-permute-start.26 = (bf16[1024,1024]{1,0:T(8,128)(2,1)}, bf16[1024,1024]{1,0:T(8,128)(2,1)}, u32[]{:S(2)}, u32[]{:S(2)}) collective-permute-start(bf16[1024,1024]{1,0:T(8,128)(2,1)} %convolution_convert_fusion.3), channel_id=1, source_target_pairs={{0,4},{4,0},{8,12},{12,8},{16,20},{20,16},{24,28},{28,24},{1,5},{5... | collective-permute-start | bytes 6291464 | tf_op jit(solution)/shard_map/ppermute | solution.py:626
  329.2 50.0 %collective-permute-start.30 = (bf16[1568,128]{1,0:T(8,128)(2,1)}, bf16[1568,128]{1,0:T(8,128)(2,1)}, u32[]{:S(2)}, u32[]{:S(2)}) collective-permute-start(bf16[1568,128]{1,0:T(8,128)(2,1)} %pad_maximum_fusion.13), channel_id=1, source_target_pairs={{1,0},{2,1},{3,2},{5,4},{6,5},{7,6},{9,8},{10,9},{11,10},{13,12},{... | collective-permute-start | bytes 1204232 | tf_op jit(solution)/shard_map/ppermute | solution.py:27
  330.5 50.0 %collective-permute-start.31 = (bf16[1568,128]{1,0:T(8,128)(2,1)}, bf16[1568,128]{1,0:T(8,128)(2,1)}, u32[]{:S(2)}, u32[]{:S(2)}) collective-permute-start(bf16[1568,128]{1,0:T(8,128)(2,1)} %pad_maximum_fusion.13), channel_id=1, source_target_pairs={{2,0},{3,1},{6,4},{7,5},{10,8},{11,9},{14,12},{15,13},{18,16},{19,... | collective-permute-start | bytes 1204232 | tf_op jit(solution)/shard_map/ppermute | solution.py:27
  331.8 50.0 %collective-permute-start.32 = (bf16[1568,128]{1,0:T(8,128)(2,1)}, bf16[1568,128]{1,0:T(8,128)(2,1)}, u32[]{:S(2)}, u32[]{:S(2)}) collective-permute-start(bf16[1568,128]{1,0:T(8,128)(2,1)} %pad_maximum_fusion.13), channel_id=1, source_target_pairs={{3,0},{7,4},{11,8},{15,12},{19,16},{23,20},{27,24},{31,28}} | collective-permute-start | bytes 1204232 | tf_op jit(solution)/shard_map/ppermute | solution.py:27
  334.3 169.1 %reduce-scatter.7.cloned.1.call-start = ((), (), s32[]{:S(2)}) async-start(), calls=%async_computation.5 | async-start | bytes 655360 | tf_op jit(solution)/shard_map/reduce_scatter | solution.py:766
  339.5 73.6 %collective-permute-start.33 = (bf16[128,4096]{1,0:T(8,128)(2,1)}, bf16[128,4096]{1,0:T(8,128)(2,1)}, u32[]{:S(2)}, u32[]{:S(2)}) collective-permute-start(bf16[128,4096]{1,0:T(8,128)(2,1)} %fusion.12), channel_id=1, source_target_pairs={{0,1},{1,0},{2,3},{3,2},{4,5},{5,4},{6,7},{7,6},{8,9},{9,8},{10,11... | collective-permute-start | bytes 3145736 | tf_op jit(solution)/shard_map/ppermute | solution.py:658
  363.0 50.7 %collective-permute-start.34 = (bf16[128,4096]{1,0:T(8,128)(2,1)}, bf16[128,4096]{1,0:T(8,128)(2,1)S(1)}, u32[]{:S(2)}, u32[]{:S(2)}) collective-permute-start(bf16[128,4096]{1,0:T(8,128)(2,1)} %fusion.13), channel_id=1, source_target_pairs={{0,2},{1,3},{2,0},{3,1},{4,6},{5,7},{6,4},{7,5},{8,10},{9,11},{10,... | collective-permute-start | bytes 3145736 | tf_op jit(solution)/shard_map/ppermute | solution.py:658
  391.1 28.9 %collective-permute-start.35 = (bf16[128,4096]{1,0:T(8,128)(2,1)S(1)}, bf16[128,4096]{1,0:T(8,128)(2,1)S(1)}, u32[]{:S(2)}, u32[]{:S(2)}) collective-permute-start(bf16[128,4096]{1,0:T(8,128)(2,1)S(1)} %copy-done.98), channel_id=1, source_target_pairs={{0,3},{1,2},{2,1},{3,0},{4,7},{5,6},{6,5},{7,4},{8,11},{9,10},{10,... | collective-permute-start | bytes 3145736 | tf_op jit(solution)/shard_map/ppermute | solution.py:658
  395.9 48.9 %collective-permute-start.41 = (bf16[256,1024]{1,0:T(8,128)(2,1)S(1)}, bf16[256,1024]{1,0:T(8,128)(2,1)}, u32[]{:S(2)}, u32[]{:S(2)}) collective-permute-start(bf16[256,1024]{1,0:T(8,128)(2,1)S(1)} %fusion.54), channel_id=1, source_target_pairs={{0,1},{1,0},{2,3},{3,2},{4,5},{5,4},{6,7},{7,6},{8,9},{9,8},{10,11... | collective-permute-start | bytes 1572872 | tf_op jit(solution)/shard_map/ppermute | solution.py:658
  413.1 33.5 %collective-permute-start.42 = (bf16[256,1024]{1,0:T(8,128)(2,1)}, bf16[256,1024]{1,0:T(8,128)(2,1)}, u32[]{:S(2)}, u32[]{:S(2)}) collective-permute-start(bf16[256,1024]{1,0:T(8,128)(2,1)} %fusion.55), channel_id=1, source_target_pairs={{0,2},{1,3},{2,0},{3,1},{4,6},{5,7},{6,4},{7,5},{8,10},{9,11},{10,... | collective-permute-start | bytes 1572872 | tf_op jit(solution)/shard_map/ppermute | solution.py:658
  413.7 32.9 %collective-permute-start.43 = (bf16[256,1024]{1,0:T(8,128)(2,1)S(1)}, bf16[256,1024]{1,0:T(8,128)(2,1)}, u32[]{:S(2)}, u32[]{:S(2)}) collective-permute-start(bf16[256,1024]{1,0:T(8,128)(2,1)S(1)} %fusion.56), channel_id=1, source_target_pairs={{0,3},{1,2},{2,1},{3,0},{4,7},{5,6},{6,5},{7,4},{8,11},{9,10},{10,... | collective-permute-start | bytes 1572872 | tf_op jit(solution)/shard_map/ppermute | solution.py:658
  430.6 51.1 %collective-permute-start.44 = (bf16[128,2304]{1,0:T(8,128)(2,1)}, bf16[128,2304]{1,0:T(8,128)(2,1)}, u32[]{:S(2)}, u32[]{:S(2)}) collective-permute-start(bf16[128,2304]{1,0:T(8,128)(2,1)} %add_convert_fusion.4), channel_id=1, source_target_pairs={{0,1},{1,0},{2,3},{3,2},{4,5},{5,4},{6,7},{7,6},{8,9},{9,8},{10,11... | collective-permute-start | bytes 1769480 | tf_op jit(solution)/shard_map/ppermute | solution.py:658
  443.3 42.3 %collective-permute-start.45 = (bf16[128,2304]{1,0:T(8,128)(2,1)}, bf16[128,2304]{1,0:T(8,128)(2,1)}, u32[]{:S(2)}, u32[]{:S(2)}) collective-permute-start(bf16[128,2304]{1,0:T(8,128)(2,1)} %add_convert_fusion.3), channel_id=1, source_target_pairs={{0,2},{1,3},{2,0},{3,1},{4,6},{5,7},{6,4},{7,5},{8,10},{9,11},{10,... | collective-permute-start | bytes 1769480 | tf_op jit(solution)/shard_map/ppermute | solution.py:658
  444.8 40.7 %collective-permute-start.46 = (bf16[128,2304]{1,0:T(8,128)(2,1)}, bf16[128,2304]{1,0:T(8,128)(2,1)}, u32[]{:S(2)}, u32[]{:S(2)}) collective-permute-start(bf16[128,2304]{1,0:T(8,128)(2,1)} %add_convert_fusion.2), channel_id=1, source_target_pairs={{0,3},{1,2},{2,1},{3,0},{4,7},{5,6},{6,5},{7,4},{8,11},{9,10},{10,... | collective-permute-start | bytes 1769480 | tf_op jit(solution)/shard_map/ppermute | solution.py:658
  459.0 52.5 %reduce-scatter.9.cloned.1.call-start = ((), (), s32[]{:S(2)}) async-start(), calls=%async_computation.6 | async-start | bytes 1310720 | tf_op jit(solution)/shard_map/reduce_scatter | solution.py:766
  464.6 65.8 %reduce-scatter.5.cloned.1.call-start = ((), (), s32[]{:S(2)}) async-start(), calls=%async_computation.4 | async-start | bytes 737280 | tf_op jit(solution)/shard_map/reduce_scatter | solution.py:766
  (207 other events, 2431.3 us)
Sparse Core Ops, SparseCore 0:
  28.7 24.2 all-gather.7
  55.1 28.7 all-gather.9
  86.1 28.5 all-gather.11
  334.4 26.9 reduce-scatter.10
  459.1 20.1 reduce-scatter.6
  481.5 25.4 reduce-scatter.8
  509.4 20.9 reduce-scatter.4

commit v3 on v2

--- a/solution.py
+++ b/solution.py
@@ -147,7 +147,7 @@
         out_shape=out_shape,
         scratch_shapes=list(scratch),
         compiler_params=pltpu.CompilerParams(
-            dimension_semantics=("arbitrary",), vmem_limit_bytes=40 * 1024 * 1024
+            dimension_semantics=("arbitrary",), vmem_limit_bytes=24 * 1024 * 1024
         ),
         cost_estimate=pl.CostEstimate(flops=flops, bytes_accessed=4000000, transcendentals=0),
     )

time: 551 us -> 550 us (level)
    unnamed x349 -> x347, local copies, waits for them, and re-layouts: 17.3 us -> 18.6 us
where the time goes in v3:
time: 550 us; the launch traced here: 541 us
  waiting for transfers between devices  177 us (32%)
  matrix products  107 us (19%)
  starting transfers between devices  81 us (15%)
  other arithmetic  49.1 us (9%)
  Pallas kernels  45.3 us (8%)
  local copies, waits for them, and re-layouts  44.4 us (8%)
  between operations  18.9 us (3%)
  blocking collectives  17.9 us (3%)
    ppermute x27, waiting for transfers between devices, shift_piece(): return lax.ppermute(x, 'seq', pairs)  94.7 us
    ppermute x27, starting transfers between devices, shift_piece(): return lax.ppermute(x, 'seq', pairs)  40.9 us
    dot_general x25, matrix products, rows_product(): lax.dot_general(left, right, (((0,), (0,)), ((), ())), preferred_element_...  40.5 us
    dot_general x18, matrix products, back_product(): lax.dot_general(left, right, (((1,), (1,)), ((), ())), preferred_element_...  37 us
    ppermute x14, starting transfers between devices, passed_along(): return lax.ppermute(x, axis, pairs)  32.2 us
    dot_general x14, matrix products, matmul(): return jnp.dot(left, right, preferred_element_type=jnp.float32)  27.3 us
    all_gather x3, waiting for transfers between devices, gather_levels(): return lax.all_gather(packed, 'dp')  26.7 us
    ppermute x14, waiting for transfers between devices, passed_along(): return lax.ppermute(x, axis, pairs)  24.7 us
  transfers between devices with their start and end apart: 66, of which 27 were waited for; matrix products, arithmetic and copies ran while one was open for 32% of the time, Pallas kernels for 8%

profile of v3, /device:TPU:0, one launch (start us, length us, event | category | flops | bytes accessed | tf_op | source)
XLA Modules:
  0.0 541.2 jit_solution(7697427133090189011)
XLA Ops:
  9.0 17.9 %all-gather = bf16[256,1920]{1,0:T(8,128)(2,1)S(1)} all-gather(bf16[32,1920]{1,0:T(8,128)(2,1)S(1)} %fusion.158), channel_id=2, replica_groups=mesh['dp'=8,'seq'=4] {'dp'}, dimensions={0}, use_global_device_ids=true | all-gather | bytes 1105920 | tf_op jit(solution)/shard_map/all_gather | solution.py:671
  37.3 15.7 %all-gather.8.cloned.1.call-done = bf16[256,2304]{1,0:T(8,128)(2,1)} async-done(((bf16[32,2304]{1,0:T(8,128)(2,1)}), bf16[256,2304]{1,0:T(8,128)(2,1)}) %all-gather.8.cloned.1.call-update) | async-done | bytes 1179664 | tf_op jit(solution)/shard_map/all_gather | solution.py:671
  72.9 11.0 %all-gather.10.cloned.1.call-done = bf16[512,2048]{1,0:T(8,128)(2,1)} async-done(((bf16[64,2048]{1,0:T(8,128)(2,1)}), bf16[512,2048]{1,0:T(8,128)(2,1)}) %all-gather.10.cloned.1.call-update) | async-done | bytes 2097168 | tf_op jit(solution)/shard_map/all_gather | solution.py:671
  84.0 7.7 %collective-permute-done.9 = bf16[128,2304]{1,0:T(8,128)(2,1)} collective-permute-done((bf16[128,2304]{1,0:T(8,128)(2,1)}, bf16[128,2304]{1,0:T(8,128)(2,1)}, u32[]{:S(2)}, u32[]{:S(2)}) %collective-permute-start.9) | collective-permute-done | bytes 589856 | tf_op jit(solution)/shard_map/ppermute | solution.py:658
  100.5 5.6 %shard_map.373 = (f32[256,1536]{1,0:T(8,128)S(1)}, f32[1536,128]{1,0:T(8,128)S(1)}) custom-call(bf16[256,1792]{1,0:T(8,128)(2,1)S(1)} %get-tuple-element.237.value_ref.write_ref.read_ref, bf16[256,1792]{1,0:T(8,128)(2,1)S(1)} %get-tuple-element.237.value_ref.write_ref.read_ref, bf16[256,1792]{1,0:T(8,128)(2,1)S(1)} %get-tuple-element.237.value_ref.write_ref.read_ref, ...), custom_call_target="tpu_custom_call" | custom-call | flops 402653184 | bytes 4000000 | tf_op jit(solution)/shard_map/pallas_call | solution.py:199
  119.2 9.3 %collective-permute-done.6.refs_2_.refs_3_ = bf16[1568,128]{1,0:T(8,128)(2,1)S(1)} collective-permute-done((bf16[1568,128]{1,0:T(8,128)(2,1)S(1)}, bf16[1568,128]{1,0:T(8,128)(2,1)S(1)}, u32[]{:S(2)}, u32[]{:S(2)}) %collective-permute-start.6) | collective-permute-done | bytes 401440 | tf_op jit(solution)/shard_map/ppermute | solution.py:27
  140.2 3.8 collective-permute-start.17
  152.3 16.2 %collective-permute-done.17 = bf16[256,2048]{1,0:T(8,128)(2,1)} collective-permute-done((bf16[256,2048]{1,0:T(8,128)(2,1)}, bf16[256,2048]{1,0:T(8,128)(2,1)}, u32[]{:S(2)}, u32[]{:S(2)}) %collective-permute-start.17) | collective-permute-done | bytes 1048608 | tf_op jit(solution)/shard_map/ppermute | solution.py:658
  170.8 20.0 %collective-permute-done.21 = bf16[128,4096]{1,0:T(8,128)(2,1)S(1)} collective-permute-done((bf16[128,4096]{1,0:T(8,128)(2,1)S(1)}, bf16[128,4096]{1,0:T(8,128)(2,1)S(1)}, u32[]{:S(2)}, u32[]{:S(2)}) %collective-permute-start.21) | collective-permute-done | bytes 1048608 | tf_op jit(solution)/shard_map/ppermute | solution.py:658
  190.8 4.9 collective-permute-start.14
  195.6 16.7 %collective-permute-done.20 = bf16[128,4096]{1,0:T(8,128)(2,1)S(1)} collective-permute-done((bf16[128,4096]{1,0:T(8,128)(2,1)S(1)}, bf16[128,4096]{1,0:T(8,128)(2,1)S(1)}, u32[]{:S(2)}, u32[]{:S(2)}) %collective-permute-start.20) | collective-permute-done | bytes 1048608 | tf_op jit(solution)/shard_map/ppermute | solution.py:658
  212.3 3.6 collective-permute-start.13
  219.7 15.0 %collective-permute-done.16 = bf16[256,2048]{1,0:T(8,128)(2,1)S(1)} collective-permute-done((bf16[256,2048]{1,0:T(8,128)(2,1)}, bf16[256,2048]{1,0:T(8,128)(2,1)S(1)}, u32[]{:S(2)}, u32[]{:S(2)}) %collective-permute-start.16) | collective-permute-done | bytes 1048608 | tf_op jit(solution)/shard_map/ppermute | solution.py:658
  239.7 7.7 %shard_map.375 = (bf16[256,512]{1,0:T(8,128)(2,1)S(1)}, f32[256,8]{1,0:T(8,128)S(1)}) custom-call(f32[256,512]{1,0:T(8,128)S(1)} %slice.505.query_ref, bf16[1024,256]{1,0:T(8,128)(2,1)S(1)} %pad_maximum_fusion.11.keys_ref.values_ref, bf16[1024,256]{1,0:T(8,128)(2,1)S(1)} %pad_maximum_fusion.11.keys_ref.values_ref, ...), custom_call_target="tpu_custom_call" | custom-call | flops 1073741824 | bytes 4000000 | tf_op jit(solution)/shard_map/pallas_call | solution.py:523
  260.6 4.1 fusion.24
  266.9 3.5 fusion
  270.4 4.3 fusion.32
  302.5 3.5 fusion.3
  306.1 3.8 fusion.21
  313.4 11.3 %shard_map.376 = (f32[256,1536]{1,0:T(8,128)S(1)}, f32[1536,128]{1,0:T(8,128)S(1)}, f32[256,24]{1,0:T(8,128)S(1)}, f32[24,256]{1,0:T(8,128)S(1)}, f32[256,128]{1,0:T(8,128)S(1)}, /*index=5*/f32[256,128]{1,0:T(8,128)S(1)}) custom-call(f32[256,1536]{1,0:T(8,128)S(1)} %get-tuple-element.90.grad_ref, ...), custom_call_target="tpu_custom_call" | custom-call | flops 805306368 | bytes 4000000 | tf_op jit(solution)/shard_map/pallas_call | solution.py:347
  341.6 3.5 fusion.13
  351.2 9.3 %reduce-scatter.11.cloned.1.call-done = bf16[64,1024]{1,0:T(8,128)(2,1)} async-done(((bf16[256,1024]{1,0:T(8,128)(2,1)}), bf16[64,1024]{1,0:T(8,128)(2,1)}) %reduce-scatter.11.cloned.1.call-update) | async-done | bytes 131088 | tf_op jit(solution)/shard_map/reduce_scatter | solution.py:766
  365.6 10.0 %shard_map.378 = (bf16[256,512]{1,0:T(8,128)(2,1)S(1)}, f32[1024,128]{1,0:T(8,128)S(1)}, f32[1024,128]{1,0:T(8,128)S(1)}) custom-call(f32[256,512]{1,0:T(8,128)S(1)} %copy-done.11, f32[256,512]{1,0:T(8,128)S(1)} %copy-done.14, f32[256,8]{1,0:T(8,128)S(1)} %copy-done.36, bf16[1024,256]{1,0:T(8,128)(2,1)S(1)} %copy-done.13, bf16[1024,256]{1,0:T(8,128)(2,1)S(1)} %copy-done.13, ...), custom_call_target="tpu_custom_call" | custom-call | flops 2684354560 | bytes 4000000 | tf_op jit(solution)/shard_map/pallas_call | solution.py:583
  382.4 7.9 %shard_map.377 = (f32[256,1536]{1,0:T(8,128)S(1)}, f32[256,24]{1,0:T(8,128)S(1)}, f32[256,128]{1,0:T(8,128)S(1)}, f32[1,24]{1,0:T(1,128)S(1)}) custom-call(bf16[256,1792]{1,0:T(8,128)(2,1)S(1)} %get-tuple-element.237.value_ref.write_ref.read_ref, bf16[256,1792]{1,0:T(8,128)(2,1)S(1)} %get-tuple-element.237.value_ref.write_ref.read_ref, ...), custom_call_target="tpu_custom_call" | custom-call | flops 201326592 | bytes 4000000 | tf_op jit(solution)/shard_map/pallas_call | solution.py:429
  390.4 4.8 collective-permute-start.35
  415.8 3.5 collective-permute-done.35
  432.6 9.9 %collective-permute-done.40 = f32[3,1792]{1,0:T(4,128)} collective-permute-done((f32[3,1792]{1,0:T(4,128)}, f32[3,1792]{1,0:T(4,128)}, u32[]{:S(2)}, u32[]{:S(2)}) %collective-permute-start.40) | collective-permute-done | bytes 21536 | tf_op jit(solution)/shard_map/ppermute | solution.py:27
  460.3 3.5 add_convert_fusion
  484.8 5.8 %collective-permute-done.48 = bf16[128,1920]{1,0:T(8,128)(2,1)S(1)} collective-permute-done((bf16[128,1920]{1,0:T(8,128)(2,1)S(1)}, bf16[128,1920]{1,0:T(8,128)(2,1)S(1)}, u32[]{:S(2)}, u32[]{:S(2)}) %collective-permute-start.48) | collective-permute-done | bytes 491552 | tf_op jit(solution)/shard_map/ppermute | solution.py:658
  490.6 8.2 %collective-permute-done.49 = bf16[128,1920]{1,0:T(8,128)(2,1)S(1)} collective-permute-done((bf16[128,1920]{1,0:T(8,128)(2,1)S(1)}, bf16[128,1920]{1,0:T(8,128)(2,1)S(1)}, u32[]{:S(2)}, u32[]{:S(2)}) %collective-permute-start.49) | collective-permute-done | bytes 491552 | tf_op jit(solution)/shard_map/ppermute | solution.py:658
  512.6 5.0 collective-permute-done.52
  520.0 9.6 %reduce-scatter.5.cloned.1.call-done = bf16[32,2304]{1,0:T(8,128)(2,1)} async-done(((bf16[128,2304]{1,0:T(8,128)(2,1)}), bf16[32,2304]{1,0:T(8,128)(2,1)}) %reduce-scatter.5.cloned.1.call-update) | async-done | bytes 147472 | tf_op jit(solution)/shard_map/reduce_scatter | solution.py:766
  (653 shorter events, 256.0 us)
Async XLA Ops:
  7.2 45.7 %all-gather.8.cloned.1.call-start = ((), (), s32[]{:S(2)}) async-start(), calls=%async_computation.8 | async-start | bytes 1327104 | tf_op jit(solution)/shard_map/all_gather | solution.py:671
  28.6 55.3 %all-gather.10.cloned.1.call-start = ((), (), s32[]{:S(2)}) async-start(), calls=%async_computation.9 | async-start | bytes 2359296 | tf_op jit(solution)/shard_map/all_gather | solution.py:671
  53.0 91.1 %all-gather.12.cloned.1.call-start = ((), (), s32[]{:S(2)}) async-start(), calls=%async_computation.10 | async-start | bytes 2359296 | tf_op jit(solution)/shard_map/all_gather | solution.py:671
  64.4 27.3 %collective-permute-start.9 = (bf16[128,2304]{1,0:T(8,128)(2,1)}, bf16[128,2304]{1,0:T(8,128)(2,1)}, u32[]{:S(2)}, u32[]{:S(2)}) collective-permute-start(bf16[128,2304]{1,0:T(8,128)(2,1)} %bitcast.16), channel_id=1, source_target_pairs={{0,2},{1,3},{2,0},{3,1},{4,6},{5,7},{6,4},{7,5},{8,10},{9,11},{10,... | collective-permute-start | bytes 1769480 | tf_op jit(solution)/shard_map/ppermute | solution.py:658
  69.0 28.2 %collective-permute-start.4 = (bf16[3,1792]{1,0:T(4,128)(2,1)S(1)}, bf16[3,1792]{1,0:T(4,128)(2,1)S(1)}, u32[]{:S(2)}, u32[]{:S(2)}) collective-permute-start(bf16[3,1792]{1,0:T(4,128)(2,1)S(1)} %slice.496), channel_id=1, source_target_pairs={{0,1},{1,2},{2,3},{4,5},{5,6},{6,7},{8,9},{9,10},{10,11},{12,13},{... | collective-permute-start | bytes 32264 | tf_op jit(solution)/shard_map/ppermute | solution.py:27
  83.9 276.6 %reduce-scatter.11.cloned.1.call-start = ((), (), s32[]{:S(2)}) async-start(), calls=%async_computation.7 | async-start | bytes 655360 | tf_op jit(solution)/shard_map/reduce_scatter | solution.py:766
  95.2 36.2 %collective-permute-start.11 = (bf16[512,2304]{1,0:T(8,128)(2,1)}, bf16[512,2304]{1,0:T(8,128)(2,1)}, u32[]{:S(2)}, u32[]{:S(2)}) collective-permute-start(bf16[512,2304]{1,0:T(8,128)(2,1)} %pad_maximum_fusion.1), channel_id=1, source_target_pairs={{0,4},{4,0},{8,12},{12,8},{16,20},{20,16},{24,28},{28,24},{1,5},{5... | collective-permute-start | bytes 7077896 | tf_op jit(solution)/shard_map/ppermute | solution.py:626
  140.2 28.2 %collective-permute-start.17 = (bf16[256,2048]{1,0:T(8,128)(2,1)}, bf16[256,2048]{1,0:T(8,128)(2,1)}, u32[]{:S(2)}, u32[]{:S(2)}) collective-permute-start(bf16[256,2048]{1,0:T(8,128)(2,1)} %bitcast.25), channel_id=1, source_target_pairs={{0,3},{1,2},{2,1},{3,0},{4,7},{5,6},{6,5},{7,4},{8,11},{9,10},{10,... | collective-permute-start | bytes 3145736 | tf_op jit(solution)/shard_map/ppermute | solution.py:658
  145.5 45.2 %collective-permute-start.21 = (bf16[128,4096]{1,0:T(8,128)(2,1)S(1)}, bf16[128,4096]{1,0:T(8,128)(2,1)S(1)}, u32[]{:S(2)}, u32[]{:S(2)}) collective-permute-start(bf16[128,4096]{1,0:T(8,128)(2,1)S(1)} %bitcast.162), channel_id=1, source_target_pairs={{0,3},{1,2},{2,1},{3,0},{4,7},{5,6},{6,5},{7,4},{8,11},{9,10},{10,... | collective-permute-start | bytes 3145736 | tf_op jit(solution)/shard_map/ppermute | solution.py:658
  145.6 66.7 %collective-permute-start.20 = (bf16[128,4096]{1,0:T(8,128)(2,1)S(1)}, bf16[128,4096]{1,0:T(8,128)(2,1)S(1)}, u32[]{:S(2)}, u32[]{:S(2)}) collective-permute-start(bf16[128,4096]{1,0:T(8,128)(2,1)S(1)} %bitcast.163), channel_id=1, source_target_pairs={{0,2},{1,3},{2,0},{3,1},{4,6},{5,7},{6,4},{7,5},{8,10},{9,11},{10,... | collective-permute-start | bytes 3145736 | tf_op jit(solution)/shard_map/ppermute | solution.py:658
  147.2 68.7 %collective-permute-start.19 = (bf16[128,4096]{1,0:T(8,128)(2,1)S(1)}, bf16[128,4096]{1,0:T(8,128)(2,1)S(1)}, u32[]{:S(2)}, u32[]{:S(2)}) collective-permute-start(bf16[128,4096]{1,0:T(8,128)(2,1)S(1)} %bitcast.164), channel_id=1, source_target_pairs={{0,1},{1,0},{2,3},{3,2},{4,5},{5,4},{6,7},{7,6},{8,9},{9,8},{10,11... | collective-permute-start | bytes 3145736 | tf_op jit(solution)/shard_map/ppermute | solution.py:658
  150.9 83.8 %collective-permute-start.16 = (bf16[256,2048]{1,0:T(8,128)(2,1)}, bf16[256,2048]{1,0:T(8,128)(2,1)S(1)}, u32[]{:S(2)}, u32[]{:S(2)}) collective-permute-start(bf16[256,2048]{1,0:T(8,128)(2,1)} %bitcast.25), channel_id=1, source_target_pairs={{0,2},{1,3},{2,0},{3,1},{4,6},{5,7},{6,4},{7,5},{8,10},{9,11},{10,... | collective-permute-start | bytes 3145736 | tf_op jit(solution)/shard_map/ppermute | solution.py:658
  168.5 67.4 %collective-permute-start.15 = (bf16[256,2048]{1,0:T(8,128)(2,1)}, bf16[256,2048]{1,0:T(8,128)(2,1)S(1)}, u32[]{:S(2)}, u32[]{:S(2)}) collective-permute-start(bf16[256,2048]{1,0:T(8,128)(2,1)} %bitcast.25), channel_id=1, source_target_pairs={{0,1},{1,0},{2,3},{3,2},{4,5},{5,4},{6,7},{7,6},{8,9},{9,8},{10,11... | collective-permute-start | bytes 3145736 | tf_op jit(solution)/shard_map/ppermute | solution.py:658
  190.8 47.3 %collective-permute-start.14 = (bf16[256,256]{1,0:T(8,128)(2,1)S(1)}, bf16[256,256]{1,0:T(8,128)(2,1)S(1)}, u32[]{:S(2)}, u32[]{:S(2)}) collective-permute-start(bf16[256,256]{1,0:T(8,128)(2,1)S(1)} %pad_maximum_fusion.19), channel_id=1, source_target_pairs={{0,3},{4,7},{8,11},{12,15},{16,19},{20,23},{24,27},{28,31}} | collective-permute-start | bytes 393224 | tf_op jit(solution)/shard_map/ppermute | solution.py:27
  212.3 27.2 %collective-permute-start.13 = (bf16[256,256]{1,0:T(8,128)(2,1)S(1)}, bf16[256,256]{1,0:T(8,128)(2,1)S(1)}, u32[]{:S(2)}, u32[]{:S(2)}) collective-permute-start(bf16[256,256]{1,0:T(8,128)(2,1)S(1)} %pad_maximum_fusion.19), channel_id=1, source_target_pairs={{0,2},{1,3},{4,6},{5,7},{8,10},{9,11},{12,14},{13,15},{16,18},{17,... | collective-permute-start | bytes 393224 | tf_op jit(solution)/shard_map/ppermute | solution.py:27
  284.5 28.8 %collective-permute-start.27 = (bf16[256,1024]{1,0:T(8,128)(2,1)S(1)}, bf16[256,1024]{1,0:T(8,128)(2,1)S(1)}, u32[]{:S(2)}, u32[]{:S(2)}) collective-permute-start(bf16[256,1024]{1,0:T(8,128)(2,1)S(1)} %add_convert_fusion.9), channel_id=1, source_target_pairs={{0,1},{1,0},{2,3},{3,2},{4,5},{5,4},{6,7},{7,6},{8,9},{9,8},{10,11... | collective-permute-start | bytes 1572872 | tf_op jit(solution)/shard_map/ppermute | solution.py:658
  309.9 52.3 %collective-permute-start.26 = (bf16[1024,1024]{1,0:T(8,128)(2,1)}, bf16[1024,1024]{1,0:T(8,128)(2,1)}, u32[]{:S(2)}, u32[]{:S(2)}) collective-permute-start(bf16[1024,1024]{1,0:T(8,128)(2,1)} %convolution_convert_fusion.3), channel_id=1, source_target_pairs={{0,4},{4,0},{8,12},{12,8},{16,20},{20,16},{24,28},{28,24},{1,5},{5... | collective-permute-start | bytes 6291464 | tf_op jit(solution)/shard_map/ppermute | solution.py:626
  328.4 50.0 %collective-permute-start.30 = (bf16[1568,128]{1,0:T(8,128)(2,1)}, bf16[1568,128]{1,0:T(8,128)(2,1)}, u32[]{:S(2)}, u32[]{:S(2)}) collective-permute-start(bf16[1568,128]{1,0:T(8,128)(2,1)} %pad_maximum_fusion.13), channel_id=1, source_target_pairs={{1,0},{2,1},{3,2},{5,4},{6,5},{7,6},{9,8},{10,9},{11,10},{13,12},{... | collective-permute-start | bytes 1204232 | tf_op jit(solution)/shard_map/ppermute | solution.py:27
  329.7 50.0 %collective-permute-start.31 = (bf16[1568,128]{1,0:T(8,128)(2,1)}, bf16[1568,128]{1,0:T(8,128)(2,1)}, u32[]{:S(2)}, u32[]{:S(2)}) collective-permute-start(bf16[1568,128]{1,0:T(8,128)(2,1)} %pad_maximum_fusion.13), channel_id=1, source_target_pairs={{2,0},{3,1},{6,4},{7,5},{10,8},{11,9},{14,12},{15,13},{18,16},{19,... | collective-permute-start | bytes 1204232 | tf_op jit(solution)/shard_map/ppermute | solution.py:27
  331.0 50.1 %collective-permute-start.32 = (bf16[1568,128]{1,0:T(8,128)(2,1)}, bf16[1568,128]{1,0:T(8,128)(2,1)}, u32[]{:S(2)}, u32[]{:S(2)}) collective-permute-start(bf16[1568,128]{1,0:T(8,128)(2,1)} %pad_maximum_fusion.13), channel_id=1, source_target_pairs={{3,0},{7,4},{11,8},{15,12},{19,16},{23,20},{27,24},{31,28}} | collective-permute-start | bytes 1204232 | tf_op jit(solution)/shard_map/ppermute | solution.py:27
  333.5 169.1 %reduce-scatter.7.cloned.1.call-start = ((), (), s32[]{:S(2)}) async-start(), calls=%async_computation.5 | async-start | bytes 655360 | tf_op jit(solution)/shard_map/reduce_scatter | solution.py:766
  338.7 73.6 %collective-permute-start.33 = (bf16[128,4096]{1,0:T(8,128)(2,1)}, bf16[128,4096]{1,0:T(8,128)(2,1)}, u32[]{:S(2)}, u32[]{:S(2)}) collective-permute-start(bf16[128,4096]{1,0:T(8,128)(2,1)} %fusion.12), channel_id=1, source_target_pairs={{0,1},{1,0},{2,3},{3,2},{4,5},{5,4},{6,7},{7,6},{8,9},{9,8},{10,11... | collective-permute-start | bytes 3145736 | tf_op jit(solution)/shard_map/ppermute | solution.py:658
  362.2 50.7 %collective-permute-start.34 = (bf16[128,4096]{1,0:T(8,128)(2,1)}, bf16[128,4096]{1,0:T(8,128)(2,1)S(1)}, u32[]{:S(2)}, u32[]{:S(2)}) collective-permute-start(bf16[128,4096]{1,0:T(8,128)(2,1)} %fusion.13), channel_id=1, source_target_pairs={{0,2},{1,3},{2,0},{3,1},{4,6},{5,7},{6,4},{7,5},{8,10},{9,11},{10,... | collective-permute-start | bytes 3145736 | tf_op jit(solution)/shard_map/ppermute | solution.py:658
  390.4 28.9 %collective-permute-start.35 = (bf16[128,4096]{1,0:T(8,128)(2,1)S(1)}, bf16[128,4096]{1,0:T(8,128)(2,1)S(1)}, u32[]{:S(2)}, u32[]{:S(2)}) collective-permute-start(bf16[128,4096]{1,0:T(8,128)(2,1)S(1)} %copy-done.98), channel_id=1, source_target_pairs={{0,3},{1,2},{2,1},{3,0},{4,7},{5,6},{6,5},{7,4},{8,11},{9,10},{10,... | collective-permute-start | bytes 3145736 | tf_op jit(solution)/shard_map/ppermute | solution.py:658
  395.2 48.9 %collective-permute-start.41 = (bf16[256,1024]{1,0:T(8,128)(2,1)S(1)}, bf16[256,1024]{1,0:T(8,128)(2,1)}, u32[]{:S(2)}, u32[]{:S(2)}) collective-permute-start(bf16[256,1024]{1,0:T(8,128)(2,1)S(1)} %fusion.54), channel_id=1, source_target_pairs={{0,1},{1,0},{2,3},{3,2},{4,5},{5,4},{6,7},{7,6},{8,9},{9,8},{10,11... | collective-permute-start | bytes 1572872 | tf_op jit(solution)/shard_map/ppermute | solution.py:658
  412.3 33.6 %collective-permute-start.42 = (bf16[256,1024]{1,0:T(8,128)(2,1)}, bf16[256,1024]{1,0:T(8,128)(2,1)}, u32[]{:S(2)}, u32[]{:S(2)}) collective-permute-start(bf16[256,1024]{1,0:T(8,128)(2,1)} %fusion.55), channel_id=1, source_target_pairs={{0,2},{1,3},{2,0},{3,1},{4,6},{5,7},{6,4},{7,5},{8,10},{9,11},{10,... | collective-permute-start | bytes 1572872 | tf_op jit(solution)/shard_map/ppermute | solution.py:658
  412.9 32.9 %collective-permute-start.43 = (bf16[256,1024]{1,0:T(8,128)(2,1)S(1)}, bf16[256,1024]{1,0:T(8,128)(2,1)}, u32[]{:S(2)}, u32[]{:S(2)}) collective-permute-start(bf16[256,1024]{1,0:T(8,128)(2,1)S(1)} %fusion.56), channel_id=1, source_target_pairs={{0,3},{1,2},{2,1},{3,0},{4,7},{5,6},{6,5},{7,4},{8,11},{9,10},{10,... | collective-permute-start | bytes 1572872 | tf_op jit(solution)/shard_map/ppermute | solution.py:658
  429.8 51.1 %collective-permute-start.44 = (bf16[128,2304]{1,0:T(8,128)(2,1)}, bf16[128,2304]{1,0:T(8,128)(2,1)}, u32[]{:S(2)}, u32[]{:S(2)}) collective-permute-start(bf16[128,2304]{1,0:T(8,128)(2,1)} %add_convert_fusion.4), channel_id=1, source_target_pairs={{0,1},{1,0},{2,3},{3,2},{4,5},{5,4},{6,7},{7,6},{8,9},{9,8},{10,11... | collective-permute-start | bytes 1769480 | tf_op jit(solution)/shard_map/ppermute | solution.py:658
  442.5 42.3 %collective-permute-start.45 = (bf16[128,2304]{1,0:T(8,128)(2,1)}, bf16[128,2304]{1,0:T(8,128)(2,1)}, u32[]{:S(2)}, u32[]{:S(2)}) collective-permute-start(bf16[128,2304]{1,0:T(8,128)(2,1)} %add_convert_fusion.3), channel_id=1, source_target_pairs={{0,2},{1,3},{2,0},{3,1},{4,6},{5,7},{6,4},{7,5},{8,10},{9,11},{10,... | collective-permute-start | bytes 1769480 | tf_op jit(solution)/shard_map/ppermute | solution.py:658
  444.1 40.7 %collective-permute-start.46 = (bf16[128,2304]{1,0:T(8,128)(2,1)}, bf16[128,2304]{1,0:T(8,128)(2,1)}, u32[]{:S(2)}, u32[]{:S(2)}) collective-permute-start(bf16[128,2304]{1,0:T(8,128)(2,1)} %add_convert_fusion.2), channel_id=1, source_target_pairs={{0,3},{1,2},{2,1},{3,0},{4,7},{5,6},{6,5},{7,4},{8,11},{9,10},{10,... | collective-permute-start | bytes 1769480 | tf_op jit(solution)/shard_map/ppermute | solution.py:658
  458.3 52.5 %reduce-scatter.9.cloned.1.call-start = ((), (), s32[]{:S(2)}) async-start(), calls=%async_computation.6 | async-start | bytes 1310720 | tf_op jit(solution)/shard_map/reduce_scatter | solution.py:766
  463.8 65.8 %reduce-scatter.5.cloned.1.call-start = ((), (), s32[]{:S(2)}) async-start(), calls=%async_computation.4 | async-start | bytes 737280 | tf_op jit(solution)/shard_map/reduce_scatter | solution.py:766
  (206 other events, 2422.6 us)
Sparse Core Ops, SparseCore 0:
  28.7 24.2 all-gather.7
  55.1 28.7 all-gather.9
  86.1 28.5 all-gather.11
  333.6 26.9 reduce-scatter.10
  458.4 20.1 reduce-scatter.6
  480.7 25.4 reduce-scatter.8
  508.6 20.9 reduce-scatter.4
